TPU v7x, 128 devices: a whole 4x4x4 slice. The times are simulated.
128 devices in a mesh: sib: 2 (over x_lo), row: 8 (over y, core), col: 8 (over z, x_hi).
Axes of the slice: x: 4 (x_hi: 2, x_lo: 2; x = x_hi * 2 + x_lo), y: 4, z: 4, core: 2. Of those that a mesh axis runs over, the one named last changes fastest.
Arguments:
- child_tiles: float32 [2, 64, 128, 128, 128], P('sib', ('row', 'col')), may hold values from -6 to 6
- child_rows: int32 [2, 64], P('sib'), may hold values from 0 to 127, as said below
- child_slots: int32 [2, 64, 128], P('sib', ('row', 'col')), may hold values from 0 to 4095, as said below
- tile_count: int32 [2, 64], P('sib', ('row', 'col')), may hold values from 64 to 128, as said below
- inverses: float32 [2, 512, 512], replicated, as said below
Outputs:
- factored: float32 [8, 16, 16, 8, 128, 128], P(None, ('sib', 'row'), None, 'col')
Inputs may be any that keep to these rules, and one draw needn't show every extreme that they name: `child_rows`: A child's entries are distinct; entry i leaves the same remainder as i when divided by the number of grid rows of the parent. `child_slots`: call the owner of parent tile (I, J) the grid row I mod (number of grid rows) and grid column J mod (number of grid columns). Among the live slots of one device at most 2 carry tiles with one owner; in every draw some device reaches 2 for some owner. `tile_count`: some device of each child has all 128 slots live. `inverses`: each matrix is lower triangular with positive diagonal.
All inputs are finite; a program needn't handle non-finite values.
Results may differ from a plain program's by a relative error of at most 0.00012.
Values sent between devices are 32-bit elements; how exact they have to be, the bound alone decides.
No kernel may reach another device: no remote copies, remote signals or barrier semaphores. Data moves between devices by JAX's collectives and lax.ppermute only.
A program may use at most 192 MiB of HBM per device.

v0:
```python
import jax
import jax.numpy as jnp
from jax import lax
from jax.sharding import PartitionSpec as P

NF = 16384
TILE = 128
PANEL = 512
NPANEL = 2
CHILD_TILES = 64
CAP = 2


def broadcast(value, axis, source):
    kept = jnp.where(lax.axis_index(axis) == source, value, 0).astype(value.dtype)
    return lax.psum(kept, axis)


def local(child_tiles, child_rows, child_slots, tile_count, inverses):
    grid_rows = lax.axis_size("sib") * lax.axis_size("row")
    columns = lax.axis_size("col")
    devices = grid_rows * columns
    tile_order = NF // TILE
    local_rows = tile_order // grid_rows
    local_cols = tile_order // columns
    tile_data = child_tiles[0, 0]
    slot_ids = child_slots[0, 0]
    live_count = tile_count[0, 0]
    row_list = child_rows[0]
    slot_total = slot_ids.shape[0]
    child_row = slot_ids // CHILD_TILES
    child_col = slot_ids % CHILD_TILES
    positions = jnp.arange(CHILD_TILES, dtype=jnp.int32)
    parent_row = jnp.sum(
        jnp.where(child_row[:, None] == positions[None, :], row_list[None, :], 0), axis=1
    )
    parent_col = jnp.sum(
        jnp.where(child_col[:, None] == positions[None, :], row_list[None, :], 0), axis=1
    )
    owner_index = parent_row % grid_rows * columns + parent_col % columns
    target = parent_row // grid_rows * local_cols + parent_col // columns
    slot_order = jnp.arange(slot_total, dtype=jnp.int32)
    is_live = slot_order < live_count
    earlier = (
        (owner_index[:, None] == owner_index[None, :])
        & is_live[None, :]
        & (slot_order[None, :] < slot_order[:, None])
    )
    slot_rank = jnp.sum(earlier.astype(jnp.int32), axis=1)
    slot_place = jnp.where(is_live, owner_index * CAP + slot_rank, devices * CAP)
    outgoing = (
        jnp.zeros((devices * CAP, TILE, TILE), jnp.float32)
        .at[slot_place]
        .set(tile_data, mode="drop")
    )
    destined = jnp.zeros((devices * CAP,), jnp.int32).at[slot_place].set(target, mode="drop")
    arrived, landing = (
        lax.all_to_all(
            outgoing.reshape(devices, CAP, TILE, TILE),
            ("sib", "row", "col"),
            split_axis=0,
            concat_axis=0,
            tiled=True,
        ),
        lax.all_to_all(
            destined.reshape(devices, CAP),
            ("sib", "row", "col"),
            split_axis=0,
            concat_axis=0,
            tiled=True,
        ),
    )
    front_tiles = jnp.zeros((local_rows * local_cols, TILE, TILE), jnp.float32)
    front_tiles = front_tiles.at[landing.reshape(-1)].add(arrived.reshape(-1, TILE, TILE))
    front_tiles = front_tiles.reshape(local_rows, local_cols, TILE, TILE)
    my_row = lax.axis_index(("sib", "row"))
    my_col = lax.axis_index("col")
    panel_tiles = PANEL // TILE
    root_count = grid_rows // columns
    tile_ids = jnp.arange(local_rows, dtype=jnp.int32) * grid_rows + my_row
    for panel_step in range(NPANEL):
        first_tile = panel_tiles * panel_step
        below_tile = first_tile + panel_tiles
        column_slot = first_tile // columns
        start_col = first_tile % columns
        is_below = tile_ids >= below_tile
        weights = inverses[panel_step]
        column_block = front_tiles[:, column_slot]
        holds_panel = (my_col >= start_col) & (my_col < start_col + panel_tiles)
        offset = jnp.clip(my_col - start_col, 0, panel_tiles - 1)
        everyone = lax.all_gather(column_block[None], "col", axis=0, tiled=True)
        chosen = everyone[start_col : start_col + panel_tiles]
        panel_rows = chosen.transpose(1, 2, 0, 3).reshape(local_rows * TILE, PANEL)
        factor = jnp.dot(panel_rows, weights.T, precision=lax.Precision.HIGHEST)
        factor = (
            factor.reshape(local_rows, TILE, PANEL) * is_below.astype(jnp.float32)[:, None, None]
        )
        panel_piece = lax.dynamic_slice_in_dim(factor, offset * TILE, TILE, 2)
        replace = is_below[:, None, None] & holds_panel
        front_tiles = front_tiles.at[:, column_slot].set(
            jnp.where(replace, panel_piece, column_block)
        )
        received = [
            broadcast(factor, ("sib", "row"), root_step * columns + my_col)
            for root_step in range(root_count)
        ]
        column_factor = jnp.stack(received, 1).reshape(local_cols, TILE, PANEL)
        front_tiles = front_tiles - jnp.einsum(
            "aip,bjp->abij", factor, column_factor, precision=lax.Precision.HIGHEST
        )
    return front_tiles.reshape(local_rows, 1, local_cols, 1, TILE, TILE)


def solution(mesh):
    return jax.shard_map(
        local,
        mesh=mesh,
        in_specs=(
            P("sib", ("row", "col"), None, None, None),
            P("sib", None),
            P("sib", ("row", "col"), None),
            P("sib", ("row", "col")),
            P(),
        ),
        out_specs=P(None, ("sib", "row"), None, "col", None, None),
        check_vma=False,
    )
```

profile of v0, /device:TPU:3, one launch (start us, length us, event | category | flops | bytes accessed | tf_op | source)
XLA Modules:
  0.0 835.3 jit_solution(17602744139437200190)
XLA Ops:
  6.5 0.7 and_select_fusion.7
  7.9 0.7 select_reduce_fusion
  8.6 0.2 convert_reduce_fusion
  8.8 1.0 scatter_custom_fusion
  9.8 0.8 all_to_all.9
  10.6 10.8 %all-to-all-start = ((s32[128,1,2]{2,1,0:T(1,128)}), s32[128,1,2]{2,1,0:T(1,128)S(1)}, u32[]{:S(2)}, u32[]{:S(2)}) async-start(s32[128,1,2]{2,1,0:T(1,128)} %bitcast.7), calls=%async_computation | async-start | bytes 131072 | tf_op jit(solution)/shard_map/all_to_all | solution.py:65
  21.4 7.9 broadcast_in_dim.69
  29.3 22.3 %scatter_fusion = f32[256,128,128]{2,1,0:T(8,128)} fusion(f32[256,128,128]{2,1,0:T(8,128)} %broadcast_in_dim.69, s32[128]{0:T(128)S(1)} %fusion.16, f32[128,128,128]{2,1,0:T(8,128)} %bitcast.120), kind=kCustom, calls=%fused_computation.1 | custom fusion | bytes 25166336 | tf_op jit(solution)/shard_map/scatter | solution.py:54
  51.7 11.2 %all-to-all-start.1 = ((f32[128,2,128,128]{3,2,1,0:T(8,128)}), f32[128,2,128,128]{3,2,1,0:T(8,128)}, u32[]{:S(2)}, u32[]{:S(2)}) async-start(f32[128,2,128,128]{3,2,1,0:T(8,128)} %bitcast.117), calls=%async_computation.1 | async-start | bytes 33554432 | tf_op jit(solution)/shard_map/all_to_all | solution.py:58
  62.8 0.0 all-gather.5.cloned.1.call-start
  62.9 0.5 broadcast.445
  63.4 0.8 reduce.7
  64.2 0.1 reshape.347
  64.4 222.4 %all-to-all-done.1 = f32[128,2,128,128]{3,2,1,0:T(8,128)} async-done(((f32[128,2,128,128]{3,2,1,0:T(8,128)}), f32[128,2,128,128]{3,2,1,0:T(8,128)}, u32[]{:S(2)}, u32[]{:S(2)}) %all-to-all-start.1) | async-done | bytes 16777248 | tf_op jit(solution)/shard_map/all_to_all | solution.py:58
  286.8 4.5 broadcast_in_dim.64
  291.2 51.3 %scatter_fusion.1 = f32[128,128,128]{2,1,0:T(8,128)} fusion(f32[128,128,128]{2,1,0:T(8,128)} %broadcast_in_dim.64, s32[256]{0:T(256)S(1)} %bitcast.125, f32[256,128,128]{2,1,0:T(8,128)} %bitcast.11), kind=kCustom, calls=%fused_computation.2 | custom fusion | flops 4194304 | bytes 50332672 | tf_op jit(solution)/shard_map/scatter-add | solution.py:74
  342.5 1.9 slice_bitcast_fusion.1
  344.5 0.0 all-gather.5.cloned.1.call-update
  344.5 0.0 all-reduce.7.cloned.1.call-start
  344.6 83.0 %all-gather.5.cloned.1.call-done = f32[64,1,128,128]{3,2,1,0:T(8,128)} async-done(((f32[8,1,128,128]{3,2,1,0:T(8,128)}), f32[64,1,128,128]{3,2,1,0:T(8,128)}) %all-gather.5.cloned.1.call-update) | async-done | bytes 4194320 | tf_op jit(solution)/shard_map/all_gather | solution.py:91
  427.6 1.6 slice-done.2
  429.2 1.4 copy.53
  430.6 1.9 dot_general.16
  432.4 5.3 convolution_multiply_fusion.1
  437.7 2.6 select_bitcast_fusion.3
  440.3 0.5 all-gather.7.cloned.1.call-start
  440.9 7.7 copy.36
  448.6 0.9 bitcast_dynamic-update-slice_fusion.1
  449.5 118.0 %all-reduce.7.cloned.1.call-done = (f32[8,1,128,512]{3,2,0,1:T(8,128)}, f32[8,1,128,512]{3,2,0,1:T(8,128)}) async-done(((f32[8,1,128,512]{3,2,0,1:T(8,128)}, f32[8,1,128,512]{3,2,0,1:T(8,128)}), (f32[8,1,128,512]{3,2,0,1:T(8,128)}, f32[8,1,128,512]{3,2,0,1:T(8,128)})) %all-reduce.7.cloned.1.call-update) | async-done | bytes 4194320 | tf_op jit(solution)/shard_map/psum | solution.py:16
  567.5 2.9 pad_maximum_fusion
  570.5 0.6 copy.37
  571.1 15.9 %bitcast_subtract_fusion.1 = f32[8,16,128,128]{3,2,0,1:T(8,128)S(1)} fusion(f32[8,16,128,128]{3,2,0,1:T(8,128)} %bitcast_dynamic-update-slice_fusion.1, f32[16,128,512,1]{2,1,3,0:T(8,128)S(1)} %bitcast.118, f32[8,128,512]{2,1,0:T(8,128)S(1)} %convolution_multiply_fusion.1), kind=kOutput, calls=%fused_computation.5 | convolution fusion | flops 12886999040 | bytes 23068672 | tf_op jit(solution)/shard_map/aip,bjp->abij/dot_general | solution.py:108
  586.9 3.4 copy-done
  590.3 0.9 slice_bitcast_fusion
  591.3 0.0 all-reduce.5.cloned.1.call-start
  591.3 72.7 %all-gather.7.cloned.1.call-done = f32[64,1,128,128]{3,2,1,0:T(8,128)} async-done(((f32[8,1,128,128]{3,2,1,0:T(8,128)}), f32[64,1,128,128]{3,2,1,0:T(8,128)}) %all-gather.7.cloned.1.call-update) | async-done | bytes 4194320 | tf_op jit(solution)/shard_map/all_gather | solution.py:91
  664.1 1.6 slice-done.3
  665.6 1.4 copy.52
  667.0 2.0 dot_general.19
  669.0 5.3 convolution_multiply_fusion
  674.3 2.6 select_bitcast_fusion.1
  677.0 0.9 bitcast_dynamic-update-slice_fusion
  677.9 126.2 %all-reduce.5.cloned.1.call-done = (f32[8,1,128,512]{3,2,0,1:T(8,128)}, f32[8,1,128,512]{3,2,0,1:T(8,128)}) async-done(((f32[8,1,128,512]{3,2,0,1:T(8,128)}, f32[8,1,128,512]{3,2,0,1:T(8,128)}), (f32[8,1,128,512]{3,2,0,1:T(8,128)}, f32[8,1,128,512]{3,2,0,1:T(8,128)})) %all-reduce.5.cloned.1.call-update) | async-done | bytes 4194320 | tf_op jit(solution)/shard_map/psum | solution.py:16
  804.2 3.1 pad_maximum_fusion.1
  807.3 0.6 copy.41
  807.9 1.7 slice-done.1
  809.6 15.0 %fusion = f32[8,1,16,1,128,128]{5,4,0,2,3,1:T(8,128)S(1)} fusion(f32[8,16,128,128]{3,2,0,1:T(8,128)S(1)} %bitcast.116, f32[16,128,512,1]{2,1,3,0:T(8,128)S(1)} %bitcast.119, f32[8,128,512]{2,1,0:T(8,128)S(1)} %convolution_multiply_fusion), kind=kOutput, calls=%fused_computation.4 | convolution fusion | flops 12886999040 | bytes 23068672 | tf_op jit(solution)/shard_map/aip,bjp->abij/dot_general | solution.py:108
  824.6 4.0 copy.43
  (17 shorter events, 0.1 us)
Async XLA Ops:
  10.6 41.1 %all-to-all-start = ((s32[128,1,2]{2,1,0:T(1,128)}), s32[128,1,2]{2,1,0:T(1,128)S(1)}, u32[]{:S(2)}, u32[]{:S(2)}) async-start(s32[128,1,2]{2,1,0:T(1,128)} %bitcast.7), calls=%async_computation | async-start | bytes 131072 | tf_op jit(solution)/shard_map/all_to_all | solution.py:65
  51.7 235.1 %all-to-all-start.1 = ((f32[128,2,128,128]{3,2,1,0:T(8,128)}), f32[128,2,128,128]{3,2,1,0:T(8,128)}, u32[]{:S(2)}, u32[]{:S(2)}) async-start(f32[128,2,128,128]{3,2,1,0:T(8,128)} %bitcast.117), calls=%async_computation.1 | async-start | bytes 33554432 | tf_op jit(solution)/shard_map/all_to_all | solution.py:58
  62.8 364.8 %all-gather.5.cloned.1.call-start = ((), (), s32[]{:S(2)}) async-start(), calls=%async_computation.2 | async-start | bytes 4718592 | tf_op jit(solution)/shard_map/all_gather | solution.py:91
  344.5 223.0 %all-reduce.7.cloned.1.call-start = ((), (), s32[]{:S(2)}) async-start(), calls=%async_computation.5 | async-start | bytes 8388608 | tf_op jit(solution)/shard_map/psum | solution.py:16
  427.6 1.6 slice-start.2
  440.3 223.7 %all-gather.7.cloned.1.call-start = ((), (), s32[]{:S(2)}) async-start(), calls=%async_computation.3 | async-start | bytes 4718592 | tf_op jit(solution)/shard_map/all_gather | solution.py:91
  586.9 3.4 copy-start
  591.3 212.9 %all-reduce.5.cloned.1.call-start = ((), (), s32[]{:S(2)}) async-start(), calls=%async_computation.4 | async-start | bytes 8388608 | tf_op jit(solution)/shard_map/psum | solution.py:16
  664.1 1.6 slice-start.3
  804.2 3.7 slice-start
  807.3 2.3 slice-start.1
Sparse Core Ops, SparseCore 0:
  344.6 82.9 all-gather.4
  440.5 127.0 all-reduce.6
  591.4 72.6 all-gather.6
  677.1 127.0 all-reduce.4
where the time goes:
time: 846 us; the launch traced here: 835 us
  waiting for transfers between devices  623 us (74%)
  local copies, waits for them, and re-layouts  67.6 us (8%)
  other arithmetic  66.8 us (8%)
  matrix products  41.5 us (5%)
  starting transfers between devices  22.6 us (3%)
  between operations  14.2 us (2%)
    psum x2, waiting for transfers between devices, broadcast(): return lax.psum(kept, axis)  244 us
    all_to_all x1, waiting for transfers between devices, local(): lax.all_to_all(outgoing.reshape(devices, CAP, TILE, TILE), ('sib', 'row',...  222 us
    all_gather x2, waiting for transfers between devices, local(): everyone = lax.all_gather(column_block[None], 'col', axis=0, tiled=True)  156 us
    scatter-add x1, other arithmetic, local(): front_tiles.at[landing.reshape(-1)].add(arrived.reshape(-1, TILE, TILE))  51.3 us
    dot_general x2, matrix products, local(): jnp.einsum('aip,bjp->abij', factor, column_factor, precision=lax.Precisio...  30.9 us
    scatter x1, local copies, waits for them, and re-layouts, local(): outgoing = jnp.zeros((devices * CAP, TILE, TILE), jnp.float32).at[slot_pl...  22.3 us
  transfers between devices with their start and end apart: 6, of which 5 were waited for; matrix products, arithmetic and copies ran while one was open for 5% of the time, Pallas kernels for 0%

commit v1 on v0

v1 whole, which is shorter than its diff:
```python
import functools

import jax
import jax.numpy as jnp
from jax import lax
from jax.experimental import pallas as pl
from jax.experimental.pallas import tpu as pltpu
from jax.sharding import PartitionSpec as P

NF = 16384
TILE = 128
PANEL = 512
NPANEL = 2
CHILD_TILES = 64
CAP = 2
PT = PANEL // TILE
WIDE = NPANEL * PANEL
META = 8
LROWS, LCOLS = 8, 16
f32, bf16, i32 = jnp.float32, jnp.bfloat16, jnp.int32
MIB = 1 << 20


def split(x):
    hi = x.astype(bf16)
    return hi, (x - hi.astype(f32)).astype(bf16)


def dot3(a, b):
    dims = (((1,), (1,)), ((), ()))
    mul = lambda u, v: lax.dot_general(u, v, dims, preferred_element_type=f32)
    return mul(a[0], b[0]) + (mul(a[0], b[1]) + mul(a[1], b[0]))


def pack_kernel(place, live, tiles, meta, out, sem, meta_sem):
    head = pltpu.make_async_copy(meta, out.at[:, CAP * TILE :, :], meta_sem)
    head.start()

    def copy(m):
        d = place[m] // CAP
        k = place[m] % CAP
        return pltpu.make_async_copy(
            tiles.at[m], out.at[d, pl.ds(pl.multiple_of(k * TILE, TILE), TILE), :], sem
        )

    lax.fori_loop(0, live[0], lambda m, c: (copy(m).start(), c)[1], 0)
    lax.fori_loop(0, live[0], lambda m, c: (copy(m).wait(), c)[1], 0)
    head.wait()


def pack(place, live, tiles, meta):
    devices = meta.shape[0]
    return pl.pallas_call(
        pack_kernel,
        out_shape=jax.ShapeDtypeStruct((devices, CAP * TILE + META, TILE), f32),
        in_specs=[
            pl.BlockSpec(memory_space=pltpu.SMEM),
            pl.BlockSpec(memory_space=pltpu.SMEM),
            pl.BlockSpec(memory_space=pl.ANY),
            pl.BlockSpec(memory_space=pltpu.VMEM),
        ],
        out_specs=pl.BlockSpec(memory_space=pl.ANY),
        scratch_shapes=[pltpu.SemaphoreType.DMA, pltpu.SemaphoreType.DMA],
        compiler_params=pltpu.CompilerParams(vmem_limit_bytes=16 * MIB),
        name="pack",
    )(place, live, tiles, meta)


def add_kernel(panel, landing, arrived, out, buf, where_to, sem):
    slots = landing.shape[0]

    def fetch(k, n):
        pair, turn = k // CAP, k % CAP
        rows = pl.ds(pl.multiple_of(turn * TILE, TILE), TILE)
        return pltpu.make_async_copy(arrived.at[pair, rows, :], buf.at[n], sem)

    def scan(k, n):
        t = landing[k]
        hit = (t >= 0) & (t % LCOLS == 0) if panel else t >= 0

        @pl.when(hit)
        def _():
            where_to[n] = t
            fetch(k, n).start()

        return n + hit.astype(i32)

    count = lax.fori_loop(0, slots, scan, 0)
    out[...] = jnp.zeros_like(out)
    lax.fori_loop(0, count, lambda n, c: (fetch(0, n).wait(), c)[1], 0)

    def add(n, c):
        t = where_to[n]
        if panel:
            a = t // LCOLS
            out[a] = out[a] + buf[n]
        else:
            a, b = t // LCOLS, t % LCOLS
            out[a, b] = out[a, b] + buf[n]
        return c

    lax.fori_loop(0, count, add, 0)


def add_up(panel, landing, arrived):
    slots = landing.shape[0]
    shape = (LROWS, TILE, TILE) if panel else (LROWS, LCOLS, TILE, TILE)
    return pl.pallas_call(
        functools.partial(add_kernel, panel),
        out_shape=jax.ShapeDtypeStruct(shape, f32),
        in_specs=[
            pl.BlockSpec(memory_space=pltpu.SMEM),
            pl.BlockSpec(memory_space=pl.ANY),
        ],
        out_specs=pl.BlockSpec(memory_space=pltpu.VMEM),
        scratch_shapes=[
            pltpu.VMEM((slots, TILE, TILE), f32),
            pltpu.SMEM((slots,), i32),
            pltpu.SemaphoreType.DMA,
        ],
        compiler_params=pltpu.CompilerParams(vmem_limit_bytes=40 * MIB),
        cost_estimate=pl.CostEstimate(
            flops=1000, bytes_accessed=MIB if panel else 24 * MIB, transcendentals=0
        ),
        name="add_panel" if panel else "add_all",
    )(landing, arrived)


def times(x, w):
    half = PANEL // 2
    left = dot3([u[:, :half] for u in x], [v[:half, :half] for v in w])
    right = dot3(x, [v[half:, :] for v in w])
    return jnp.concatenate([left, right], axis=1)


def factor(a, inv, low):
    first = times(split(a[:, :PANEL]), inv[0])
    rest = a[:, PANEL:] - dot3(split(first), low)
    return first, times(split(rest), inv[1])


CHUNK = 256


def rows_kernel(at, *refs):
    pieces, corner, inverses = refs[:8], refs[8], refs[9]
    l_hi, l_lo, l_own, inv_hi, inv_lo, low_hi, low_lo = refs[10:17]
    raw, own_f32, square = refs[17:20]
    sib, y, core, z, xh = (at[i] for i in range(5))
    my_row = (sib * 4 + y) * 2 + core
    my_col = z * 2 + xh
    sources = [
        my_col,
        z * 2 + 1 - xh,
        (z + 3) % 4 * 2 + xh,
        (z + 1) % 4 * 2 + xh,
        (z + 3) % 4 * 2 + 1 - xh,
        (z + 1) % 4 * 2 + 1 - xh,
        (z + 2) % 4 * 2 + xh,
        (z + 2) % 4 * 2 + 1 - xh,
    ]
    for piece, source in zip(pieces, sources):
        lanes = pl.ds(pl.multiple_of(source * TILE, TILE), TILE)
        for a in range(LROWS):
            raw[a * TILE : (a + 1) * TILE, lanes] = piece[a]
    for p in range(NPANEL):
        hi, lo = split(inverses[p])
        inv_hi[p] = hi
        inv_lo[p] = lo
    inv = [(inv_hi[p], inv_lo[p]) for p in range(NPANEL)]

    y_bit = jnp.where(y >= 2, y, 3 - y) % 2
    z_bit = jnp.where(z < 2, z, 3 - z)
    for q in range(16):
        yb = y_bit ^ (q & 1)
        zb = z_bit ^ (q >> 1 & 1)
        xb = xh ^ (q >> 2 & 1)
        cb = core ^ (q >> 3 & 1)
        r = pl.multiple_of((yb * 2 + cb) * TILE, TILE)
        c = pl.multiple_of((zb * 2 + xb) * TILE, TILE)
        square[pl.ds(r, TILE), pl.ds(c, TILE)] = corner[q]

    low_hi[...], low_lo[...] = split(times(split(square[...]), inv[0]))

    def chunk(i, carry):
        rows = pl.ds(pl.multiple_of(i * CHUNK, CHUNK), CHUNK)
        inv = [(inv_hi[p], inv_lo[p]) for p in range(NPANEL)]
        first, second = factor(raw[rows, :], inv, (low_hi[...], low_lo[...]))
        own_f32[rows, :PANEL] = first
        own_f32[rows, PANEL:] = second
        row_tile = jnp.where(
            (i == 0) & (lax.broadcasted_iota(i32, (CHUNK, 1), 0) < TILE), my_row, NF
        )
        first = jnp.where(row_tile >= PT, first, 0.0)
        second = jnp.where(row_tile >= 2 * PT, second, 0.0)
        hi, lo = split(first)
        l_hi[rows, :PANEL] = hi
        l_lo[rows, :PANEL] = lo
        hi, lo = split(second)
        l_hi[rows, PANEL:] = hi
        l_lo[rows, PANEL:] = lo
        return carry

    lax.fori_loop(0, LROWS * TILE // CHUNK, chunk, 0)
    lanes = pl.ds(pl.multiple_of(my_col * TILE, TILE), TILE)
    for a in range(LROWS):
        l_own[a] = own_f32[a * TILE : (a + 1) * TILE, lanes]


def rows_factor(at, pieces, corner, inverses):
    vmem = pl.BlockSpec(memory_space=pltpu.VMEM)
    height = LROWS * TILE
    shapes = [
        ((height, WIDE), bf16),
        ((height, WIDE), bf16),
        ((LROWS, TILE, TILE), f32),
        ((NPANEL, PANEL, PANEL), bf16),
        ((NPANEL, PANEL, PANEL), bf16),
        ((PANEL, PANEL), bf16),
        ((PANEL, PANEL), bf16),
    ]
    return pl.pallas_call(
        rows_kernel,
        out_shape=[jax.ShapeDtypeStruct(s, t) for s, t in shapes],
        in_specs=[pl.BlockSpec(memory_space=pltpu.SMEM)] + [vmem] * 10,
        out_specs=[vmem] * 7,
        scratch_shapes=[
            pltpu.VMEM((height, WIDE), f32),
            pltpu.VMEM((height, WIDE), f32),
            pltpu.VMEM((PANEL, PANEL), f32),
        ],
        compiler_params=pltpu.CompilerParams(vmem_limit_bytes=48 * MIB),
        cost_estimate=pl.CostEstimate(
            flops=6_000_000_000, bytes_accessed=14 * MIB, transcendentals=0
        ),
        name="rows_factor",
    )(at, *pieces, corner, inverses)


def update_kernel(
    at, column, front, l_hi, l_lo, l_own, inv_hi, inv_lo, low_hi, low_lo, out, raw, c_hi, c_lo
):
    step = pl.program_id(0)
    sib, y, core, z, xh = (at[i] for i in range(5))
    my_row = (sib * 4 + y) * 2 + core
    my_col = z * 2 + xh
    for s in range(2):
        for py in range(4):
            for pc in range(2):
                source = (py - z + 4) % 4 * 2 + pc
                lanes = pl.ds(pl.multiple_of(source * TILE, TILE), TILE)
                raw[s * TILE : (s + 1) * TILE, lanes] = column[(s * 4 + py) * 2 + pc, 0]
    inv = [(inv_hi[p], inv_lo[p]) for p in range(NPANEL)]
    first, second = factor(raw[...], inv, (low_hi[...], low_lo[...]))
    col_tile = jnp.where(
        (step == 0) & (lax.broadcasted_iota(i32, (2 * TILE, 1), 0) < TILE), my_col, NF
    )
    first = jnp.where(col_tile >= PT, first, 0.0)
    second = jnp.where(col_tile >= 2 * PT, second, 0.0)
    hi, lo = split(first)
    c_hi[:, :PANEL] = hi
    c_lo[:, :PANEL] = lo
    hi, lo = split(second)
    c_hi[:, PANEL:] = hi
    c_lo[:, PANEL:] = lo

    def rows(i, carry):
        here = pl.ds(pl.multiple_of(i * CHUNK, CHUNK), CHUNK)
        change = dot3((l_hi[here, :], l_lo[here, :]), (c_hi[...], c_lo[...]))
        for p in range(CHUNK // TILE):
            for b in range(2):
                piece = change[p * TILE : (p + 1) * TILE, b * TILE : (b + 1) * TILE]
                t = i * (CHUNK // TILE) + p
                out[t, b] = front[t, b] - piece
        return carry

    lax.fori_loop(0, LROWS * TILE // CHUNK, rows, 0)

    @pl.when(step == 0)
    def _():
        for t in range(1, LROWS):
            out[t, 0] = l_own[t]

        @pl.when((my_row >= 2 * PT) | ((my_row >= PT) & (my_col < PT)))
        def _():
            out[0, 0] = l_own[0]


def update(at, column, front, l_hi, l_lo, l_own, inv_hi, inv_lo, low_hi, low_lo):
    height = LROWS * TILE
    whole = lambda x: pl.BlockSpec(x.shape, lambda j: (0,) * x.ndim)
    block = pl.BlockSpec((LROWS, 2, TILE, TILE), lambda j: (0, j, 0, 0))
    return pl.pallas_call(
        update_kernel,
        grid=(LCOLS // 2,),
        out_shape=jax.ShapeDtypeStruct((LROWS, LCOLS, TILE, TILE), f32),
        in_specs=[
            pl.BlockSpec(memory_space=pltpu.SMEM),
            pl.BlockSpec((16, 1, TILE, TILE), lambda j: (0, j, 0, 0)),
            block,
        ]
        + [whole(x) for x in (l_hi, l_lo, l_own, inv_hi, inv_lo, low_hi, low_lo)],
        out_specs=block,
        scratch_shapes=[
            pltpu.VMEM((2 * TILE, WIDE), f32),
            pltpu.VMEM((2 * TILE, WIDE), bf16),
            pltpu.VMEM((2 * TILE, WIDE), bf16),
        ],
        compiler_params=pltpu.CompilerParams(vmem_limit_bytes=48 * MIB),
        cost_estimate=pl.CostEstimate(
            flops=22_000_000_000, bytes_accessed=30 * MIB, transcendentals=0
        ),
        name="update",
    )(at, column, front, l_hi, l_lo, l_own, inv_hi, inv_lo, low_hi, low_lo)


def move(x, axis, size, to):
    return lax.ppermute(x, axis, [(i, to(i)) for i in range(size)])


def gather_row(x):
    up, down = lambda c: (c + 2) % 8, lambda c: (c - 2) % 8
    other = move(x, "col", 8, lambda c: c ^ 1)
    x_up, x_down = move(x, "col", 8, up), move(x, "col", 8, down)
    other_up, other_down = move(other, "col", 8, up), move(other, "col", 8, down)
    x_far, other_far = move(x_up, "col", 8, up), move(other_down, "col", 8, down)
    return [x, other, x_up, x_down, other_up, other_down, x_far, other_far]


def gather_corner(tile):
    sib, row, col = (lax.axis_index(n) for n in ("sib", "row", "col"))
    other = lax.ppermute(tile, "sib", [(0, 1)])
    tile = jnp.where(sib == 0, tile, other)
    other = lax.ppermute(tile, "row", [(4, 2), (5, 3), (6, 0), (7, 1)])
    tile = jnp.where(row >= 4, tile, other)
    other = lax.ppermute(tile, "col", [(0, 6), (1, 7), (2, 4), (3, 5)])
    tiles = jnp.where(col < 4, tile, other)[None]
    for axis, bit in (("row", 2), ("col", 2), ("col", 1), ("row", 1)):
        got = move(tiles, axis, 8, lambda i: i ^ bit)
        tiles = jnp.concatenate([tiles, got], axis=0)
    return tiles


def gather_column(x):
    moves = []
    for y in range(4):
        for core in range(2):
            for z in range(4):
                for xh in range(2):
                    to = ((y + z) % 4 * 2 + xh) * 8 + y * 2 + core
                    moves.append(((y * 2 + core) * 8 + z * 2 + xh, to))
    return lax.all_gather(lax.ppermute(x, ("row", "col"), moves), ("sib", "row"))


def local(child_tiles, child_rows, child_slots, tile_count, inverses):
    grid_rows = lax.axis_size("sib") * lax.axis_size("row")
    columns = lax.axis_size("col")
    devices = grid_rows * columns
    slot_ids = child_slots[0, 0]
    live = tile_count[0]
    row_list = child_rows[0]
    child_row, child_col = slot_ids // CHILD_TILES, slot_ids % CHILD_TILES
    positions = jnp.arange(CHILD_TILES, dtype=i32)
    lookup = lambda x: jnp.sum(
        jnp.where(x[:, None] == positions[None, :], row_list[None, :], 0), axis=1
    )
    parent_row, parent_col = lookup(child_row), lookup(child_col)
    owner = parent_row % grid_rows * columns + parent_col % columns
    target = parent_row // grid_rows * LCOLS + parent_col // columns
    order = jnp.arange(slot_ids.shape[0], dtype=i32)
    is_live = order < live
    earlier = (
        (owner[:, None] == owner[None, :])
        & is_live[None, :]
        & (order[None, :] < order[:, None])
    )
    rank = jnp.sum(earlier.astype(i32), axis=1)
    place = jnp.where(is_live, owner * CAP + rank, devices * CAP)
    filled = place[None, :] == jnp.arange(devices * CAP, dtype=i32)[:, None]
    destined = jnp.sum(jnp.where(filled, target[None, :] + 1, 0), axis=1) - 1
    meta = jnp.broadcast_to(
        destined.astype(f32).reshape(devices, CAP, 1, 1),
        (devices, CAP, META // CAP, TILE),
    ).reshape(devices, META, TILE)
    outgoing = pack(place, live, child_tiles[0, 0], meta)
    arrived = lax.all_to_all(
        outgoing, ("sib", "row", "col"), split_axis=0, concat_axis=0, tiled=True
    )
    landing = arrived[:, CAP * TILE :: META // CAP, 0].astype(i32).reshape(-1)

    panel = add_up(True, landing, arrived)
    column = gather_column(panel)
    pieces = gather_row(panel)
    corner = gather_corner(panel[0])
    row = lax.axis_index("row")
    col = lax.axis_index("col")
    at = jnp.stack([lax.axis_index("sib"), row // 2, row % 2, col // 2, col % 2])
    at = at.astype(i32)
    front = add_up(False, landing, arrived)
    known = rows_factor(at, pieces, corner, inverses)
    out = update(at, column, front, *known)
    return out.reshape(LROWS, 1, LCOLS, 1, TILE, TILE)


def solution(mesh):
    return jax.shard_map(
        local,
        mesh=mesh,
        in_specs=(
            P("sib", ("row", "col"), None, None, None),
            P("sib", None),
            P("sib", ("row", "col"), None),
            P("sib", ("row", "col")),
            P(),
        ),
        out_specs=P(None, ("sib", "row"), None, "col", None, None),
        check_vma=False,
    )
```

time: 846 us -> 418 us (0.49); the launches traced: 835 us -> 416 us
  waiting for transfers between devices: 623 us -> 62.3 us
  blocking collectives: 0 us -> 206 us
  Pallas kernels: 0 us -> 78.1 us
  other arithmetic: 66.8 us -> 5.51 us
  local copies, waits for them, and re-layouts: 67.6 us -> 21.8 us
  matrix products: 41.5 us -> 0 us
    psum x2 -> x0, waiting for transfers between devices: 244 us -> none  [broadcast(): return lax.psum(kept, axis)]
    all_to_all x2 -> x0, waiting for transfers between devices: 222 us -> none  [the longest x1 222 us: local(): lax.all_to_all(outgoing.reshape(devices, CAP, TILE, TILE), ('sib', 'row',...]
    all_to_all x0 -> x1, blocking collectives: none -> 206 us  [local(): lax.all_to_all(outgoing, ('sib', 'row', 'col'), split_axis=0, concat_axis...]
    all_gather x2 -> x1, waiting for transfers between devices: 156 us -> 0.01 us  [gather_column(): lax.all_gather(lax.ppermute(x, ('row', 'col'), moves), ('sib', 'row'))]
    pallas_call x0 -> x5, Pallas kernels: none -> 78.1 us  [the longest x1 39.9 us: update(): pl.pallas_call(update_kernel, grid=(LCOLS // 2,), out_shape=jax.ShapeDtyp...]
    ppermute x0 -> x15, waiting for transfers between devices: none -> 62.2 us  [the longest x11 40.4 us: move(): return lax.ppermute(x, axis, [(i, to(i)) for i in range(size)])]
    scatter-add x1 -> x0, other arithmetic: 51.3 us -> none  [local(): front_tiles.at[landing.reshape(-1)].add(arrived.reshape(-1, TILE, TILE))]
    dot_general x4 -> x0, matrix products: 41.5 us -> none  [the longest x2 30.9 us: local(): jnp.einsum('aip,bjp->abij', factor, column_factor, precision=lax.Precisio...]
  transfers between devices with their start and end apart: 6 -> 16, of which waited for: 5 -> 7; matrix products, arithmetic and copies ran while one was open for 5% -> 1% of each run, Pallas kernels for 0% -> 5%
where the time goes in v1:
time: 418 us; the launch traced here: 416 us
  blocking collectives  206 us (49%)
  Pallas kernels  78.1 us (19%)
  waiting for transfers between devices  62.3 us (15%)
  starting transfers between devices  28.1 us (7%)
  local copies, waits for them, and re-layouts  21.8 us (5%)
  between operations  14.3 us (3%)
  other arithmetic  5.51 us (1%)
    all_to_all x1, blocking collectives, local(): lax.all_to_all(outgoing, ('sib', 'row', 'col'), split_axis=0, concat_axis...  206 us
    ppermute x11, waiting for transfers between devices, move(): return lax.ppermute(x, axis, [(i, to(i)) for i in range(size)])  40.4 us
    pallas_call x1, Pallas kernels, update(): pl.pallas_call(update_kernel, grid=(LCOLS // 2,), out_shape=jax.ShapeDtyp...  39.9 us
    ppermute x11, starting transfers between devices, move(): return lax.ppermute(x, axis, [(i, to(i)) for i in range(size)])  19.9 us
    unnamed x35, local copies, waits for them, and re-layouts  17.1 us
    pallas_call x1, Pallas kernels, rows_factor(): pl.pallas_call(rows_kernel, out_shape=[jax.ShapeDtypeStruct(s, t) for s,...  15.1 us
    pallas_call x2, Pallas kernels, add_up(): pl.pallas_call(functools.partial(add_kernel, panel), out_shape=jax.ShapeD...  13 us
    pallas_call x1, Pallas kernels, pack(): pl.pallas_call(pack_kernel, out_shape=jax.ShapeDtypeStruct((devices, CAP...  10.1 us
  transfers between devices with their start and end apart: 16, of which 7 were waited for; matrix products, arithmetic and copies ran while one was open for 1% of the time, Pallas kernels for 5%

profile of v1, /device:TPU:3, one launch (start us, length us, event | category | flops | bytes accessed | tf_op | source)
XLA Modules:
  0.0 416.1 jit_solution(5936162788904565855)
XLA Ops:
  7.2 0.7 and_select_fusion.5
  7.9 0.7 select_reduce_fusion.1
  8.6 0.2 convert_reduce_fusion.1
  8.8 0.1 select_reduce_fusion
  9.0 0.1 convert_element_type.22
  9.3 0.2 broadcast_in_dim.66.meta
  9.5 3.4 copy-done
  12.9 10.1 %pack.1 = f32[128,264,128]{2,1,0:T(8,128)S(1)} custom-call(s32[128]{0:T(128)S(1)} %add_select_fusion.place, s32[1]{0:T(128)} %bitcast.38.live, f32[128,128,128]{2,1,0:T(8,128)S(1)} %bitcast.39, f32[128,8,128]{2,1,0:T(8,128)S(1)} %broadcast_in_dim.66.meta), custom_call_target="tpu_custom_call" | custom-call | tf_op jit(solution)/shard_map/pack/pallas_call | solution.py:53
  23.0 206.1 %all_to_all.5.arrived = f32[128,264,128]{2,1,0:T(8,128)} all-to-all(f32[128,264,128]{2,1,0:T(8,128)S(1)} %pack.1), channel_id=1, replica_groups=mesh['sib'=2,'row'=8,'col'=8] {'sib','row','col'}, dimensions={0} | all-to-all | bytes 34603008 | tf_op jit(solution)/shard_map/all_to_all | solution.py:386
  229.1 2.9 slice.6
  232.0 2.2 convert_reduce_fusion
  234.3 0.1 convert_element_type.24.landing
  234.4 5.4 %add_panel.1.refs_0_ = f32[8,128,128]{2,1,0:T(8,128)S(1)} custom-call(s32[256]{0:T(256)S(1)} %convert_element_type.24.landing, f32[128,264,128]{2,1,0:T(8,128)} %all_to_all.5.arrived), custom_call_target="tpu_custom_call" | custom-call | flops 1000 | bytes 1048576 | tf_op jit(solution)/shard_map/add_panel/pallas_call | solution.py:108
  239.8 2.0 collective-permute-start
  241.8 10.0 %collective-permute-done = f32[8,128,128]{2,1,0:T(8,128)S(1)} collective-permute-done((f32[8,128,128]{2,1,0:T(8,128)S(1)}, f32[8,128,128]{2,1,0:T(8,128)S(1)}, u32[]{:S(2)}, u32[]{:S(2)}) %collective-permute-start) | collective-permute-done | bytes 524320 | tf_op jit(solution)/shard_map/ppermute | solution.py:352
  251.8 0.8 copy-done.13
  252.7 1.3 collective-permute-start.8
  254.0 4.0 collective-permute-done.8
  258.0 1.3 collective-permute-start.9
  259.3 7.8 %collective-permute-done.9 = f32[128,128]{1,0:T(8,128)S(1)} collective-permute-done((f32[128,128]{1,0:T(8,128)S(1)}, f32[128,128]{1,0:T(8,128)S(1)}, u32[]{:S(2)}, u32[]{:S(2)}) %collective-permute-start.9) | collective-permute-done | bytes 65568 | tf_op jit(solution)/shard_map/ppermute | solution.py:334
  267.1 3.6 collective-permute-start.10
  270.7 4.8 %collective-permute-start.1 = (f32[8,128,128]{2,1,0:T(8,128)S(1)}, f32[8,128,128]{2,1,0:T(8,128)S(1)}, u32[]{:S(2)}, u32[]{:S(2)}) collective-permute-start(f32[8,128,128]{2,1,0:T(8,128)S(1)} %add_panel.1.refs_0_), channel_id=1, source_target_pairs={{0,1},{1,0},{2,3},{3,2},{4,5},{5,4},{6,7},{7,6},{8,9},{9,8},{10,11... | collective-permute-start | bytes 1572872 | tf_op jit(solution)/shard_map/ppermute | solution.py:318
  275.6 0.6 constant_dynamic-update-slice_fusion.4
  276.2 4.9 %collective-permute-done.11 = f32[1,128,128]{2,1,0:T(8,128)S(1)} collective-permute-done((f32[1,128,128]{2,1,0:T(8,128)S(1)}, f32[1,128,128]{2,1,0:T(8,128)S(1)}, u32[]{:S(2)}, u32[]{:S(2)}) %collective-permute-start.11) | collective-permute-done | bytes 65568 | tf_op jit(solution)/shard_map/ppermute | solution.py:318
  281.2 1.5 collective-permute-start.2
  282.6 15.2 %collective-permute-done.1.refs_1_ = f32[8,128,128]{2,1,0:T(8,128)S(1)} collective-permute-done((f32[8,128,128]{2,1,0:T(8,128)S(1)}, f32[8,128,128]{2,1,0:T(8,128)S(1)}, u32[]{:S(2)}, u32[]{:S(2)}) %collective-permute-start.1) | collective-permute-done | bytes 524320 | tf_op jit(solution)/shard_map/ppermute | solution.py:318
  297.9 3.8 collective-permute-start.13
  301.6 10.8 %collective-permute-done.13 = f32[4,128,128]{2,1,0:T(8,128)S(1)} collective-permute-done((f32[4,128,128]{2,1,0:T(8,128)S(1)}, f32[4,128,128]{2,1,0:T(8,128)S(1)}, u32[]{:S(2)}, u32[]{:S(2)}) %collective-permute-start.13) | collective-permute-done | bytes 262176 | tf_op jit(solution)/shard_map/ppermute | solution.py:318
  312.4 0.8 pad_maximum_fusion
  313.3 5.4 %collective-permute-start.14 = (f32[8,128,128]{2,1,0:T(8,128)}, f32[8,128,128]{2,1,0:T(8,128)}, u32[]{:S(2)}, u32[]{:S(2)}) collective-permute-start(f32[8,128,128]{2,1,0:T(8,128)} %pad_maximum_fusion), channel_id=1, source_target_pairs={{0,8},{8,0},{16,24},{24,16},{32,40},{40,32},{48,56},{56,48},{1,9},... | collective-permute-start | bytes 1572872 | tf_op jit(solution)/shard_map/ppermute | solution.py:318
  318.7 1.7 collective-permute-start.4
  320.4 1.4 collective-permute-start.6
  321.8 1.2 collective-permute-start.7
  323.1 7.6 %add_all.1.front = f32[8,16,128,128]{3,2,1,0:T(8,128)S(1)} custom-call(s32[256]{0:T(256)S(1)} %convert_element_type.24.landing, f32[128,264,128]{2,1,0:T(8,128)} %all_to_all.5.arrived), custom_call_target="tpu_custom_call" | custom-call | flops 1000 | bytes 25165824 | tf_op jit(solution)/shard_map/add_all/pallas_call | solution.py:108
  330.7 3.2 copy-done.1
  334.0 1.1 constant_dynamic-update-slice_fusion.refs_8_
  335.1 9.6 %collective-permute-done.6.refs_6_ = f32[8,128,128]{2,1,0:T(8,128)} collective-permute-done((f32[8,128,128]{2,1,0:T(8,128)S(1)}, f32[8,128,128]{2,1,0:T(8,128)}, u32[]{:S(2)}, u32[]{:S(2)}) %collective-permute-start.6) | collective-permute-done | bytes 524320 | tf_op jit(solution)/shard_map/ppermute | solution.py:318
  344.7 15.1 %rows_factor.1 = (bf16[1024,1024]{1,0:T(8,128)(2,1)}, bf16[1024,1024]{1,0:T(8,128)(2,1)}, f32[8,128,128]{2,1,0:T(8,128)S(1)}, bf16[2,512,512]{2,1,0:T(8,128)(2,1...) custom-call(s32[5]{0:T(128)S(1)} %stack.23.at, ...), custom_call_target="tpu_custom_call" | custom-call | flops 6000000000 | bytes 14680064 | tf_op jit(solution)/shard_map/rows_factor/pallas_call | solution.py:222
  359.8 0.8 copy-done.5
  360.6 0.8 copy-done.7
  361.4 0.8 copy-done.9
  362.2 1.6 copy-done.2
  363.8 1.2 copy-done.3
  365.0 1.2 copy-done.4
  366.3 1.0 copy-done.6
  367.3 1.0 copy-done.8
  368.3 1.0 copy-done.10
  369.4 39.9 %update.1 = f32[8,16,128,128]{3,2,1,0:T(8,128)} custom-call(s32[5]{0:T(128)S(1)} %stack.23.at, f32[16,8,128,128]{3,2,1,0:T(8,128)} %bitcast.42, f32[8,16,128,128]{3,2,1,0:T(8,128)} %copy-done.1, bf16[1024,1024]{1,0:T(8,128)(2,1)S(1)} %copy-done.2, bf16[1024,1024]{1,0:T(8,128)(2,1)} %get-tuple-element.13.l_lo, f32[8,128,128]{2,1,0:T(8,128)S(1)} %copy-done.6, ...), custom_call_target="tpu_custom_call" | custom-call | flops 22000001024 | bytes 31457280 | tf_op jit(solution)/shard_map/update/pallas_call | solution.py:293
  (51 shorter events, 0.6 us)
Async XLA Ops:
  6.5 355.7 %all-gather.3.cloned.1.call-start = ((), (), s32[]{:S(2)}) async-start(), calls=%async_computation.1 | async-start | bytes 8912896 | tf_op jit(solution)/shard_map/all_gather | solution.py:352
  9.5 3.4 copy-start
  239.8 12.0 %collective-permute-start = (f32[8,128,128]{2,1,0:T(8,128)S(1)}, f32[8,128,128]{2,1,0:T(8,128)S(1)}, u32[]{:S(2)}, u32[]{:S(2)}) collective-permute-start(f32[8,128,128]{2,1,0:T(8,128)S(1)} %add_panel.1.refs_0_), channel_id=1, source_target_pairs={{0,0},{1,8},{2,16},{3,24},{4,32},{5,40},{6,48},{7,56},{8,1},{9,9},... | collective-permute-start | bytes 1572872 | tf_op jit(solution)/shard_map/ppermute | solution.py:352
  251.8 0.8 copy-start.13
  252.7 5.3 %collective-permute-start.8 = (f32[128,128]{1,0:T(8,128)S(1)}, f32[128,128]{1,0:T(8,128)S(1)}, u32[]{:S(2)}, u32[]{:S(2)}) collective-permute-start(f32[128,128]{1,0:T(8,128)S(1)} %slice_bitcast_fusion), channel_id=1, source_target_pairs={{0,64},{1,65},{2,66},{3,67},{4,68},{5,69},{6,70},{7,71},{8,72},{9,... | collective-permute-start | bytes 196616 | tf_op jit(solution)/shard_map/ppermute | solution.py:332
  258.0 9.1 %collective-permute-start.9 = (f32[128,128]{1,0:T(8,128)S(1)}, f32[128,128]{1,0:T(8,128)S(1)}, u32[]{:S(2)}, u32[]{:S(2)}) collective-permute-start(f32[128,128]{1,0:T(8,128)S(1)} %broadcast_select_fusion), channel_id=1, source_target_pairs={{32,16},{40,24},{48,0},{56,8},{33,17},{41,25},{49,1},{57,9},{34,18... | collective-permute-start | bytes 196616 | tf_op jit(solution)/shard_map/ppermute | solution.py:334
  267.1 8.4 %collective-permute-start.10 = (f32[128,128]{1,0:T(8,128)S(1)}, f32[128,128]{1,0:T(8,128)S(1)}, u32[]{:S(2)}, u32[]{:S(2)}) collective-permute-start(f32[128,128]{1,0:T(8,128)S(1)} %broadcast_select_fusion.1), channel_id=1, source_target_pairs={{0,6},{1,7},{2,4},{3,5},{8,14},{9,15},{10,12},{11,13},{16,22},{17,... | collective-permute-start | bytes 196616 | tf_op jit(solution)/shard_map/ppermute | solution.py:336
  270.7 27.1 %collective-permute-start.1 = (f32[8,128,128]{2,1,0:T(8,128)S(1)}, f32[8,128,128]{2,1,0:T(8,128)S(1)}, u32[]{:S(2)}, u32[]{:S(2)}) collective-permute-start(f32[8,128,128]{2,1,0:T(8,128)S(1)} %add_panel.1.refs_0_), channel_id=1, source_target_pairs={{0,1},{1,0},{2,3},{3,2},{4,5},{5,4},{6,7},{7,6},{8,9},{9,8},{10,11... | collective-permute-start | bytes 1572872 | tf_op jit(solution)/shard_map/ppermute | solution.py:318
  276.2 4.9 %collective-permute-start.11 = (f32[1,128,128]{2,1,0:T(8,128)S(1)}, f32[1,128,128]{2,1,0:T(8,128)S(1)}, u32[]{:S(2)}, u32[]{:S(2)}) collective-permute-start(f32[1,128,128]{2,1,0:T(8,128)S(1)} %get-tuple-element.22), channel_id=1, source_target_pairs={{0,16},{8,24},{16,0},{24,8},{32,48},{40,56},{48,32},{56,40},{1,17}... | collective-permute-start | bytes 196616 | tf_op jit(solution)/shard_map/ppermute | solution.py:318
  281.1 32.2 %copy-start.11 = (f32[1,128,128]{2,1,0:T(8,128)}, f32[1,128,128]{2,1,0:T(8,128)S(1)}, u32[]{:S(2)}) copy-start(f32[1,128,128]{2,1,0:T(8,128)S(1)} %collective-permute-done.11) | copy-start | bytes 196612
  281.1 16.7 %collective-permute-start.12 = (f32[2,128,128]{2,1,0:T(8,128)S(1)}, f32[2,128,128]{2,1,0:T(8,128)S(1)}, u32[]{:S(2)}, u32[]{:S(2)}) collective-permute-start(f32[2,128,128]{2,1,0:T(8,128)S(1)} %pad_maximum_fusion.2), channel_id=1, source_target_pairs={{0,2},{1,3},{2,0},{3,1},{4,6},{5,7},{6,4},{7,5},{8,10},{9,11},{10,... | collective-permute-start | bytes 393224 | tf_op jit(solution)/shard_map/ppermute | solution.py:318
  281.2 39.2 %collective-permute-start.2 = (f32[8,128,128]{2,1,0:T(8,128)S(1)}, f32[8,128,128]{2,1,0:T(8,128)S(1)}, u32[]{:S(2)}, u32[]{:S(2)}) collective-permute-start(f32[8,128,128]{2,1,0:T(8,128)S(1)} %add_panel.1.refs_0_), channel_id=1, source_target_pairs={{0,2},{1,3},{2,4},{3,5},{4,6},{5,7},{6,0},{7,1},{8,10},{9,11},{10,... | collective-permute-start | bytes 1572872 | tf_op jit(solution)/shard_map/ppermute | solution.py:318
  297.8 24.0 %collective-permute-start.5 = (f32[8,128,128]{2,1,0:T(8,128)S(1)}, f32[8,128,128]{2,1,0:T(8,128)S(1)}, u32[]{:S(2)}, u32[]{:S(2)}) collective-permute-start(f32[8,128,128]{2,1,0:T(8,128)S(1)} %collective-permute-done.1.refs_1_), channel_id=1, source_target_pairs={{0,6},{1,7},{2,0},{3,1},{4,2},{5,3},{6,4},{7,5},{8,14},{9,15},{10,... | collective-permute-start | bytes 1572872 | tf_op jit(solution)/shard_map/ppermute | solution.py:318
  297.9 14.6 %collective-permute-start.13 = (f32[4,128,128]{2,1,0:T(8,128)S(1)}, f32[4,128,128]{2,1,0:T(8,128)S(1)}, u32[]{:S(2)}, u32[]{:S(2)}) collective-permute-start(f32[4,128,128]{2,1,0:T(8,128)S(1)} %pad_maximum_fusion.1), channel_id=1, source_target_pairs={{0,1},{1,0},{2,3},{3,2},{4,5},{5,4},{6,7},{7,6},{8,9},{9,8},{10,11... | collective-permute-start | bytes 786440 | tf_op jit(solution)/shard_map/ppermute | solution.py:318
  313.3 20.8 %collective-permute-start.14 = (f32[8,128,128]{2,1,0:T(8,128)}, f32[8,128,128]{2,1,0:T(8,128)}, u32[]{:S(2)}, u32[]{:S(2)}) collective-permute-start(f32[8,128,128]{2,1,0:T(8,128)} %pad_maximum_fusion), channel_id=1, source_target_pairs={{0,8},{8,0},{16,24},{24,16},{32,40},{40,32},{48,56},{56,48},{1,9},... | collective-permute-start | bytes 1572872 | tf_op jit(solution)/shard_map/ppermute | solution.py:318
  318.7 16.4 %collective-permute-start.3 = (f32[8,128,128]{2,1,0:T(8,128)S(1)}, f32[8,128,128]{2,1,0:T(8,128)S(1)}, u32[]{:S(2)}, u32[]{:S(2)}) collective-permute-start(f32[8,128,128]{2,1,0:T(8,128)S(1)} %add_panel.1.refs_0_), channel_id=1, source_target_pairs={{0,6},{1,7},{2,0},{3,1},{4,2},{5,3},{6,4},{7,5},{8,14},{9,15},{10,... | collective-permute-start | bytes 1572872 | tf_op jit(solution)/shard_map/ppermute | solution.py:318
  318.7 26.0 %collective-permute-start.4 = (f32[8,128,128]{2,1,0:T(8,128)S(1)}, f32[8,128,128]{2,1,0:T(8,128)S(1)}, u32[]{:S(2)}, u32[]{:S(2)}) collective-permute-start(f32[8,128,128]{2,1,0:T(8,128)S(1)} %collective-permute-done.1.refs_1_), channel_id=1, source_target_pairs={{0,2},{1,3},{2,4},{3,5},{4,6},{5,7},{6,0},{7,1},{8,10},{9,11},{10,... | collective-permute-start | bytes 1572872 | tf_op jit(solution)/shard_map/ppermute | solution.py:318
  320.4 24.4 %collective-permute-start.6 = (f32[8,128,128]{2,1,0:T(8,128)S(1)}, f32[8,128,128]{2,1,0:T(8,128)}, u32[]{:S(2)}, u32[]{:S(2)}) collective-permute-start(f32[8,128,128]{2,1,0:T(8,128)S(1)} %collective-permute-done.2.refs_2_), channel_id=1, source_target_pairs={{0,2},{1,3},{2,4},{3,5},{4,6},{5,7},{6,0},{7,1},{8,10},{9,11},{10,... | collective-permute-start | bytes 1572872 | tf_op jit(solution)/shard_map/ppermute | solution.py:318
  321.8 22.9 %collective-permute-start.7 = (f32[8,128,128]{2,1,0:T(8,128)S(1)}, f32[8,128,128]{2,1,0:T(8,128)}, u32[]{:S(2)}, u32[]{:S(2)}) collective-permute-start(f32[8,128,128]{2,1,0:T(8,128)S(1)} %collective-permute-done.5.refs_5_), channel_id=1, source_target_pairs={{0,6},{1,7},{2,0},{3,1},{4,2},{5,3},{6,4},{7,5},{8,14},{9,15},{10,... | collective-permute-start | bytes 1572872 | tf_op jit(solution)/shard_map/ppermute | solution.py:318
  323.1 10.8 %copy-start.12 = (f32[1,128,128]{2,1,0:T(8,128)S(1)}, f32[1,128,128]{2,1,0:T(8,128)}, u32[]{:S(2)}) copy-start(f32[1,128,128]{2,1,0:T(8,128)} %copy-done.11) | copy-start | bytes 196612
  323.1 10.8 %copy-start.14 = (f32[16,128,128]{2,1,0:T(8,128)S(1)}, f32[16,128,128]{2,1,0:T(8,128)}, u32[]{:S(2)}) copy-start(f32[16,128,128]{2,1,0:T(8,128)} %get-tuple-element.21) | copy-start | bytes 3145732
  330.7 3.2 copy-start.1
  335.1 9.6 %copy-start.15 = (f32[16,128,128]{2,1,0:T(8,128)}, f32[16,128,128]{2,1,0:T(8,128)S(1)}, u32[]{:S(2)}) copy-start(f32[16,128,128]{2,1,0:T(8,128)S(1)} %constant_dynamic-update-slice_fusion.refs_8_) | copy-start | bytes 3145732
  359.8 0.8 copy-start.5
  360.6 0.8 copy-start.7
  361.4 0.8 copy-start.9
  362.2 1.6 copy-start.2
  363.8 1.2 copy-start.3
  365.0 1.2 copy-start.4
  366.3 1.0 copy-start.6
  367.3 1.0 copy-start.8
  368.3 1.0 copy-start.10
Sparse Core Ops, SparseCore 0:
  252.8 73.8 all-gather.2

commit v2 on v1

v2 whole, which is shorter than its diff:
```python
import functools

import jax
import jax.numpy as jnp
from jax import lax
from jax.experimental import pallas as pl
from jax.experimental.pallas import tpu as pltpu
from jax.sharding import PartitionSpec as P

NF = 16384
TILE = 128
PANEL = 512
NPANEL = 2
CHILD_TILES = 64
CAP = 2
PT = PANEL // TILE
WIDE = NPANEL * PANEL
META = 8
LROWS, LCOLS = 8, 16
f32, bf16, i32 = jnp.float32, jnp.bfloat16, jnp.int32
MIB = 1 << 20


def split(x):
    hi = x.astype(bf16)
    return hi, (x - hi.astype(f32)).astype(bf16)


def pack_kernel(place, live, tiles, meta, out, sem, meta_sem):
    head = pltpu.make_async_copy(meta, out.at[:, CAP * TILE :, :], meta_sem)
    head.start()

    def copy(m):
        d = place[m] // CAP
        k = place[m] % CAP
        return pltpu.make_async_copy(
            tiles.at[m], out.at[d, pl.ds(pl.multiple_of(k * TILE, TILE), TILE), :], sem
        )

    lax.fori_loop(0, live[0], lambda m, c: (copy(m).start(), c)[1], 0)
    lax.fori_loop(0, live[0], lambda m, c: (copy(m).wait(), c)[1], 0)
    head.wait()


def pack(place, live, tiles, meta):
    devices = meta.shape[0]
    return pl.pallas_call(
        pack_kernel,
        out_shape=jax.ShapeDtypeStruct((devices, CAP * TILE + META, TILE), f32),
        in_specs=[
            pl.BlockSpec(memory_space=pltpu.SMEM),
            pl.BlockSpec(memory_space=pltpu.SMEM),
            pl.BlockSpec(memory_space=pl.ANY),
            pl.BlockSpec(memory_space=pltpu.VMEM),
        ],
        out_specs=pl.BlockSpec(memory_space=pl.ANY),
        scratch_shapes=[pltpu.SemaphoreType.DMA, pltpu.SemaphoreType.DMA],
        compiler_params=pltpu.CompilerParams(vmem_limit_bytes=16 * MIB),
        name="pack",
    )(place, live, tiles, meta)


def add_kernel(panel, *refs):
    if panel:
        arrived, out, landing, buf, where_to, sem, head, places, head_sem = refs
        slots = arrived.shape[0] * CAP
        copy = pltpu.make_async_copy(arrived.at[:, CAP * TILE :, :], head, head_sem)
        copy.start()
        copy.wait()
        places[...] = jnp.sum(head[...], axis=0).astype(i32) - 1
        copy = pltpu.make_async_copy(places, landing, head_sem)
        copy.start()
        out[...] = jnp.zeros_like(out)
        copy.wait()
    else:
        landing, arrived, out, buf, where_to, sem = refs
        slots = arrived.shape[0] * CAP

    def fetch(k, n):
        pair, turn = k // CAP, k % CAP
        rows = pl.ds(pl.multiple_of(turn * TILE, TILE), TILE)
        return pltpu.make_async_copy(arrived.at[pair, rows, :], buf.at[n], sem)

    def scan(k, n):
        t = landing[k % CAP, k // CAP]
        hit = (t >= 0) & (t % LCOLS == 0) if panel else t >= 0

        @pl.when(hit)
        def _():
            where_to[n] = t
            fetch(k, n).start()

        return n + hit.astype(i32)

    count = lax.fori_loop(0, slots, scan, 0)
    if not panel:
        out[...] = jnp.zeros_like(out)
    lax.fori_loop(0, count, lambda n, c: (fetch(0, n).wait(), c)[1], 0)

    def add(n, c):
        t = where_to[n]
        if panel:
            a = t // LCOLS
            out[a] = out[a] + buf[n]
        else:
            a, b = t // LCOLS, t % LCOLS
            out[a, b] = out[a, b] + buf[n]
        return c

    lax.fori_loop(0, count, add, 0)


def add_up(panel, arrived, landing=None):
    devices = arrived.shape[0]
    vmem = pl.BlockSpec(memory_space=pltpu.VMEM)
    smem = pl.BlockSpec(memory_space=pltpu.SMEM)
    scratch = [
        pltpu.VMEM((devices * CAP, TILE, TILE), f32),
        pltpu.SMEM((devices * CAP,), i32),
        pltpu.SemaphoreType.DMA,
    ]
    any_space = pl.BlockSpec(memory_space=pl.ANY)
    if panel:
        return pl.pallas_call(
            functools.partial(add_kernel, True),
            out_shape=[
                jax.ShapeDtypeStruct((LROWS, TILE, TILE), f32),
                jax.ShapeDtypeStruct((META, devices), i32),
            ],
            in_specs=[any_space],
            out_specs=[vmem, smem],
            scratch_shapes=scratch
            + [
                pltpu.VMEM((devices, META, TILE), f32),
                pltpu.VMEM((META, devices), i32),
                pltpu.SemaphoreType.DMA,
            ],
            compiler_params=pltpu.CompilerParams(vmem_limit_bytes=56 * MIB),
            name="add_panel",
        )(arrived)
    return pl.pallas_call(
        functools.partial(add_kernel, False),
        out_shape=jax.ShapeDtypeStruct((LROWS, LCOLS, TILE, TILE), f32),
        in_specs=[smem, any_space],
        out_specs=vmem,
        scratch_shapes=scratch,
        compiler_params=pltpu.CompilerParams(vmem_limit_bytes=30 * MIB),
        cost_estimate=pl.CostEstimate(
            flops=1000, bytes_accessed=24 * MIB, transcendentals=0
        ),
        name="add_all",
    )(landing, arrived)


BLOCK = 256
KP = 3 * PANEL


def left_form(ref, rows, lane, x):
    hi, lo = split(x)
    for k in range(x.shape[1] // BLOCK):
        for part, half in enumerate((hi, hi, lo)):
            at = lane + (3 * k + part) * BLOCK
            ref[rows, at : at + BLOCK] = half[:, k * BLOCK : (k + 1) * BLOCK]


def right_form(ref, row, x):
    hi, lo = split(x)
    for k in range(x.shape[0] // BLOCK):
        for part, half in enumerate((hi, lo, hi)):
            at = row + (3 * k + part) * BLOCK
            ref[at : at + BLOCK, :] = half[k * BLOCK : (k + 1) * BLOCK, :]


def mul(a, b):
    return jnp.dot(a, b, preferred_element_type=f32)


def row_place(at):
    sib, y, core, z, xh = (at[i] for i in range(5))
    return (sib * 4 + y) * 2 + core, z * 2 + xh


def rows_kernel(at, own, up, down, far, far2, inverses, l0, a1, l0_own, inv, raw, left, w0):
    z, xh = at[3], at[4]
    my_row, my_col = row_place(at)
    around = lambda dz, flip: (z + dz + 4) % 4 * 2 + jnp.where(flip, 1 - xh, xh)
    pieces = [
        (own, 0, around(0, False)),
        (own, 8, around(0, True)),
        (up, 0, around(-1, False)),
        (up, 8, around(-1, True)),
        (down, 0, around(1, False)),
        (down, 8, around(1, True)),
        (far, 0, around(2, False)),
        (far2, 0, around(2, True)),
    ]
    for piece, first, source in pieces:
        lanes = pl.ds(pl.multiple_of(source % PT * TILE, TILE), TILE)

        @pl.when(source < PT)
        def _():
            for a in range(LROWS):
                raw[a * TILE : (a + 1) * TILE, lanes] = piece[first + a]

        @pl.when(source >= PT)
        def _():
            for a in range(LROWS):
                a1[a * TILE : (a + 1) * TILE, lanes] = piece[first + a]

    for p in range(NPANEL):
        left_form(inv.at[p], slice(None), 0, inverses[p])
    right_form(w0, 0, inverses[0].T)
    height = 512
    for i in range(LROWS * TILE // height):
        rows = slice(i * height, (i + 1) * height)
        left_form(left, rows, 0, raw[rows, :])
        low = mul(left[rows, : KP // 2], w0[: KP // 2, :BLOCK])
        high = mul(left[rows, :], w0[:, BLOCK:])
        if i == 0:
            tile = jnp.where(
                lax.broadcasted_iota(i32, (height, 1), 0) < TILE, my_row, NF
            )
            low = jnp.where(tile >= PT, low, 0.0)
            high = jnp.where(tile >= PT, high, 0.0)
        raw[rows, :BLOCK] = low
        raw[rows, BLOCK:] = high
        left_form(l0, rows, 0, low)
        left_form(l0, rows, KP // 2, high)
    lanes = pl.ds(pl.multiple_of(my_col % PT * TILE, TILE), TILE)
    for a in range(LROWS):
        l0_own[a] = raw[a * TILE : (a + 1) * TILE, lanes]


def rows_factor(at, pieces, inverses):
    vmem = pl.BlockSpec(memory_space=pltpu.VMEM)
    height = LROWS * TILE
    shapes = [
        ((height, KP), bf16),
        ((height, PANEL), f32),
        ((LROWS, TILE, TILE), f32),
        ((NPANEL, PANEL, KP), bf16),
    ]
    return pl.pallas_call(
        rows_kernel,
        out_shape=[jax.ShapeDtypeStruct(s, t) for s, t in shapes],
        in_specs=[pl.BlockSpec(memory_space=pltpu.SMEM)] + [vmem] * 6,
        out_specs=[vmem] * 4,
        scratch_shapes=[
            pltpu.VMEM((height, PANEL), f32),
            pltpu.VMEM((height, KP), bf16),
            pltpu.VMEM((KP, PANEL), bf16),
        ],
        compiler_params=pltpu.CompilerParams(vmem_limit_bytes=32 * MIB),
        cost_estimate=pl.CostEstimate(
            flops=4_000_000_000, bytes_accessed=14 * MIB, transcendentals=0
        ),
        name="rows_factor",
    )(at, *pieces, inverses)


def update_kernel(
    at, column, corner, front, l0, a1, l0_own, inv, inverses, out, l1, c, raw, right, big, low, low_t, l1_own
):
    step = pl.program_id(0)
    z = at[3]
    my_row, my_col = row_place(at)

    def factor_columns(x, inverse, put):
        put(0, mul(inverse[:BLOCK, : KP // 2], x[: KP // 2, :]))
        put(1, mul(inverse[BLOCK:, :], x[...]))

    @pl.when(step == 0)
    def _():
        for i in range(PT):
            for j in range(PT):
                raw_t = corner[i, j].T
                big[j * TILE : (j + 1) * TILE, i * TILE : (i + 1) * TILE] = raw_t
        right_form(low_t, 0, big[:PANEL, :])

        def put(half, value):
            big[half * BLOCK : (half + 1) * BLOCK, :] = value

        factor_columns(low_t, inv[0], put)
        right_form(low_t, 0, big[:PANEL, :])
        left_form(low, slice(None), 0, big[:PANEL, :].T)
        big[...] = a1[...] - mul(l0[...], low_t[...])
        left_form(l1, slice(None), 0, big[...])
        right_form(low_t, 0, inverses[1].T)
        tile = jnp.where(
            lax.broadcasted_iota(i32, (LROWS * TILE, 1), 0) < TILE, my_row, NF
        )
        first = mul(l1[:, : KP // 2], low_t[: KP // 2, :BLOCK])
        second = mul(l1[...], low_t[:, BLOCK:])
        first = jnp.where(tile >= 2 * PT, first, 0.0)
        second = jnp.where(tile >= 2 * PT, second, 0.0)
        big[:, :BLOCK] = first
        big[:, BLOCK:] = second
        left_form(l1, slice(None), 0, first)
        left_form(l1, slice(None), KP // 2, second)
        lanes = pl.ds(pl.multiple_of(my_col % PT * TILE, TILE), TILE)
        for t in range(LROWS):
            l1_own[t] = big[t * TILE : (t + 1) * TILE, lanes]

    for s in range(2):
        for py in range(4):
            for pc in range(2):
                source = (py - z + 4) % 4 * 2 + pc
                rows = pl.ds(pl.multiple_of(source * TILE, TILE), TILE)
                tile_t = column[(s * 4 + py) * 2 + pc, 0].T
                raw[rows, s * TILE : (s + 1) * TILE] = tile_t
    col_tile = jnp.where(
        (step == 0) & (lax.broadcasted_iota(i32, (1, 2 * TILE), 1) < TILE), my_col, NF
    )
    right_form(right, 0, raw[:PANEL, :])

    def put(panel):
        def store(half, value):
            value = jnp.where(col_tile >= (panel + 1) * PT, value, 0.0)
            right_form(c, panel * KP + half * KP // 2, value)

        return store

    factor_columns(right, inv[0], put(0))
    right_form(right, 0, raw[PANEL:, :] - mul(low[...], c[:KP, :]))
    factor_columns(right, inv[1], put(1))

    change = mul(l0[...], c[:KP, :]) + mul(l1[...], c[KP:, :])
    for t in range(LROWS):
        for b in range(2):
            piece = change[t * TILE : (t + 1) * TILE, b * TILE : (b + 1) * TILE]
            out[t, b] = front[t, b] - piece

    @pl.when(step == 0)
    def _():
        for own, mine in ((l0_own, my_col < PT), (l1_own, my_col >= PT)):

            @pl.when(mine)
            def _():
                for t in range(1, LROWS):
                    out[t, 0] = own[t]

                @pl.when((my_row >= 2 * PT) | ((my_row >= PT) & (my_col < PT)))
                def _():
                    out[0, 0] = own[0]


def update(at, column, front, l0, a1, l0_own, inv, inverses):
    height = LROWS * TILE
    vmem = pl.BlockSpec(memory_space=pltpu.VMEM)
    block = pl.BlockSpec((LROWS, 2, TILE, TILE), lambda j: (0, j, 0, 0))
    return pl.pallas_call(
        update_kernel,
        grid=(LCOLS // 2,),
        out_shape=jax.ShapeDtypeStruct((LROWS, LCOLS, TILE, TILE), f32),
        in_specs=[
            pl.BlockSpec(memory_space=pltpu.SMEM),
            pl.BlockSpec((16, 1, TILE, TILE), lambda j: (0, j, 0, 0)),
            pl.BlockSpec((PT, PT, TILE, TILE), lambda j: (1, 2, 0, 0)),
            block,
        ]
        + [vmem] * 5,
        out_specs=block,
        scratch_shapes=[
            pltpu.VMEM((height, KP), bf16),
            pltpu.VMEM((2 * KP, 2 * TILE), bf16),
            pltpu.VMEM((WIDE, 2 * TILE), f32),
            pltpu.VMEM((KP, 2 * TILE), bf16),
            pltpu.VMEM((height, PANEL), f32),
            pltpu.VMEM((PANEL, KP), bf16),
            pltpu.VMEM((KP, PANEL), bf16),
            pltpu.VMEM((LROWS, TILE, TILE), f32),
        ],
        compiler_params=pltpu.CompilerParams(vmem_limit_bytes=40 * MIB),
        cost_estimate=pl.CostEstimate(
            flops=24_000_000_000, bytes_accessed=30 * MIB, transcendentals=0
        ),
        name="update",
    )(at, column, column, front, l0, a1, l0_own, inv, inverses)


def move(x, axis, size, to):
    return lax.ppermute(x, axis, [(i, to(i)) for i in range(size)])


def gather_row(x):
    up, down = lambda c: (c + 2) % 8, lambda c: (c - 2) % 8
    own = jnp.concatenate([x, move(x, "col", 8, lambda c: c ^ 1)], axis=0)
    from_up, from_down = move(own, "col", 8, up), move(own, "col", 8, down)
    far = move(from_up[:LROWS], "col", 8, up)
    far2 = move(from_down[LROWS:], "col", 8, down)
    return [own, from_up, from_down, far, far2]


def gather_column(x):
    moves = []
    for y in range(4):
        for core in range(2):
            for z in range(4):
                for xh in range(2):
                    to = ((y + z) % 4 * 2 + xh) * 8 + y * 2 + core
                    moves.append(((y * 2 + core) * 8 + z * 2 + xh, to))
    there = lax.ppermute(x, ("row", "col"), moves)
    top = jnp.broadcast_to(x[:1], (8, TILE, TILE))
    top = lax.all_to_all(top, "col", split_axis=0, concat_axis=0, tiled=True)[:PT]
    return lax.all_gather(jnp.concatenate([there, top], axis=0), ("sib", "row"))


def local(child_tiles, child_rows, child_slots, tile_count, inverses):
    grid_rows = lax.axis_size("sib") * lax.axis_size("row")
    columns = lax.axis_size("col")
    devices = grid_rows * columns
    slot_ids = child_slots[0, 0]
    live = tile_count[0]
    row_list = child_rows[0]
    child_row, child_col = slot_ids // CHILD_TILES, slot_ids % CHILD_TILES
    positions = jnp.arange(CHILD_TILES, dtype=i32)
    lookup = lambda x: jnp.sum(
        jnp.where(x[:, None] == positions[None, :], row_list[None, :], 0), axis=1
    )
    parent_row, parent_col = lookup(child_row), lookup(child_col)
    owner = parent_row % grid_rows * columns + parent_col % columns
    target = parent_row // grid_rows * LCOLS + parent_col // columns
    order = jnp.arange(slot_ids.shape[0], dtype=i32)
    is_live = order < live
    earlier = (
        (owner[:, None] == owner[None, :])
        & is_live[None, :]
        & (order[None, :] < order[:, None])
    )
    rank = jnp.sum(earlier.astype(i32), axis=1)
    place = jnp.where(is_live, owner * CAP + rank, devices * CAP)
    filled = place[None, :] == jnp.arange(devices * CAP, dtype=i32)[:, None]
    destined = jnp.sum(jnp.where(filled, target[None, :] + 1, 0), axis=1)
    me = lax.axis_index(("sib", "row", "col"))
    mine = jnp.arange(devices, dtype=i32) == me
    meta = jnp.where(mine, destined.reshape(devices, CAP, 1), 0).astype(f32)
    meta = jnp.pad(meta, ((0, 0), (0, META - CAP), (0, 0)))
    outgoing = pack(place, live, child_tiles[0, 0], meta)
    arrived = lax.all_to_all(
        outgoing, ("sib", "row", "col"), split_axis=0, concat_axis=0, tiled=True
    )
    panel, landing = add_up(True, arrived)
    column = gather_column(panel)
    pieces = gather_row(panel)
    row = lax.axis_index("row")
    col = lax.axis_index("col")
    at = jnp.stack([lax.axis_index("sib"), row // 2, row % 2, col // 2, col % 2])
    at = at.astype(i32)
    front = add_up(False, arrived, landing)
    l0, a1, l0_own, inv = rows_factor(at, pieces, inverses)
    out = update(at, column, front, l0, a1, l0_own, inv, inverses)
    return out.reshape(LROWS, 1, LCOLS, 1, TILE, TILE)


def solution(mesh):
    return jax.shard_map(
        local,
        mesh=mesh,
        in_specs=(
            P("sib", ("row", "col"), None, None, None),
            P("sib", None),
            P("sib", ("row", "col"), None),
            P("sib", ("row", "col")),
            P(),
        ),
        out_specs=P(None, ("sib", "row"), None, "col", None, None),
        check_vma=False,
    )
```

time: 418 us -> 396 us (0.947)
  starting transfers between devices: 28.1 us -> 9.38 us
  blocking collectives: 206 us -> 224 us
  waiting for transfers between devices: 62.3 us -> 47.5 us
  Pallas kernels: 78.1 us -> 70.6 us
    ppermute x4 -> x1, waiting for transfers between devices: 21.8 us -> 0.01 us  [gather_column(): there = lax.ppermute(x, ('row', 'col'), moves)]
    all_to_all x0 -> x1, blocking collectives: none -> 18.6 us  [gather_column(): lax.all_to_all(top, 'col', split_axis=0, concat_axis=0, tiled=True)[:PT]]
    ppermute x11 -> x5, starting transfers between devices: 19.9 us -> 6.57 us  [move(): return lax.ppermute(x, axis, [(i, to(i)) for i in range(size)])]
    all_gather x1, waiting for transfers between devices: 0.01 us -> 11.9 us  [gather_column(): return lax.all_gather(jnp.concatenate([there, top], axis=0), ('sib', 'row'))]
    pallas_call x1, Pallas kernels: 15.1 us -> 4.19 us  [rows_factor(): pl.pallas_call(rows_kernel, out_shape=[jax.ShapeDtypeStruct(s, t) for s,...]
    ppermute x4 -> x1, starting transfers between devices: 8.21 us -> 2.8 us  [gather_column(): there = lax.ppermute(x, ('row', 'col'), moves)]
    ppermute x11 -> x5, waiting for transfers between devices: 40.4 us -> 35.6 us  [move(): return lax.ppermute(x, axis, [(i, to(i)) for i in range(size)])]
    unnamed x35 -> x27, local copies, waits for them, and re-layouts: 17.1 us -> 21.3 us
  transfers between devices with their start and end apart: 16 -> 7, of which waited for: 7 -> 3; matrix products, arithmetic and copies ran while one was open for 1% -> 1% of each run, Pallas kernels for 5% -> 3%
where the time goes in v2:
time: 396 us; the launch traced here: 393 us
  blocking collectives  224 us (57%)
  Pallas kernels  70.6 us (18%)
  waiting for transfers between devices  47.5 us (12%)
  local copies, waits for them, and re-layouts  24.2 us (6%)
  between operations  14.2 us (4%)
  starting transfers between devices  9.38 us (2%)
    all_to_all x1, blocking collectives, local(): lax.all_to_all(outgoing, ('sib', 'row', 'col'), split_axis=0, concat_axis...  206 us
    pallas_call x1, Pallas kernels, update(): pl.pallas_call(update_kernel, grid=(LCOLS // 2,), out_shape=jax.ShapeDtyp...  39.2 us
    ppermute x5, waiting for transfers between devices, move(): return lax.ppermute(x, axis, [(i, to(i)) for i in range(size)])  35.6 us
    unnamed x27, local copies, waits for them, and re-layouts  21.3 us
    all_to_all x1, blocking collectives, gather_column(): lax.all_to_all(top, 'col', split_axis=0, concat_axis=0, tiled=True)[:PT]  18.6 us
    all_gather x1, waiting for transfers between devices, gather_column(): return lax.all_gather(jnp.concatenate([there, top], axis=0), ('sib', 'row'))  11.9 us
    pallas_call x1, Pallas kernels, pack(): pl.pallas_call(pack_kernel, out_shape=jax.ShapeDtypeStruct((devices, CAP...  10.7 us
    pallas_call x1, Pallas kernels, add_up(): pl.pallas_call(functools.partial(add_kernel, True), out_shape=[jax.ShapeD...  8.94 us
  transfers between devices with their start and end apart: 7, of which 3 were waited for; matrix products, arithmetic and copies ran while one was open for 1% of the time, Pallas kernels for 3%

profile of v2, /device:TPU:3, one launch (start us, length us, event | category | flops | bytes accessed | tf_op | source)
XLA Modules:
  0.0 393.3 jit_solution(1242772903733730079)
XLA Ops:
  6.5 0.0 all-gather.3.cloned.1.call-start
  7.2 0.7 and_select_fusion.5
  7.9 0.7 select_reduce_fusion.1
  8.7 0.2 convert_reduce_fusion
  8.8 0.1 select_reduce_fusion
  9.0 0.1 broadcast_in_dim.78
  9.1 0.2 select_convert_fusion
  9.4 0.0 copy-start
  9.4 3.4 copy-done
  12.7 10.7 %pack.1 = f32[128,264,128]{2,1,0:T(8,128)S(1)} custom-call(s32[128]{0:T(128)S(1)} %add_select_fusion.place, s32[1]{0:T(128)} %bitcast.32.live, f32[128,128,128]{2,1,0:T(8,128)S(1)} %bitcast.33, f32[128,8,128]{2,1,0:T(8,128)S(1)} %pad.4.meta), custom_call_target="tpu_custom_call" | custom-call | tf_op jit(solution)/shard_map/pack/pallas_call | solution.py:47
  23.4 205.8 %all_to_all.10.refs_0_.refs_1_ = f32[128,264,128]{2,1,0:T(8,128)} all-to-all(f32[128,264,128]{2,1,0:T(8,128)S(1)} %pack.1), channel_id=1, replica_groups=mesh['sib'=2,'row'=8,'col'=8] {'sib','row','col'}, dimensions={0} | all-to-all | bytes 34603008 | tf_op jit(solution)/shard_map/all_to_all | solution.py:440
  229.2 8.9 %add_panel.1 = (f32[8,128,128]{2,1,0:T(8,128)}, s32[8,128]{1,0:T(8,128)}) custom-call(f32[128,264,128]{2,1,0:T(8,128)} %all_to_all.10.refs_0_.refs_1_), custom_call_target="tpu_custom_call" | custom-call | tf_op jit(solution)/shard_map/add_panel/pallas_call | solution.py:124
  238.2 0.0 copy-start.2
  238.2 2.8 collective-permute-start
  241.0 0.9 slice_bitcast_fusion
  241.9 18.6 %all_to_all.11 = f32[8,128,128]{2,1,0:T(8,128)S(1)} all-to-all(f32[8,128,128]{2,1,0:T(8,128)S(1)} %broadcast_in_dim.82), channel_id=1, replica_groups=mesh['sib'=2,'row'=8,'col'=8] {'col'}, dimensions={0} | all-to-all | bytes 1048576 | tf_op jit(solution)/shard_map/all_to_all | solution.py:405
  260.6 0.0 collective-permute-done
  260.6 0.9 pad_maximum_fusion
  261.5 0.0 all-gather.3.cloned.1.call-update
  261.5 0.4 collective-permute-start.1
  261.9 1.1 constant_dynamic-update-slice_fusion.1
  263.0 15.4 %collective-permute-done.1 = f32[8,128,128]{2,1,0:T(8,128)S(1)} collective-permute-done((f32[8,128,128]{2,1,0:T(8,128)}, f32[8,128,128]{2,1,0:T(8,128)S(1)}, u32[]{:S(2)}, u32[]{:S(2)}) %collective-permute-start.1) | collective-permute-done | bytes 524320 | tf_op jit(solution)/shard_map/ppermute | solution.py:383
  278.4 3.8 collective-permute-start.3
  282.2 0.3 collective-permute-start.2
  282.5 20.3 %collective-permute-done.3.down = f32[16,128,128]{2,1,0:T(8,128)S(1)} collective-permute-done((f32[16,128,128]{2,1,0:T(8,128)S(1)}, f32[16,128,128]{2,1,0:T(8,128)S(1)}, u32[]{:S(2)}, u32[]{:S(2)}) %collective-permute-start.3) | collective-permute-done | bytes 1048608 | tf_op jit(solution)/shard_map/ppermute | solution.py:383
  302.8 0.8 slice.18
  303.6 2.1 collective-permute-start.5
  305.7 0.0 collective-permute-done.2.up
  305.7 0.8 slice.17
  306.6 0.0 collective-permute-start.4
  306.6 0.1 stack.23.at
  306.6 7.6 %add_all.1.front = f32[8,16,128,128]{3,2,1,0:T(8,128)S(1)} custom-call(s32[8,128]{1,0:T(8,128)S(1)} %copy-done.2, f32[128,264,128]{2,1,0:T(8,128)} %all_to_all.10.refs_0_.refs_1_), custom_call_target="tpu_custom_call" | custom-call | flops 1000 | bytes 25165824 | tf_op jit(solution)/shard_map/add_all/pallas_call | solution.py:141
  314.3 3.2 copy-done.1
  317.5 0.0 collective-permute-done.5.far2
  317.5 0.0 collective-permute-done.4.far
  317.5 4.2 %rows_factor.1 = (bf16[1024,1536]{1,0:T(8,128)(2,1)S(1)}, f32[1024,512]{1,0:T(8,128)S(1)}, f32[8,128,128]{2,1,0:T(8,128)S(1)}, bf16[2,512,1536]{2,1,0:T(8,128)(2,1)S(1)}) custom-call(s32[5]{0:T(128)S(1)} %stack.23.at, f32[16,128,128]{2,1,0:T(8,128)S(1)} %constant_dynamic-update-slice_fusion.own, f32[16,128,128]{2,1,0:T(8,128)S(1)} %collective-permute-done.2.up, ...), custom_call_target="tpu_custom_call" | custom-call | flops 4000000000 | bytes 14680064 | tf_op jit(solution)/shard_map/rows_factor/pallas_call | solution.py:244
  321.7 0.0 copy-start.5
  321.7 1.7 copy-done.5
  323.4 1.7 copy-done.7
  325.1 1.5 copy-done.9
  326.6 0.8 copy-done.11
  327.4 11.9 %all-gather.3.cloned.1.call-done = f32[192,128,128]{2,1,0:T(8,128)} async-done(((f32[12,128,128]{2,1,0:T(8,128)}), f32[192,128,128]{2,1,0:T(8,128)}) %all-gather.3.cloned.1.call-update) | async-done | bytes 12582928 | tf_op jit(solution)/shard_map/all_gather | solution.py:406
  339.2 1.6 copy-done.4
  340.8 1.9 copy-done.6
  342.7 1.9 copy-done.8
  344.6 1.6 copy-done.10
  346.2 1.0 copy-done.12
  347.2 39.2 %update.1 = f32[8,16,128,128]{3,2,1,0:T(8,128)} custom-call(s32[5]{0:T(128)S(1)} %stack.23.at, f32[16,12,128,128]{3,2,1,0:T(8,128)} %bitcast.35, f32[16,12,128,128]{3,2,1,0:T(8,128)} %bitcast.36, f32[8,16,128,128]{3,2,1,0:T(8,128)} %copy-done.1, bf16[1024,1536]{1,0:T(8,128)(2,1)S(1)} %copy-done.6, f32[1024,512]{1,0:T(8,128)S(1)} %copy-done.10, ...), custom_call_target="tpu_custom_call" | custom-call | flops 24000000000 | bytes 31457280 | tf_op jit(solution)/shard_map/update/pallas_call | solution.py:352
  (20 shorter events, 0.2 us)
Async XLA Ops:
  6.5 332.7 %all-gather.3.cloned.1.call-start = ((), (), s32[]{:S(2)}) async-start(), calls=%async_computation.2 | async-start | bytes 13369344 | tf_op jit(solution)/shard_map/all_gather | solution.py:406
  9.4 3.4 copy-start
  238.2 68.5 %copy-start.2 = (s32[8,128]{1,0:T(8,128)S(1)}, s32[8,128]{1,0:T(8,128)}, u32[]{:S(2)}) copy-start(s32[8,128]{1,0:T(8,128)} %get-tuple-element.12.refs_0_) | copy-start | bytes 12292
  238.2 22.4 %collective-permute-start = (f32[8,128,128]{2,1,0:T(8,128)}, f32[8,128,128]{2,1,0:T(8,128)S(1)}, u32[]{:S(2)}, u32[]{:S(2)}) collective-permute-start(f32[8,128,128]{2,1,0:T(8,128)} %get-tuple-element.11), channel_id=1, source_target_pairs={{0,0},{1,8},{2,16},{3,24},{4,32},{5,40},{6,48},{7,56},{8,1},{9,9},... | collective-permute-start | bytes 1572872 | tf_op jit(solution)/shard_map/ppermute | solution.py:403
  261.5 16.9 %collective-permute-start.1 = (f32[8,128,128]{2,1,0:T(8,128)}, f32[8,128,128]{2,1,0:T(8,128)S(1)}, u32[]{:S(2)}, u32[]{:S(2)}) collective-permute-start(f32[8,128,128]{2,1,0:T(8,128)} %get-tuple-element.11), channel_id=1, source_target_pairs={{0,1},{1,0},{2,3},{3,2},{4,5},{5,4},{6,7},{7,6},{8,9},{9,8},{10,11... | collective-permute-start | bytes 1572872 | tf_op jit(solution)/shard_map/ppermute | solution.py:383
  278.4 24.4 %collective-permute-start.3 = (f32[16,128,128]{2,1,0:T(8,128)S(1)}, f32[16,128,128]{2,1,0:T(8,128)S(1)}, u32[]{:S(2)}, u32[]{:S(2)}) collective-permute-start(f32[16,128,128]{2,1,0:T(8,128)S(1)} %constant_dynamic-update-slice_fusion.own), channel_id=1, source_target_pairs={{0,6},{1,7},{2,0},{3,1},{4,2},{5,3},{6,4},{7,5},{8,14},{9,15},{10,... | collective-permute-start | bytes 3145736 | tf_op jit(solution)/shard_map/ppermute | solution.py:383
  282.2 23.5 %collective-permute-start.2 = (f32[16,128,128]{2,1,0:T(8,128)S(1)}, f32[16,128,128]{2,1,0:T(8,128)S(1)}, u32[]{:S(2)}, u32[]{:S(2)}) collective-permute-start(f32[16,128,128]{2,1,0:T(8,128)S(1)} %constant_dynamic-update-slice_fusion.own), channel_id=1, source_target_pairs={{0,2},{1,3},{2,4},{3,5},{4,6},{5,7},{6,0},{7,1},{8,10},{9,11},{10,... | collective-permute-start | bytes 3145736 | tf_op jit(solution)/shard_map/ppermute | solution.py:383
  303.6 13.9 %collective-permute-start.5 = (f32[8,128,128]{2,1,0:T(8,128)}, f32[8,128,128]{2,1,0:T(8,128)}, u32[]{:S(2)}, u32[]{:S(2)}) collective-permute-start(f32[8,128,128]{2,1,0:T(8,128)} %slice.18), channel_id=1, source_target_pairs={{0,6},{1,7},{2,0},{3,1},{4,2},{5,3},{6,4},{7,5},{8,14},{9,15},{10,... | collective-permute-start | bytes 1572872 | tf_op jit(solution)/shard_map/ppermute | solution.py:383
  306.6 11.0 %collective-permute-start.4 = (f32[8,128,128]{2,1,0:T(8,128)}, f32[8,128,128]{2,1,0:T(8,128)}, u32[]{:S(2)}, u32[]{:S(2)}) collective-permute-start(f32[8,128,128]{2,1,0:T(8,128)} %slice.17), channel_id=1, source_target_pairs={{0,2},{1,3},{2,4},{3,5},{4,6},{5,7},{6,0},{7,1},{8,10},{9,11},{10,... | collective-permute-start | bytes 1572872 | tf_op jit(solution)/shard_map/ppermute | solution.py:383
  306.6 10.9 %copy-start.3 = (f32[2,512,512]{2,1,0:T(8,128)S(1)}, f32[2,512,512]{2,1,0:T(8,128)}, u32[]{:S(2)}) copy-start(f32[2,512,512]{2,1,0:T(8,128)} %inverses.3) | copy-start | bytes 6291460
  314.3 3.2 copy-start.1
  321.7 1.7 copy-start.5
  323.4 1.7 copy-start.7
  325.1 1.5 copy-start.9
  326.5 0.8 copy-start.11
  339.2 1.6 copy-start.4
  340.8 1.9 copy-start.6
  342.7 1.9 copy-start.8
  344.6 1.6 copy-start.10
  346.2 1.0 copy-start.12
Sparse Core Ops, SparseCore 0:
  261.6 77.5 all-gather.2

commit v3 on v2

--- a/solution.py
+++ b/solution.py
@@ -55,7 +55,7 @@
         ],
         out_specs=pl.BlockSpec(memory_space=pl.ANY),
         scratch_shapes=[pltpu.SemaphoreType.DMA, pltpu.SemaphoreType.DMA],
-        compiler_params=pltpu.CompilerParams(vmem_limit_bytes=16 * MIB),
+        compiler_params=pltpu.CompilerParams(vmem_limit_bytes=60 * MIB),
         name="pack",
     )(place, live, tiles, meta)
 
@@ -153,179 +153,158 @@
 
 
 BLOCK = 256
+KB = 3 * BLOCK
 KP = 3 * PANEL
 
 
-def left_form(ref, rows, lane, x):
+def left_form(ref, lane, x):
     hi, lo = split(x)
     for k in range(x.shape[1] // BLOCK):
         for part, half in enumerate((hi, hi, lo)):
             at = lane + (3 * k + part) * BLOCK
-            ref[rows, at : at + BLOCK] = half[:, k * BLOCK : (k + 1) * BLOCK]
-
-
-def right_form(ref, row, x):
+            ref[:, at : at + BLOCK] = half[:, k * BLOCK : (k + 1) * BLOCK]
+
+
+def right_rows(ref, x):
+    hi, lo = split(x)
+    for k in range(x.shape[1] // BLOCK):
+        for part, half in enumerate((hi, lo, hi)):
+            at = (3 * k + part) * BLOCK
+            ref[:, at : at + BLOCK] = half[:, k * BLOCK : (k + 1) * BLOCK]
+
+
+def right_columns(ref, x):
     hi, lo = split(x)
     for k in range(x.shape[0] // BLOCK):
         for part, half in enumerate((hi, lo, hi)):
-            at = row + (3 * k + part) * BLOCK
+            at = (3 * k + part) * BLOCK
             ref[at : at + BLOCK, :] = half[k * BLOCK : (k + 1) * BLOCK, :]
 
 
-def mul(a, b):
+def times(a, b):
     return jnp.dot(a, b, preferred_element_type=f32)
 
 
-def row_place(at):
-    sib, y, core, z, xh = (at[i] for i in range(5))
-    return (sib * 4 + y) * 2 + core, z * 2 + xh
-
-
-def rows_kernel(at, own, up, down, far, far2, inverses, l0, a1, l0_own, inv, raw, left, w0):
-    z, xh = at[3], at[4]
-    my_row, my_col = row_place(at)
-    around = lambda dz, flip: (z + dz + 4) % 4 * 2 + jnp.where(flip, 1 - xh, xh)
-    pieces = [
-        (own, 0, around(0, False)),
-        (own, 8, around(0, True)),
+def times_transposed(a, b):
+    return lax.dot_general(a, b, (((1,), (1,)), ((), ())), preferred_element_type=f32)
+
+
+def inverse_transposed(x, w):
+    return times_transposed(x[:, :KB], w[:BLOCK, :KB]), times_transposed(x[...], w[BLOCK:, :])
+
+
+def inverse(x, w):
+    return times(x[...], w[:, :BLOCK]), times(x[:, KB:], w[KB:, BLOCK:])
+
+
+def row_factors(at, pieces, corner, inverses, z, own, f0, f1, left, r_rows, r_cols, low):
+    dz, xh = at[3], at[4]
+    row = (at[0] * 4 + at[1]) * 2 + at[2]
+    col = dz * 2 + xh
+    around = lambda d, other: (dz + d + 4) % 4 * 2 + (1 - xh if other else xh)
+    here, up, down, far, far2 = pieces
+    for piece, first, source in (
+        (here, 0, around(0, False)),
+        (here, 8, around(0, True)),
         (up, 0, around(-1, False)),
         (up, 8, around(-1, True)),
         (down, 0, around(1, False)),
         (down, 8, around(1, True)),
         (far, 0, around(2, False)),
         (far2, 0, around(2, True)),
-    ]
-    for piece, first, source in pieces:
+    ):
         lanes = pl.ds(pl.multiple_of(source % PT * TILE, TILE), TILE)
-
-        @pl.when(source < PT)
+        for panel, ref in enumerate((f0, f1)):
+
+            @pl.when(source // PT == panel)
+            def _():
+                for a in range(LROWS):
+                    ref[a * TILE : (a + 1) * TILE, lanes] = piece[first + a]
+
+    tile = jnp.where(lax.broadcasted_iota(i32, (LROWS * TILE, 1), 0) < TILE, row, NF)
+    my_lanes = pl.ds(pl.multiple_of(col % PT * TILE, TILE), TILE)
+
+    def keep(ref, tiles):
+        for a in range(tiles):
+            own[a] = ref[a * TILE : (a + 1) * TILE, my_lanes]
+
+    right_rows(r_rows, inverses[0])
+    for i in range(PT):
+        for j in range(PT):
+            low[i * TILE : (i + 1) * TILE, j * TILE : (j + 1) * TILE] = corner[i, j]
+    left_form(left.at[:PANEL], 0, low[...])
+    one, two = inverse_transposed(left.at[:PANEL], r_rows)
+    low[:, :BLOCK] = one
+    low[:, BLOCK:] = two
+    left_form(left, 0, f0[...])
+    one, two = inverse_transposed(left, r_rows)
+    f0[:, :BLOCK] = jnp.where(tile >= PT, one, 0.0)
+    f0[:, BLOCK:] = jnp.where(tile >= PT, two, 0.0)
+
+    @pl.when(col < PT)
+    def _():
+        keep(f0, LROWS)
+
+    left_form(left, 0, f0[...])
+    right_rows(r_rows, low[...])
+    f1[...] = f1[...] - times_transposed(left[...], r_rows[...])
+
+    @pl.when(col >= PT)
+    def _():
+        keep(f1, 1)
+
+    left_form(left, 0, f1[...])
+    right_rows(r_rows, inverses[1])
+    one, two = inverse_transposed(left, r_rows)
+    f1[:, :BLOCK] = jnp.where(tile >= 2 * PT, one, 0.0)
+    f1[:, BLOCK:] = jnp.where(tile >= 2 * PT, two, 0.0)
+
+    @pl.when(col >= PT)
+    def _():
+        for a in range(1, LROWS):
+            own[a] = f1[a * TILE : (a + 1) * TILE, my_lanes]
+
+        @pl.when(row >= 2 * PT)
         def _():
-            for a in range(LROWS):
-                raw[a * TILE : (a + 1) * TILE, lanes] = piece[first + a]
-
-        @pl.when(source >= PT)
-        def _():
-            for a in range(LROWS):
-                a1[a * TILE : (a + 1) * TILE, lanes] = piece[first + a]
-
-    for p in range(NPANEL):
-        left_form(inv.at[p], slice(None), 0, inverses[p])
-    right_form(w0, 0, inverses[0].T)
-    height = 512
-    for i in range(LROWS * TILE // height):
-        rows = slice(i * height, (i + 1) * height)
-        left_form(left, rows, 0, raw[rows, :])
-        low = mul(left[rows, : KP // 2], w0[: KP // 2, :BLOCK])
-        high = mul(left[rows, :], w0[:, BLOCK:])
-        if i == 0:
-            tile = jnp.where(
-                lax.broadcasted_iota(i32, (height, 1), 0) < TILE, my_row, NF
-            )
-            low = jnp.where(tile >= PT, low, 0.0)
-            high = jnp.where(tile >= PT, high, 0.0)
-        raw[rows, :BLOCK] = low
-        raw[rows, BLOCK:] = high
-        left_form(l0, rows, 0, low)
-        left_form(l0, rows, KP // 2, high)
-    lanes = pl.ds(pl.multiple_of(my_col % PT * TILE, TILE), TILE)
-    for a in range(LROWS):
-        l0_own[a] = raw[a * TILE : (a + 1) * TILE, lanes]
-
-
-def rows_factor(at, pieces, inverses):
-    vmem = pl.BlockSpec(memory_space=pltpu.VMEM)
-    height = LROWS * TILE
-    shapes = [
-        ((height, KP), bf16),
-        ((height, PANEL), f32),
-        ((LROWS, TILE, TILE), f32),
-        ((NPANEL, PANEL, KP), bf16),
-    ]
-    return pl.pallas_call(
-        rows_kernel,
-        out_shape=[jax.ShapeDtypeStruct(s, t) for s, t in shapes],
-        in_specs=[pl.BlockSpec(memory_space=pltpu.SMEM)] + [vmem] * 6,
-        out_specs=[vmem] * 4,
-        scratch_shapes=[
-            pltpu.VMEM((height, PANEL), f32),
-            pltpu.VMEM((height, KP), bf16),
-            pltpu.VMEM((KP, PANEL), bf16),
-        ],
-        compiler_params=pltpu.CompilerParams(vmem_limit_bytes=32 * MIB),
-        cost_estimate=pl.CostEstimate(
-            flops=4_000_000_000, bytes_accessed=14 * MIB, transcendentals=0
-        ),
-        name="rows_factor",
-    )(at, *pieces, inverses)
+            own[0] = f1[:TILE, my_lanes]
+
+    left_form(left, 0, f1[...])
+    right_columns(r_cols, inverses[1])
+    one, two = inverse(left, r_cols)
+    f1[:, :BLOCK] = one
+    f1[:, BLOCK:] = two
+    left_form(z, KP, f1[...])
+    right_columns(r_cols, low[...])
+    f0[...] = f0[...] - times(z[:, KP:], r_cols[...])
+    left_form(left, 0, f0[...])
+    right_columns(r_cols, inverses[0])
+    one, two = inverse(left, r_cols)
+    f0[:, :BLOCK] = one
+    f0[:, BLOCK:] = two
+    left_form(z, 0, f0[...])
 
 
 def update_kernel(
-    at, column, corner, front, l0, a1, l0_own, inv, inverses, out, l1, c, raw, right, big, low, low_t, l1_own
+    at, column, corner, front, here, up, down, far, far2, inverses, out,
+    z, right, raw, own, f0, f1, left, r_rows, r_cols, low,
 ):
     step = pl.program_id(0)
-    z = at[3]
-    my_row, my_col = row_place(at)
-
-    def factor_columns(x, inverse, put):
-        put(0, mul(inverse[:BLOCK, : KP // 2], x[: KP // 2, :]))
-        put(1, mul(inverse[BLOCK:, :], x[...]))
 
     @pl.when(step == 0)
     def _():
-        for i in range(PT):
-            for j in range(PT):
-                raw_t = corner[i, j].T
-                big[j * TILE : (j + 1) * TILE, i * TILE : (i + 1) * TILE] = raw_t
-        right_form(low_t, 0, big[:PANEL, :])
-
-        def put(half, value):
-            big[half * BLOCK : (half + 1) * BLOCK, :] = value
-
-        factor_columns(low_t, inv[0], put)
-        right_form(low_t, 0, big[:PANEL, :])
-        left_form(low, slice(None), 0, big[:PANEL, :].T)
-        big[...] = a1[...] - mul(l0[...], low_t[...])
-        left_form(l1, slice(None), 0, big[...])
-        right_form(low_t, 0, inverses[1].T)
-        tile = jnp.where(
-            lax.broadcasted_iota(i32, (LROWS * TILE, 1), 0) < TILE, my_row, NF
+        pieces = here, up, down, far, far2
+        row_factors(
+            at, pieces, corner, inverses, z, own, f0, f1, left, r_rows, r_cols, low
         )
-        first = mul(l1[:, : KP // 2], low_t[: KP // 2, :BLOCK])
-        second = mul(l1[...], low_t[:, BLOCK:])
-        first = jnp.where(tile >= 2 * PT, first, 0.0)
-        second = jnp.where(tile >= 2 * PT, second, 0.0)
-        big[:, :BLOCK] = first
-        big[:, BLOCK:] = second
-        left_form(l1, slice(None), 0, first)
-        left_form(l1, slice(None), KP // 2, second)
-        lanes = pl.ds(pl.multiple_of(my_col % PT * TILE, TILE), TILE)
-        for t in range(LROWS):
-            l1_own[t] = big[t * TILE : (t + 1) * TILE, lanes]
 
     for s in range(2):
         for py in range(4):
             for pc in range(2):
-                source = (py - z + 4) % 4 * 2 + pc
-                rows = pl.ds(pl.multiple_of(source * TILE, TILE), TILE)
-                tile_t = column[(s * 4 + py) * 2 + pc, 0].T
-                raw[rows, s * TILE : (s + 1) * TILE] = tile_t
-    col_tile = jnp.where(
-        (step == 0) & (lax.broadcasted_iota(i32, (1, 2 * TILE), 1) < TILE), my_col, NF
-    )
-    right_form(right, 0, raw[:PANEL, :])
-
-    def put(panel):
-        def store(half, value):
-            value = jnp.where(col_tile >= (panel + 1) * PT, value, 0.0)
-            right_form(c, panel * KP + half * KP // 2, value)
-
-        return store
-
-    factor_columns(right, inv[0], put(0))
-    right_form(right, 0, raw[PANEL:, :] - mul(low[...], c[:KP, :]))
-    factor_columns(right, inv[1], put(1))
-
-    change = mul(l0[...], c[:KP, :]) + mul(l1[...], c[KP:, :])
+                source = (py - at[3] + 4) % 4 * 2 + pc
+                lanes = pl.ds(pl.multiple_of(source * TILE, TILE), TILE)
+                raw[s * TILE : (s + 1) * TILE, lanes] = column[(s * 4 + py) * 2 + pc, 0]
+    right_rows(right, raw[...])
+    change = times_transposed(z[...], right[...])
     for t in range(LROWS):
         for b in range(2):
             piece = change[t * TILE : (t + 1) * TILE, b * TILE : (b + 1) * TILE]
@@ -333,19 +312,15 @@
 
     @pl.when(step == 0)
     def _():
-        for own, mine in ((l0_own, my_col < PT), (l1_own, my_col >= PT)):
-
-            @pl.when(mine)
-            def _():
-                for t in range(1, LROWS):
-                    out[t, 0] = own[t]
-
-                @pl.when((my_row >= 2 * PT) | ((my_row >= PT) & (my_col < PT)))
-                def _():
-                    out[0, 0] = own[0]
-
-
-def update(at, column, front, l0, a1, l0_own, inv, inverses):
+        for t in range(1, LROWS):
+            out[t, 0] = own[t]
+
+        @pl.when((at[0] * 4 + at[1]) * 2 + at[2] >= PT)
+        def _():
+            out[0, 0] = own[0]
+
+
+def update(at, column, front, pieces, inverses):
     height = LROWS * TILE
     vmem = pl.BlockSpec(memory_space=pltpu.VMEM)
     block = pl.BlockSpec((LROWS, 2, TILE, TILE), lambda j: (0, j, 0, 0))
@@ -359,24 +334,26 @@
             pl.BlockSpec((PT, PT, TILE, TILE), lambda j: (1, 2, 0, 0)),
             block,
         ]
-        + [vmem] * 5,
+        + [vmem] * 6,
         out_specs=block,
         scratch_shapes=[
+            pltpu.VMEM((height, 2 * KP), bf16),
+            pltpu.VMEM((2 * TILE, 2 * KP), bf16),
+            pltpu.VMEM((2 * TILE, WIDE), f32),
+            pltpu.VMEM((LROWS, TILE, TILE), f32),
+            pltpu.VMEM((height, PANEL), f32),
+            pltpu.VMEM((height, PANEL), f32),
             pltpu.VMEM((height, KP), bf16),
-            pltpu.VMEM((2 * KP, 2 * TILE), bf16),
-            pltpu.VMEM((WIDE, 2 * TILE), f32),
-            pltpu.VMEM((KP, 2 * TILE), bf16),
-            pltpu.VMEM((height, PANEL), f32),
             pltpu.VMEM((PANEL, KP), bf16),
             pltpu.VMEM((KP, PANEL), bf16),
-            pltpu.VMEM((LROWS, TILE, TILE), f32),
+            pltpu.VMEM((PANEL, PANEL), f32),
         ],
         compiler_params=pltpu.CompilerParams(vmem_limit_bytes=40 * MIB),
         cost_estimate=pl.CostEstimate(
             flops=24_000_000_000, bytes_accessed=30 * MIB, transcendentals=0
         ),
         name="update",
-    )(at, column, column, front, l0, a1, l0_own, inv, inverses)
+    )(at, column, column, front, *pieces, inverses)
 
 
 def move(x, axis, size, to):
@@ -448,8 +425,7 @@
     at = jnp.stack([lax.axis_index("sib"), row // 2, row % 2, col // 2, col % 2])
     at = at.astype(i32)
     front = add_up(False, arrived, landing)
-    l0, a1, l0_own, inv = rows_factor(at, pieces, inverses)
-    out = update(at, column, front, l0, a1, l0_own, inv, inverses)
+    out = update(at, column, front, pieces, inverses)
     return out.reshape(LROWS, 1, LCOLS, 1, TILE, TILE)
 
 

time: 396 us -> 622 us (1.57)
  Pallas kernels: 70.6 us -> 259 us
  blocking collectives: 224 us -> 269 us
  local copies, waits for them, and re-layouts: 24.2 us -> 9.6 us
  waiting for transfers between devices: 47.5 us -> 55.9 us
    pallas_call x1, Pallas kernels: 10.7 us -> 211 us  [pack(): pl.pallas_call(pack_kernel, out_shape=jax.ShapeDtypeStruct((devices, CAP...]
    all_to_all x1, blocking collectives: 206 us -> 249 us  [local(): lax.all_to_all(outgoing, ('sib', 'row', 'col'), split_axis=0, concat_axis...]
    unnamed x27 -> x9, local copies, waits for them, and re-layouts: 21.3 us -> 5.92 us
    all_gather x1, waiting for transfers between devices: 11.9 us -> 22.5 us  [gather_column(): return lax.all_gather(jnp.concatenate([there, top], axis=0), ('sib', 'row'))]
    pallas_call x1, Pallas kernels: 39.2 us -> 32.3 us  [update(): pl.pallas_call(update_kernel, grid=(LCOLS // 2,), out_shape=jax.ShapeDtyp...]
  transfers between devices with their start and end apart: 7 -> 7, of which waited for: 3 -> 3; matrix products, arithmetic and copies ran while one was open for 1% -> 1% of each run, Pallas kernels for 3% -> 1%
where the time goes in v3:
time: 622 us; the launch traced here: 621 us
  blocking collectives  269 us (43%)
  Pallas kernels  259 us (42%)
  waiting for transfers between devices  55.9 us (9%)
  between operations  14.2 us (2%)
  starting transfers between devices  10.7 us (2%)
  local copies, waits for them, and re-layouts  9.6 us (2%)
    all_to_all x1, blocking collectives, local(): lax.all_to_all(outgoing, ('sib', 'row', 'col'), split_axis=0, concat_axis...  249 us
    pallas_call x1, Pallas kernels, pack(): pl.pallas_call(pack_kernel, out_shape=jax.ShapeDtypeStruct((devices, CAP...  211 us
    ppermute x5, waiting for transfers between devices, move(): return lax.ppermute(x, axis, [(i, to(i)) for i in range(size)])  33.4 us
    pallas_call x1, Pallas kernels, update(): pl.pallas_call(update_kernel, grid=(LCOLS // 2,), out_shape=jax.ShapeDtyp...  32.3 us
    all_gather x1, waiting for transfers between devices, gather_column(): return lax.all_gather(jnp.concatenate([there, top], axis=0), ('sib', 'row'))  22.5 us
    all_to_all x1, blocking collectives, gather_column(): lax.all_to_all(top, 'col', split_axis=0, concat_axis=0, tiled=True)[:PT]  19.6 us
  transfers between devices with their start and end apart: 7, of which 3 were waited for; matrix products, arithmetic and copies ran while one was open for 1% of the time, Pallas kernels for 1%

profile of v3, /device:TPU:3, one launch (start us, length us, event | category | flops | bytes accessed | tf_op | source)
XLA Modules:
  0.0 620.8 jit_solution(13794872179180062959)
XLA Ops:
  6.5 0.0 all-gather.3.cloned.1.call-start
  7.2 0.7 and_select_fusion.5
  7.9 0.7 select_reduce_fusion.1
  8.7 0.2 convert_reduce_fusion
  8.8 0.0 copy-start.3
  8.9 0.1 select_reduce_fusion
  9.0 0.1 broadcast_in_dim.78
  9.1 0.2 select_convert_fusion
  9.3 0.8 pad.4.meta
  10.2 0.0 copy-done.3
  10.2 210.6 %pack.1 = f32[128,264,128]{2,1,0:T(8,128)} custom-call(s32[128]{0:T(128)} %copy-done.3, s32[1]{0:T(128)} %bitcast.32.live, f32[128,128,128]{2,1,0:T(8,128)} %bitcast.33, f32[128,8,128]{2,1,0:T(8,128)} %pad.4.meta), custom_call_target="tpu_custom_call" | custom-call | tf_op jit(solution)/shard_map/pack/pallas_call | solution.py:47
  220.8 249.2 %all_to_all.10.refs_0_.refs_1_ = f32[128,264,128]{2,1,0:T(8,128)} all-to-all(f32[128,264,128]{2,1,0:T(8,128)} %pack.1), channel_id=1, replica_groups=mesh['sib'=2,'row'=8,'col'=8] {'sib','row','col'}, dimensions={0} | all-to-all | bytes 34603008 | tf_op jit(solution)/shard_map/all_to_all | solution.py:417
  470.0 8.1 %add_panel.1 = (f32[8,128,128]{2,1,0:T(8,128)}, s32[8,128]{1,0:T(8,128)}) custom-call(f32[128,264,128]{2,1,0:T(8,128)} %all_to_all.10.refs_0_.refs_1_), custom_call_target="tpu_custom_call" | custom-call | tf_op jit(solution)/shard_map/add_panel/pallas_call | solution.py:124
  478.1 0.0 copy-start.1
  478.1 2.9 collective-permute-start
  481.0 0.9 slice_bitcast_fusion
  481.9 19.6 %all_to_all.11 = f32[8,128,128]{2,1,0:T(8,128)S(1)} all-to-all(f32[8,128,128]{2,1,0:T(8,128)S(1)} %broadcast_in_dim.82), channel_id=1, replica_groups=mesh['sib'=2,'row'=8,'col'=8] {'col'}, dimensions={0} | all-to-all | bytes 1048576 | tf_op jit(solution)/shard_map/all_to_all | solution.py:382
  501.5 0.0 collective-permute-done
  501.5 0.9 pad_maximum_fusion
  502.5 0.0 all-gather.3.cloned.1.call-update
  502.5 0.1 collective-permute-start.1
  502.6 1.1 constant_dynamic-update-slice_fusion.1
  503.7 14.8 %collective-permute-done.1 = f32[8,128,128]{2,1,0:T(8,128)S(1)} collective-permute-done((f32[8,128,128]{2,1,0:T(8,128)}, f32[8,128,128]{2,1,0:T(8,128)S(1)}, u32[]{:S(2)}, u32[]{:S(2)}) %collective-permute-start.1) | collective-permute-done | bytes 524320 | tf_op jit(solution)/shard_map/ppermute | solution.py:360
  518.6 4.3 collective-permute-start.3
  522.9 0.0 collective-permute-start.2
  522.9 18.5 %collective-permute-done.3.down = f32[16,128,128]{2,1,0:T(8,128)S(1)} collective-permute-done((f32[16,128,128]{2,1,0:T(8,128)S(1)}, f32[16,128,128]{2,1,0:T(8,128)S(1)}, u32[]{:S(2)}, u32[]{:S(2)}) %collective-permute-start.3) | collective-permute-done | bytes 1048608 | tf_op jit(solution)/shard_map/ppermute | solution.py:360
  541.4 0.8 slice.18
  542.2 3.4 collective-permute-start.5
  545.6 0.0 collective-permute-done.2.up
  545.6 0.9 slice.17
  546.5 0.0 collective-permute-start.4
  546.5 0.1 stack.23.at
  546.5 0.0 copy-done.1
  546.5 7.7 %add_all.1.front = f32[8,16,128,128]{3,2,1,0:T(8,128)S(1)} custom-call(s32[8,128]{1,0:T(8,128)S(1)} %copy-done.1, f32[128,264,128]{2,1,0:T(8,128)} %all_to_all.10.refs_0_.refs_1_), custom_call_target="tpu_custom_call" | custom-call | flops 1000 | bytes 25165824 | tf_op jit(solution)/shard_map/add_all/pallas_call | solution.py:141
  554.3 0.0 copy-start
  554.3 3.2 copy-done
  557.5 0.0 collective-permute-done.5.far2
  557.5 0.0 collective-permute-done.4.far
  557.5 22.5 %all-gather.3.cloned.1.call-done = f32[192,128,128]{2,1,0:T(8,128)} async-done(((f32[12,128,128]{2,1,0:T(8,128)}), f32[192,128,128]{2,1,0:T(8,128)}) %all-gather.3.cloned.1.call-update) | async-done | bytes 12582928 | tf_op jit(solution)/shard_map/all_gather | solution.py:383
  580.0 0.0 copy-start.2
  580.0 1.6 copy-done.2
  581.6 32.3 %update.1 = f32[8,16,128,128]{3,2,1,0:T(8,128)} custom-call(s32[5]{0:T(128)S(1)} %stack.23.at, f32[16,12,128,128]{3,2,1,0:T(8,128)} %bitcast.35, f32[16,12,128,128]{3,2,1,0:T(8,128)} %bitcast.36, f32[8,16,128,128]{3,2,1,0:T(8,128)} %copy-done, f32[16,128,128]{2,1,0:T(8,128)S(1)} %constant_dynamic-update-slice_fusion.here, ...), custom_call_target="tpu_custom_call" | custom-call | flops 24000000000 | bytes 31457280 | tf_op jit(solution)/shard_map/update/pallas_call | solution.py:327
  (7 shorter events, 0.1 us)
Async XLA Ops:
  6.5 573.5 %all-gather.3.cloned.1.call-start = ((), (), s32[]{:S(2)}) async-start(), calls=%async_computation.2 | async-start | bytes 13369344 | tf_op jit(solution)/shard_map/all_gather | solution.py:383
  8.8 1.3 copy-start.3
  478.1 68.5 %copy-start.1 = (s32[8,128]{1,0:T(8,128)S(1)}, s32[8,128]{1,0:T(8,128)}, u32[]{:S(2)}) copy-start(s32[8,128]{1,0:T(8,128)} %get-tuple-element.8.refs_0_) | copy-start | bytes 12292
  478.1 23.4 %collective-permute-start = (f32[8,128,128]{2,1,0:T(8,128)}, f32[8,128,128]{2,1,0:T(8,128)S(1)}, u32[]{:S(2)}, u32[]{:S(2)}) collective-permute-start(f32[8,128,128]{2,1,0:T(8,128)} %get-tuple-element.7), channel_id=1, source_target_pairs={{0,0},{1,8},{2,16},{3,24},{4,32},{5,40},{6,48},{7,56},{8,1},{9,9},... | collective-permute-start | bytes 1572872 | tf_op jit(solution)/shard_map/ppermute | solution.py:380
  502.5 16.0 %collective-permute-start.1 = (f32[8,128,128]{2,1,0:T(8,128)}, f32[8,128,128]{2,1,0:T(8,128)S(1)}, u32[]{:S(2)}, u32[]{:S(2)}) collective-permute-start(f32[8,128,128]{2,1,0:T(8,128)} %get-tuple-element.7), channel_id=1, source_target_pairs={{0,1},{1,0},{2,3},{3,2},{4,5},{5,4},{6,7},{7,6},{8,9},{9,8},{10,11... | collective-permute-start | bytes 1572872 | tf_op jit(solution)/shard_map/ppermute | solution.py:360
  518.6 22.8 %collective-permute-start.3 = (f32[16,128,128]{2,1,0:T(8,128)S(1)}, f32[16,128,128]{2,1,0:T(8,128)S(1)}, u32[]{:S(2)}, u32[]{:S(2)}) collective-permute-start(f32[16,128,128]{2,1,0:T(8,128)S(1)} %constant_dynamic-update-slice_fusion.here), channel_id=1, source_target_pairs={{0,6},{1,7},{2,0},{3,1},{4,2},{5,3},{6,4},{7,5},{8,14},{9,15},{10,... | collective-permute-start | bytes 3145736 | tf_op jit(solution)/shard_map/ppermute | solution.py:360
  522.9 22.7 %collective-permute-start.2 = (f32[16,128,128]{2,1,0:T(8,128)S(1)}, f32[16,128,128]{2,1,0:T(8,128)S(1)}, u32[]{:S(2)}, u32[]{:S(2)}) collective-permute-start(f32[16,128,128]{2,1,0:T(8,128)S(1)} %constant_dynamic-update-slice_fusion.here), channel_id=1, source_target_pairs={{0,2},{1,3},{2,4},{3,5},{4,6},{5,7},{6,0},{7,1},{8,10},{9,11},{10,... | collective-permute-start | bytes 3145736 | tf_op jit(solution)/shard_map/ppermute | solution.py:360
  542.2 15.3 %collective-permute-start.5 = (f32[8,128,128]{2,1,0:T(8,128)}, f32[8,128,128]{2,1,0:T(8,128)}, u32[]{:S(2)}, u32[]{:S(2)}) collective-permute-start(f32[8,128,128]{2,1,0:T(8,128)} %slice.18), channel_id=1, source_target_pairs={{0,6},{1,7},{2,0},{3,1},{4,2},{5,3},{6,4},{7,5},{8,14},{9,15},{10,... | collective-permute-start | bytes 1572872 | tf_op jit(solution)/shard_map/ppermute | solution.py:360
  546.5 11.1 %collective-permute-start.4 = (f32[8,128,128]{2,1,0:T(8,128)}, f32[8,128,128]{2,1,0:T(8,128)}, u32[]{:S(2)}, u32[]{:S(2)}) collective-permute-start(f32[8,128,128]{2,1,0:T(8,128)} %slice.17), channel_id=1, source_target_pairs={{0,2},{1,3},{2,4},{3,5},{4,6},{5,7},{6,0},{7,1},{8,10},{9,11},{10,... | collective-permute-start | bytes 1572872 | tf_op jit(solution)/shard_map/ppermute | solution.py:360
  554.3 3.2 copy-start
  580.0 1.6 copy-start.2
Sparse Core Ops, SparseCore 0:
  502.6 77.3 all-gather.2

commit v4 on v3

--- a/solution.py
+++ b/solution.py
@@ -26,10 +26,7 @@
     return hi, (x - hi.astype(f32)).astype(bf16)
 
 
-def pack_kernel(place, live, tiles, meta, out, sem, meta_sem):
-    head = pltpu.make_async_copy(meta, out.at[:, CAP * TILE :, :], meta_sem)
-    head.start()
-
+def pack_kernel(place, live, tiles, meta, out, sem):
     def copy(m):
         d = place[m] // CAP
         k = place[m] % CAP
@@ -38,8 +35,8 @@
         )
 
     lax.fori_loop(0, live[0], lambda m, c: (copy(m).start(), c)[1], 0)
+    out[:, CAP * TILE :, :] = meta[...]
     lax.fori_loop(0, live[0], lambda m, c: (copy(m).wait(), c)[1], 0)
-    head.wait()
 
 
 def pack(place, live, tiles, meta):
@@ -50,12 +47,12 @@
         in_specs=[
             pl.BlockSpec(memory_space=pltpu.SMEM),
             pl.BlockSpec(memory_space=pltpu.SMEM),
-            pl.BlockSpec(memory_space=pl.ANY),
+            pl.BlockSpec(memory_space=pltpu.HBM),
             pl.BlockSpec(memory_space=pltpu.VMEM),
         ],
-        out_specs=pl.BlockSpec(memory_space=pl.ANY),
-        scratch_shapes=[pltpu.SemaphoreType.DMA, pltpu.SemaphoreType.DMA],
-        compiler_params=pltpu.CompilerParams(vmem_limit_bytes=60 * MIB),
+        out_specs=pl.BlockSpec(memory_space=pltpu.VMEM),
+        scratch_shapes=[pltpu.SemaphoreType.DMA],
+        compiler_params=pltpu.CompilerParams(vmem_limit_bytes=24 * MIB),
         name="pack",
     )(place, live, tiles, meta)
 

time: 622 us -> 383 us (0.62)
  Pallas kernels: 259 us -> 58.3 us
  blocking collectives: 269 us -> 227 us
    pallas_call x1, Pallas kernels: 211 us -> 9.79 us  [pack(): pl.pallas_call(pack_kernel, out_shape=jax.ShapeDtypeStruct((devices, CAP...]
    all_to_all x1, blocking collectives: 249 us -> 208 us  [local(): lax.all_to_all(outgoing, ('sib', 'row', 'col'), split_axis=0, concat_axis...]
  transfers between devices with their start and end apart: 7 -> 7, of which waited for: 3 -> 3; matrix products, arithmetic and copies ran while one was open for 1% -> 1% of each run, Pallas kernels for 1% -> 2%
where the time goes in v4:
time: 383 us; the launch traced here: 381 us
  blocking collectives  227 us (59%)
  Pallas kernels  58.3 us (15%)
  waiting for transfers between devices  57.4 us (15%)
  between operations  14.2 us (4%)
  local copies, waits for them, and re-layouts  12.2 us (3%)
  starting transfers between devices  9.49 us (2%)
    all_to_all x1, blocking collectives, local(): lax.all_to_all(outgoing, ('sib', 'row', 'col'), split_axis=0, concat_axis...  208 us
    ppermute x5, waiting for transfers between devices, move(): return lax.ppermute(x, axis, [(i, to(i)) for i in range(size)])  34.9 us
    pallas_call x1, Pallas kernels, update(): pl.pallas_call(update_kernel, grid=(LCOLS // 2,), out_shape=jax.ShapeDtyp...  32.2 us
    all_gather x1, waiting for transfers between devices, gather_column(): return lax.all_gather(jnp.concatenate([there, top], axis=0), ('sib', 'row'))  22.5 us
    all_to_all x1, blocking collectives, gather_column(): lax.all_to_all(top, 'col', split_axis=0, concat_axis=0, tiled=True)[:PT]  18.8 us
    pallas_call x1, Pallas kernels, pack(): pl.pallas_call(pack_kernel, out_shape=jax.ShapeDtypeStruct((devices, CAP...  9.79 us
    unnamed x9, local copies, waits for them, and re-layouts  9.3 us
    pallas_call x1, Pallas kernels, add_up(): pl.pallas_call(functools.partial(add_kernel, False), out_shape=jax.ShapeD...  8.21 us
  transfers between devices with their start and end apart: 7, of which 3 were waited for; matrix products, arithmetic and copies ran while one was open for 1% of the time, Pallas kernels for 2%

profile of v4, /device:TPU:3, one launch (start us, length us, event | category | flops | bytes accessed | tf_op | source)
XLA Modules:
  0.0 381.4 jit_solution(3492072671691919334)
XLA Ops:
  6.5 0.0 all-gather.3.cloned.1.call-start
  7.2 0.7 and_select_fusion.5
  7.9 0.7 select_reduce_fusion.1
  8.7 0.2 convert_reduce_fusion
  8.8 0.1 select_reduce_fusion
  9.0 0.1 broadcast_in_dim.78
  9.1 0.2 select_convert_fusion
  9.4 0.0 copy-start
  9.4 3.4 copy-done
  12.7 9.8 %pack.1 = f32[128,264,128]{2,1,0:T(8,128)S(1)} custom-call(s32[128]{0:T(128)S(1)} %add_select_fusion.place, s32[1]{0:T(128)} %bitcast.32.live, f32[128,128,128]{2,1,0:T(8,128)S(1)} %bitcast.33, f32[128,8,128]{2,1,0:T(8,128)S(1)} %pad.4.meta), custom_call_target="tpu_custom_call" | custom-call | tf_op jit(solution)/shard_map/pack/pallas_call | solution.py:44
  22.5 208.1 %all_to_all.10.refs_0_.refs_1_ = f32[128,264,128]{2,1,0:T(8,128)} all-to-all(f32[128,264,128]{2,1,0:T(8,128)S(1)} %pack.1), channel_id=1, replica_groups=mesh['sib'=2,'row'=8,'col'=8] {'sib','row','col'}, dimensions={0} | all-to-all | bytes 34603008 | tf_op jit(solution)/shard_map/all_to_all | solution.py:414
  230.7 8.1 %add_panel.1 = (f32[8,128,128]{2,1,0:T(8,128)}, s32[8,128]{1,0:T(8,128)}) custom-call(f32[128,264,128]{2,1,0:T(8,128)} %all_to_all.10.refs_0_.refs_1_), custom_call_target="tpu_custom_call" | custom-call | tf_op jit(solution)/shard_map/add_panel/pallas_call | solution.py:121
  238.8 0.0 copy-start.2
  238.8 3.2 collective-permute-start
  242.0 0.9 slice_bitcast_fusion
  242.9 18.8 %all_to_all.11 = f32[8,128,128]{2,1,0:T(8,128)S(1)} all-to-all(f32[8,128,128]{2,1,0:T(8,128)S(1)} %broadcast_in_dim.82), channel_id=1, replica_groups=mesh['sib'=2,'row'=8,'col'=8] {'col'}, dimensions={0} | all-to-all | bytes 1048576 | tf_op jit(solution)/shard_map/all_to_all | solution.py:379
  261.7 0.0 collective-permute-done
  261.7 0.9 pad_maximum_fusion
  262.6 0.0 all-gather.3.cloned.1.call-update
  262.7 0.1 collective-permute-start.1
  262.8 1.1 constant_dynamic-update-slice_fusion.1
  263.9 14.7 %collective-permute-done.1 = f32[8,128,128]{2,1,0:T(8,128)S(1)} collective-permute-done((f32[8,128,128]{2,1,0:T(8,128)}, f32[8,128,128]{2,1,0:T(8,128)S(1)}, u32[]{:S(2)}, u32[]{:S(2)}) %collective-permute-start.1) | collective-permute-done | bytes 524320 | tf_op jit(solution)/shard_map/ppermute | solution.py:357
  278.6 4.1 %collective-permute-start.3 = (f32[16,128,128]{2,1,0:T(8,128)S(1)}, f32[16,128,128]{2,1,0:T(8,128)S(1)}, u32[]{:S(2)}, u32[]{:S(2)}) collective-permute-start(f32[16,128,128]{2,1,0:T(8,128)S(1)} %constant_dynamic-update-slice_fusion.here), channel_id=1, source_target_pairs={{0,6},{1,7},{2,0},{3,1},{4,2},{5,3},{6,4},{7,5},{8,14},{9,15},{10,... | collective-permute-start | bytes 3145736 | tf_op jit(solution)/shard_map/ppermute | solution.py:357
  282.7 0.6 collective-permute-start.2
  283.3 20.3 %collective-permute-done.3.down = f32[16,128,128]{2,1,0:T(8,128)S(1)} collective-permute-done((f32[16,128,128]{2,1,0:T(8,128)S(1)}, f32[16,128,128]{2,1,0:T(8,128)S(1)}, u32[]{:S(2)}, u32[]{:S(2)}) %collective-permute-start.3) | collective-permute-done | bytes 1048608 | tf_op jit(solution)/shard_map/ppermute | solution.py:357
  303.6 0.8 slice.18
  304.4 1.3 collective-permute-start.5
  305.7 0.0 collective-permute-done.2.up
  305.7 0.9 slice.17
  306.5 0.2 collective-permute-start.4
  306.7 0.1 stack.23.at
  306.8 0.0 copy-done.2
  306.8 8.2 %add_all.1.front = f32[8,16,128,128]{3,2,1,0:T(8,128)S(1)} custom-call(s32[8,128]{1,0:T(8,128)S(1)} %copy-done.2, f32[128,264,128]{2,1,0:T(8,128)} %all_to_all.10.refs_0_.refs_1_), custom_call_target="tpu_custom_call" | custom-call | flops 1000 | bytes 25165824 | tf_op jit(solution)/shard_map/add_all/pallas_call | solution.py:138
  315.0 0.0 copy-start.1
  315.0 3.2 copy-done.1
  318.2 0.0 collective-permute-done.5.far2
  318.2 0.0 collective-permute-done.4.far
  318.2 22.5 %all-gather.3.cloned.1.call-done = f32[192,128,128]{2,1,0:T(8,128)} async-done(((f32[12,128,128]{2,1,0:T(8,128)}), f32[192,128,128]{2,1,0:T(8,128)}) %all-gather.3.cloned.1.call-update) | async-done | bytes 12582928 | tf_op jit(solution)/shard_map/all_gather | solution.py:380
  340.7 0.0 copy-start.3
  340.7 1.6 copy-done.3
  342.3 32.2 %update.1 = f32[8,16,128,128]{3,2,1,0:T(8,128)} custom-call(s32[5]{0:T(128)S(1)} %stack.23.at, f32[16,12,128,128]{3,2,1,0:T(8,128)} %bitcast.35, f32[16,12,128,128]{3,2,1,0:T(8,128)} %bitcast.36, f32[8,16,128,128]{3,2,1,0:T(8,128)} %copy-done.1, f32[16,128,128]{2,1,0:T(8,128)S(1)} %constant_dynamic-update-slice_fusion.here, ...), custom_call_target="tpu_custom_call" | custom-call | flops 24000000000 | bytes 31457280 | tf_op jit(solution)/shard_map/update/pallas_call | solution.py:324
  (8 shorter events, 0.2 us)
Async XLA Ops:
  6.5 334.2 %all-gather.3.cloned.1.call-start = ((), (), s32[]{:S(2)}) async-start(), calls=%async_computation.2 | async-start | bytes 13369344 | tf_op jit(solution)/shard_map/all_gather | solution.py:380
  9.4 3.4 copy-start
  238.8 68.0 %copy-start.2 = (s32[8,128]{1,0:T(8,128)S(1)}, s32[8,128]{1,0:T(8,128)}, u32[]{:S(2)}) copy-start(s32[8,128]{1,0:T(8,128)} %get-tuple-element.8.refs_0_) | copy-start | bytes 12292
  238.8 22.9 %collective-permute-start = (f32[8,128,128]{2,1,0:T(8,128)}, f32[8,128,128]{2,1,0:T(8,128)S(1)}, u32[]{:S(2)}, u32[]{:S(2)}) collective-permute-start(f32[8,128,128]{2,1,0:T(8,128)} %get-tuple-element.7), channel_id=1, source_target_pairs={{0,0},{1,8},{2,16},{3,24},{4,32},{5,40},{6,48},{7,56},{8,1},{9,9},... | collective-permute-start | bytes 1572872 | tf_op jit(solution)/shard_map/ppermute | solution.py:377
  262.7 15.9 %collective-permute-start.1 = (f32[8,128,128]{2,1,0:T(8,128)}, f32[8,128,128]{2,1,0:T(8,128)S(1)}, u32[]{:S(2)}, u32[]{:S(2)}) collective-permute-start(f32[8,128,128]{2,1,0:T(8,128)} %get-tuple-element.7), channel_id=1, source_target_pairs={{0,1},{1,0},{2,3},{3,2},{4,5},{5,4},{6,7},{7,6},{8,9},{9,8},{10,11... | collective-permute-start | bytes 1572872 | tf_op jit(solution)/shard_map/ppermute | solution.py:357
  278.6 25.0 %collective-permute-start.3 = (f32[16,128,128]{2,1,0:T(8,128)S(1)}, f32[16,128,128]{2,1,0:T(8,128)S(1)}, u32[]{:S(2)}, u32[]{:S(2)}) collective-permute-start(f32[16,128,128]{2,1,0:T(8,128)S(1)} %constant_dynamic-update-slice_fusion.here), channel_id=1, source_target_pairs={{0,6},{1,7},{2,0},{3,1},{4,2},{5,3},{6,4},{7,5},{8,14},{9,15},{10,... | collective-permute-start | bytes 3145736 | tf_op jit(solution)/shard_map/ppermute | solution.py:357
  282.7 23.0 %collective-permute-start.2 = (f32[16,128,128]{2,1,0:T(8,128)S(1)}, f32[16,128,128]{2,1,0:T(8,128)S(1)}, u32[]{:S(2)}, u32[]{:S(2)}) collective-permute-start(f32[16,128,128]{2,1,0:T(8,128)S(1)} %constant_dynamic-update-slice_fusion.here), channel_id=1, source_target_pairs={{0,2},{1,3},{2,4},{3,5},{4,6},{5,7},{6,0},{7,1},{8,10},{9,11},{10,... | collective-permute-start | bytes 3145736 | tf_op jit(solution)/shard_map/ppermute | solution.py:357
  304.4 13.9 %collective-permute-start.5 = (f32[8,128,128]{2,1,0:T(8,128)}, f32[8,128,128]{2,1,0:T(8,128)}, u32[]{:S(2)}, u32[]{:S(2)}) collective-permute-start(f32[8,128,128]{2,1,0:T(8,128)} %slice.18), channel_id=1, source_target_pairs={{0,6},{1,7},{2,0},{3,1},{4,2},{5,3},{6,4},{7,5},{8,14},{9,15},{10,... | collective-permute-start | bytes 1572872 | tf_op jit(solution)/shard_map/ppermute | solution.py:357
  306.5 11.7 %collective-permute-start.4 = (f32[8,128,128]{2,1,0:T(8,128)}, f32[8,128,128]{2,1,0:T(8,128)}, u32[]{:S(2)}, u32[]{:S(2)}) collective-permute-start(f32[8,128,128]{2,1,0:T(8,128)} %slice.17), channel_id=1, source_target_pairs={{0,2},{1,3},{2,4},{3,5},{4,6},{5,7},{6,0},{7,1},{8,10},{9,11},{10,... | collective-permute-start | bytes 1572872 | tf_op jit(solution)/shard_map/ppermute | solution.py:357
  315.0 3.2 copy-start.1
  340.7 1.6 copy-start.3
Sparse Core Ops, SparseCore 0:
  262.8 77.8 all-gather.2

commit v5 on v4

--- a/solution.py
+++ b/solution.py
@@ -26,33 +26,27 @@
     return hi, (x - hi.astype(f32)).astype(bf16)
 
 
-def pack_kernel(place, live, tiles, meta, out, sem):
-    def copy(m):
+def pack_kernel(place, live, tiles, meta, out):
+    def put(m, carry):
         d = place[m] // CAP
         k = place[m] % CAP
-        return pltpu.make_async_copy(
-            tiles.at[m], out.at[d, pl.ds(pl.multiple_of(k * TILE, TILE), TILE), :], sem
-        )
-
-    lax.fori_loop(0, live[0], lambda m, c: (copy(m).start(), c)[1], 0)
+        out[d, pl.ds(pl.multiple_of(k * TILE, TILE), TILE), :] = tiles[m]
+        return carry
+
     out[:, CAP * TILE :, :] = meta[...]
-    lax.fori_loop(0, live[0], lambda m, c: (copy(m).wait(), c)[1], 0)
+    lax.fori_loop(0, live[0], put, 0)
 
 
 def pack(place, live, tiles, meta):
     devices = meta.shape[0]
+    vmem = pl.BlockSpec(memory_space=pltpu.VMEM)
+    smem = pl.BlockSpec(memory_space=pltpu.SMEM)
     return pl.pallas_call(
         pack_kernel,
         out_shape=jax.ShapeDtypeStruct((devices, CAP * TILE + META, TILE), f32),
-        in_specs=[
-            pl.BlockSpec(memory_space=pltpu.SMEM),
-            pl.BlockSpec(memory_space=pltpu.SMEM),
-            pl.BlockSpec(memory_space=pltpu.HBM),
-            pl.BlockSpec(memory_space=pltpu.VMEM),
-        ],
-        out_specs=pl.BlockSpec(memory_space=pltpu.VMEM),
-        scratch_shapes=[pltpu.SemaphoreType.DMA],
-        compiler_params=pltpu.CompilerParams(vmem_limit_bytes=24 * MIB),
+        in_specs=[smem, smem, vmem, vmem],
+        out_specs=vmem,
+        compiler_params=pltpu.CompilerParams(vmem_limit_bytes=16 * MIB),
         name="pack",
     )(place, live, tiles, meta)
 
@@ -226,9 +220,13 @@
             own[a] = ref[a * TILE : (a + 1) * TILE, my_lanes]
 
     right_rows(r_rows, inverses[0])
-    for i in range(PT):
+    y_bit = jnp.where(at[1] >= 2, at[1], 3 - at[1]) - 2
+    for k in range(PT):
+        i = (y_bit ^ (k & 1)) * 2 + (at[2] ^ (k >> 1))
+        rows = pl.ds(pl.multiple_of(i * TILE, TILE), TILE)
         for j in range(PT):
-            low[i * TILE : (i + 1) * TILE, j * TILE : (j + 1) * TILE] = corner[i, j]
+            here = corner[k >> 1][(k & 1) * PT + j]
+            low[rows, j * TILE : (j + 1) * TILE] = here
     left_form(left.at[:PANEL], 0, low[...])
     one, two = inverse_transposed(left.at[:PANEL], r_rows)
     low[:, :BLOCK] = one
@@ -282,24 +280,36 @@
 
 
 def update_kernel(
-    at, column, corner, front, here, up, down, far, far2, inverses, out,
-    z, right, raw, own, f0, f1, left, r_rows, r_cols, low,
+    at, *refs
 ):
+    columns, pieces, corner = refs[:10], refs[10:15], refs[15:17]
+    front, inverses, out = refs[17:20]
+    z, right, raw, own, f0, f1, left, r_rows, r_cols, low = refs[20:]
     step = pl.program_id(0)
 
     @pl.when(step == 0)
     def _():
-        pieces = here, up, down, far, far2
         row_factors(
             at, pieces, corner, inverses, z, own, f0, f1, left, r_rows, r_cols, low
         )
 
-    for s in range(2):
-        for py in range(4):
-            for pc in range(2):
-                source = (py - at[3] + 4) % 4 * 2 + pc
-                lanes = pl.ds(pl.multiple_of(source * TILE, TILE), TILE)
-                raw[s * TILE : (s + 1) * TILE, lanes] = column[(s * 4 + py) * 2 + pc, 0]
+    for k in range(2):
+        core = at[2] ^ k
+        here, up, down, far, far2 = columns[5 * k : 5 * k + 5]
+        for ref, n, other, dy in (
+            (here, 0, 0, 0),
+            (here, 1, 1, 0),
+            (up, 0, 0, -1),
+            (up, 1, 1, -1),
+            (down, 0, 0, 1),
+            (down, 1, 1, 1),
+            (far, 0, 0, 2),
+            (far2, 0, 1, 2),
+        ):
+            source = (at[1] + dy - at[3] + 8) % 4 * 2 + core
+            rows = pl.ds(pl.multiple_of((at[0] ^ other) * TILE, TILE), TILE)
+            lanes = pl.ds(pl.multiple_of(source * TILE, TILE), TILE)
+            raw[rows, lanes] = ref[n, 0]
     right_rows(right, raw[...])
     change = times_transposed(z[...], right[...])
     for t in range(LROWS):
@@ -317,7 +327,7 @@
             out[0, 0] = own[0]
 
 
-def update(at, column, front, pieces, inverses):
+def update(at, columns, front, pieces, corner, inverses):
     height = LROWS * TILE
     vmem = pl.BlockSpec(memory_space=pltpu.VMEM)
     block = pl.BlockSpec((LROWS, 2, TILE, TILE), lambda j: (0, j, 0, 0))
@@ -327,11 +337,14 @@
         out_shape=jax.ShapeDtypeStruct((LROWS, LCOLS, TILE, TILE), f32),
         in_specs=[
             pl.BlockSpec(memory_space=pltpu.SMEM),
-            pl.BlockSpec((16, 1, TILE, TILE), lambda j: (0, j, 0, 0)),
-            pl.BlockSpec((PT, PT, TILE, TILE), lambda j: (1, 2, 0, 0)),
+            *(
+                pl.BlockSpec((x.shape[0], 1, TILE, TILE), lambda j: (0, j, 0, 0))
+                for x in columns
+            ),
+            *[vmem] * 7,
             block,
-        ]
-        + [vmem] * 6,
+            vmem,
+        ],
         out_specs=block,
         scratch_shapes=[
             pltpu.VMEM((height, 2 * KP), bf16),
@@ -350,34 +363,51 @@
             flops=24_000_000_000, bytes_accessed=30 * MIB, transcendentals=0
         ),
         name="update",
-    )(at, column, column, front, *pieces, inverses)
+    )(at, *columns, *pieces, *corner, front, inverses)
 
 
 def move(x, axis, size, to):
     return lax.ppermute(x, axis, [(i, to(i)) for i in range(size)])
 
 
-def gather_row(x):
-    up, down = lambda c: (c + 2) % 8, lambda c: (c - 2) % 8
-    own = jnp.concatenate([x, move(x, "col", 8, lambda c: c ^ 1)], axis=0)
-    from_up, from_down = move(own, "col", 8, up), move(own, "col", 8, down)
-    far = move(from_up[:LROWS], "col", 8, up)
-    far2 = move(from_down[LROWS:], "col", 8, down)
-    return [own, from_up, from_down, far, far2]
-
-
-def gather_column(x):
-    moves = []
+def ring_gather(own, axis):
+    half = own.shape[0] // 2
+    up, down = lambda i: (i + 2) % 8, lambda i: (i - 2) % 8
+    before, behind = move(own, axis, 8, up), move(own, axis, 8, down)
+    return [own, before, behind, move(before[:half], axis, 8, up), move(behind[half:], axis, 8, down)]
+
+
+def gather_corner(top):
+    sib, row = lax.axis_index("sib"), lax.axis_index("row")
+    flip = [(4, 2), (5, 3), (6, 0), (7, 1)]
+    a = lax.ppermute(top, "sib", [(0, 1)])
+    b = lax.ppermute(top, "row", flip)
+    c = lax.ppermute(top, ("sib", "row"), [(i, 8 + j) for i, j in flip])
+    mine = jnp.where(row >= 4, jnp.where(sib == 0, top, a), jnp.where(sib == 0, b, c))
+    both = jnp.concatenate([mine, move(mine, "row", 8, lambda i: i ^ 2)], axis=0)
+    return [both, move(both, "row", 8, lambda i: i ^ 1)]
+
+
+def gather(panel):
+    there = []
     for y in range(4):
         for core in range(2):
             for z in range(4):
                 for xh in range(2):
                     to = ((y + z) % 4 * 2 + xh) * 8 + y * 2 + core
-                    moves.append(((y * 2 + core) * 8 + z * 2 + xh, to))
-    there = lax.ppermute(x, ("row", "col"), moves)
-    top = jnp.broadcast_to(x[:1], (8, TILE, TILE))
+                    there.append(((y * 2 + core) * 8 + z * 2 + xh, to))
+    across = lax.ppermute(panel, ("row", "col"), there)
+    pair = jnp.concatenate([panel, move(panel, "col", 8, lambda i: i ^ 1)], axis=0)
+    top = jnp.broadcast_to(panel[:1], (8, TILE, TILE))
     top = lax.all_to_all(top, "col", split_axis=0, concat_axis=0, tiled=True)[:PT]
-    return lax.all_gather(jnp.concatenate([there, top], axis=0), ("sib", "row"))
+    pair, top, across = lax.optimization_barrier((pair, top, across))
+    pieces = ring_gather(pair, "col")
+    corner = gather_corner(top)
+    pair = jnp.concatenate([across, move(across, "sib", 2, lambda i: 1 - i)], axis=0)
+    columns = ring_gather(pair, "row")
+    columns = columns + [move(x, "row", 8, lambda i: i ^ 1) for x in columns]
+    columns = [x.reshape(-1, LROWS, TILE, TILE) for x in columns]
+    return columns, pieces, corner
 
 
 def local(child_tiles, child_rows, child_slots, tile_count, inverses):
@@ -415,14 +445,13 @@
         outgoing, ("sib", "row", "col"), split_axis=0, concat_axis=0, tiled=True
     )
     panel, landing = add_up(True, arrived)
-    column = gather_column(panel)
-    pieces = gather_row(panel)
+    columns, pieces, corner = gather(panel)
     row = lax.axis_index("row")
     col = lax.axis_index("col")
     at = jnp.stack([lax.axis_index("sib"), row // 2, row % 2, col // 2, col % 2])
     at = at.astype(i32)
     front = add_up(False, arrived, landing)
-    out = update(at, column, front, pieces, inverses)
+    out = update(at, columns, front, pieces, corner, inverses)
     return out.reshape(LROWS, 1, LCOLS, 1, TILE, TILE)
 
 

time: 383 us -> 372 us (0.971)
  starting transfers between devices: 9.49 us -> 57.3 us
  blocking collectives: 227 us -> 204 us
  waiting for transfers between devices: 57.4 us -> 36.6 us
  between operations: 14.2 us -> 0.97 us
  Pallas kernels: 58.3 us -> 51.4 us
    ppermute x5 -> x17, starting transfers between devices: 6.27 us -> 43.5 us  [move(): return lax.ppermute(x, axis, [(i, to(i)) for i in range(size)])]
    all_gather x1 -> x0, waiting for transfers between devices: 22.5 us -> none  [gather_column(): return lax.all_gather(jnp.concatenate([there, top], axis=0), ('sib', 'row'))]
    all_to_all x1 -> x0, blocking collectives: 18.8 us -> none  [gather_column(): lax.all_to_all(top, 'col', split_axis=0, concat_axis=0, tiled=True)[:PT]]
    ppermute x5 -> x17, waiting for transfers between devices: 34.9 us -> 18.9 us  [move(): return lax.ppermute(x, axis, [(i, to(i)) for i in range(size)])]
    all_to_all x0 -> x1, waiting for transfers between devices: none -> 11.8 us  [gather(): lax.all_to_all(top, 'col', split_axis=0, concat_axis=0, tiled=True)[:PT]]
    pallas_call x1, Pallas kernels: 9.79 us -> 2.34 us  [pack(): pl.pallas_call(pack_kernel, out_shape=jax.ShapeDtypeStruct((devices, CAP...]
    ppermute x1 -> x4, starting transfers between devices: 3.22 us -> 9.24 us  [the longest x1 5.38 us: gather(): across = lax.ppermute(panel, ('row', 'col'), there)]
    ppermute x1 -> x4, waiting for transfers between devices: 0.01 us -> 5.89 us  [the longest x1 4.43 us: gather_corner(): b = lax.ppermute(top, 'row', flip)]
  transfers between devices with their start and end apart: 7 -> 22, of which waited for: 3 -> 8; matrix products, arithmetic and copies ran while one was open for 1% -> 2% of each run, Pallas kernels for 2% -> 2%
where the time goes in v5:
time: 372 us; the launch traced here: 369 us
  blocking collectives  204 us (55%)
  starting transfers between devices  57.3 us (15%)
  Pallas kernels  51.4 us (14%)
  waiting for transfers between devices  36.6 us (10%)
  local copies, waits for them, and re-layouts  14.8 us (4%)
  other arithmetic  4.13 us (1%)
    all_to_all x1, blocking collectives, local(): lax.all_to_all(outgoing, ('sib', 'row', 'col'), split_axis=0, concat_axis...  204 us
    ppermute x17, starting transfers between devices, move(): return lax.ppermute(x, axis, [(i, to(i)) for i in range(size)])  43.5 us
    pallas_call x1, Pallas kernels, update(): pl.pallas_call(update_kernel, grid=(LCOLS // 2,), out_shape=jax.ShapeDtyp...  33.2 us
    ppermute x17, waiting for transfers between devices, move(): return lax.ppermute(x, axis, [(i, to(i)) for i in range(size)])  18.9 us
    all_to_all x1, waiting for transfers between devices, gather(): lax.all_to_all(top, 'col', split_axis=0, concat_axis=0, tiled=True)[:PT]  11.8 us
    unnamed x23, local copies, waits for them, and re-layouts  8.49 us
    pallas_call x1, Pallas kernels, add_up(): pl.pallas_call(functools.partial(add_kernel, True), out_shape=[jax.ShapeD...  8.48 us
  transfers between devices with their start and end apart: 22, of which 8 were waited for; matrix products, arithmetic and copies ran while one was open for 2% of the time, Pallas kernels for 2%

profile of v5, /device:TPU:3, one launch (start us, length us, event | category | flops | bytes accessed | tf_op | source)
XLA Modules:
  0.0 369.4 jit_solution(1577386017682526193)
XLA Ops:
  0.7 0.7 and_select_fusion.5
  1.4 0.7 select_reduce_fusion.1
  2.1 0.2 convert_reduce_fusion
  2.3 0.1 select_reduce_fusion
  2.4 0.1 broadcast_in_dim.78
  2.6 0.2 select_convert_fusion
  2.8 3.4 copy-done
  6.2 2.3 pack.1
  8.6 204.2 %all_to_all.10.refs_0_.refs_1_ = f32[128,264,128]{2,1,0:T(8,128)} all-to-all(f32[128,264,128]{2,1,0:T(8,128)S(1)} %pack.1), channel_id=1, replica_groups=mesh['sib'=2,'row'=8,'col'=8] {'sib','row','col'}, dimensions={0} | all-to-all | bytes 34603008 | tf_op jit(solution)/shard_map/all_to_all | solution.py:444
  212.8 8.5 %add_panel.1 = (f32[8,128,128]{2,1,0:T(8,128)}, s32[8,128]{1,0:T(8,128)}) custom-call(f32[128,264,128]{2,1,0:T(8,128)} %all_to_all.10.refs_0_.refs_1_), custom_call_target="tpu_custom_call" | custom-call | tf_op jit(solution)/shard_map/add_panel/pallas_call | solution.py:115
  221.3 0.5 collective-permute-start
  221.8 0.9 slice_bitcast_fusion
  222.6 0.8 broadcast_in_dim.82
  223.5 4.6 %all-to-all-start.1 = ((f32[8,128,128]{2,1,0:T(8,128)}), f32[8,128,128]{2,1,0:T(8,128)S(1)}, u32[]{:S(2)}, u32[]{:S(2)}) async-start(f32[8,128,128]{2,1,0:T(8,128)} %broadcast_in_dim.82), calls=%async_computation.1 | async-start | bytes 1048576 | tf_op jit(solution)/shard_map/all_to_all | solution.py:402
  228.1 5.4 %collective-permute-start.1 = (f32[8,128,128]{2,1,0:T(8,128)}, f32[8,128,128]{2,1,0:T(8,128)S(1)}, u32[]{:S(2)}, u32[]{:S(2)}) collective-permute-start(f32[8,128,128]{2,1,0:T(8,128)} %get-tuple-element.10), channel_id=1, source_target_pairs={{0,0},{1,8},{2,16},{3,24},{4,32},{5,40},{6,48},{7,56},{8,1},{9,9},... | collective-permute-start | bytes 1572872 | tf_op jit(solution)/shard_map/ppermute | solution.py:399
  233.5 11.8 %all-to-all-done.1 = f32[8,128,128]{2,1,0:T(8,128)S(1)} async-done(((f32[8,128,128]{2,1,0:T(8,128)}), f32[8,128,128]{2,1,0:T(8,128)S(1)}, u32[]{:S(2)}, u32[]{:S(2)}) %all-to-all-start.1) | async-done | bytes 524320 | tf_op jit(solution)/shard_map/all_to_all | solution.py:402
  245.3 1.1 pad_maximum_fusion.refs_10_
  246.5 1.5 collective-permute-done.1
  247.9 1.3 collective-permute-start.18
  249.2 1.3 collective-permute-start.17
  250.5 1.3 collective-permute-start.16
  251.8 2.9 collective-permute-start.2
  254.7 6.3 %collective-permute-start.13 = (f32[16,128,128]{2,1,0:T(8,128)S(1)}, f32[16,128,128]{2,1,0:T(8,128)S(1)}, u32[]{:S(2)}, u32[]{:S(2)}) collective-permute-start(f32[16,128,128]{2,1,0:T(8,128)S(1)} %pad_maximum_fusion.refs_10_), channel_id=1, source_target_pairs={{0,6},{1,7},{2,0},{3,1},{4,2},{5,3},{6,4},{7,5},{8,14},{9,15},{10,... | collective-permute-start | bytes 3145736 | tf_op jit(solution)/shard_map/ppermute | solution.py:370
  261.0 4.4 %collective-permute-done.17 = f32[4,128,128]{2,1,0:T(8,128)S(1)} collective-permute-done((f32[4,128,128]{2,1,0:T(8,128)S(1)}, f32[4,128,128]{2,1,0:T(8,128)S(1)}, u32[]{:S(2)}, u32[]{:S(2)}) %collective-permute-start.17) | collective-permute-done | bytes 262176 | tf_op jit(solution)/shard_map/ppermute | solution.py:384
  265.5 1.0 select_select_fusion
  266.5 2.4 collective-permute-start.19
  268.9 3.0 collective-permute-done.2
  271.9 1.1 constant_dynamic-update-slice_fusion
  273.0 5.4 %collective-permute-start.4 = (f32[16,128,128]{2,1,0:T(8,128)S(1)}, f32[16,128,128]{2,1,0:T(8,128)}, u32[]{:S(2)}, u32[]{:S(2)}) collective-permute-start(f32[16,128,128]{2,1,0:T(8,128)S(1)} %constant_dynamic-update-slice_fusion), channel_id=1, source_target_pairs={{0,48},{8,56},{16,0},{24,8},{32,16},{40,24},{48,32},{56,40},{1,49}... | collective-permute-start | bytes 3145736 | tf_op jit(solution)/shard_map/ppermute | solution.py:370
  278.3 3.0 collective-permute-start.7
  281.4 0.4 collective-permute-done.13.refs_12_
  281.8 2.6 collective-permute-start.20
  284.4 15.0 %collective-permute-done.4 = f32[16,128,128]{2,1,0:T(8,128)} collective-permute-done((f32[16,128,128]{2,1,0:T(8,128)S(1)}, f32[16,128,128]{2,1,0:T(8,128)}, u32[]{:S(2)}, u32[]{:S(2)}) %collective-permute-start.4) | collective-permute-done | bytes 1048608 | tf_op jit(solution)/shard_map/ppermute | solution.py:370
  299.4 4.5 %collective-permute-start.15 = (f32[8,128,128]{2,1,0:T(8,128)S(1)}, f32[8,128,128]{2,1,0:T(8,128)S(1)}, u32[]{:S(2)}, u32[]{:S(2)}) collective-permute-start(f32[8,128,128]{2,1,0:T(8,128)S(1)} %slice.28), channel_id=1, source_target_pairs={{0,6},{1,7},{2,0},{3,1},{4,2},{5,3},{6,4},{7,5},{8,14},{9,15},{10,... | collective-permute-start | bytes 1572872 | tf_op jit(solution)/shard_map/ppermute | solution.py:370
  303.9 1.1 slice.26
  305.0 3.6 collective-permute-start.6
  308.5 1.1 slice.25
  309.7 3.6 collective-permute-start.9
  313.4 1.0 slice.27
  314.5 1.0 copy-done.2
  315.5 0.8 copy-done.9
  316.3 0.2 collective-permute-done.6
  316.5 4.2 %collective-permute-start.11 = (f32[8,128,128]{2,1,0:T(8,128)}, f32[8,128,128]{2,1,0:T(8,128)}, u32[]{:S(2)}, u32[]{:S(2)}) collective-permute-start(f32[8,128,128]{2,1,0:T(8,128)} %collective-permute-done.6), channel_id=1, source_target_pairs={{0,8},{8,0},{16,24},{24,16},{32,40},{40,32},{48,56},{56,48},{1,9},... | collective-permute-start | bytes 1572872 | tf_op jit(solution)/shard_map/ppermute | solution.py:370
  320.7 0.2 collective-permute-done.5
  320.9 4.4 %collective-permute-start.10 = (f32[8,128,128]{2,1,0:T(8,128)}, f32[8,128,128]{2,1,0:T(8,128)}, u32[]{:S(2)}, u32[]{:S(2)}) collective-permute-start(f32[8,128,128]{2,1,0:T(8,128)} %collective-permute-done.5), channel_id=1, source_target_pairs={{0,8},{8,0},{16,24},{24,16},{32,40},{40,32},{48,56},{56,48},{1,9},... | collective-permute-start | bytes 1572872 | tf_op jit(solution)/shard_map/ppermute | solution.py:370
  325.5 7.4 %add_all.1.refs_17_ = f32[8,16,128,128]{3,2,1,0:T(8,128)S(1)} custom-call(s32[8,128]{1,0:T(8,128)S(1)} %copy-done.6, f32[128,264,128]{2,1,0:T(8,128)} %all_to_all.10.refs_0_.refs_1_), custom_call_target="tpu_custom_call" | custom-call | flops 1000 | bytes 25165824 | tf_op jit(solution)/shard_map/add_all/pallas_call | solution.py:132
  332.9 3.3 copy-done.1
  336.2 33.2 %update.1 = f32[8,16,128,128]{3,2,1,0:T(8,128)} custom-call(s32[5]{0:T(128)S(1)} %stack.23.at, f32[2,8,128,128]{3,2,1,0:T(8,128)S(1)} %bitcast.43, f32[2,8,128,128]{3,2,1,0:T(8,128)} %bitcast.12.refs_1_, f32[2,8,128,128]{3,2,1,0:T(8,128)} %bitcast.13.refs_2_, f32[1,8,128,128]{3,2,1,0:T(8,128)} %bitcast.14.refs_3_, f32[1,8,128,128]{3,2,1,0:T(8,128)} %bitcast.15.refs_4_, ...), custom_call_target="tpu_custom_call" | custom-call | flops 24000000000 | bytes 31457280 | tf_op jit(solution)/shard_map/update/pallas_call | solution.py:334
  (47 shorter events, 0.5 us)
Async XLA Ops:
  2.8 3.4 copy-start
  221.2 104.2 %copy-start.6 = (s32[8,128]{1,0:T(8,128)S(1)}, s32[8,128]{1,0:T(8,128)}, u32[]{:S(2)}) copy-start(s32[8,128]{1,0:T(8,128)} %get-tuple-element.14.refs_0_) | copy-start | bytes 12292
  221.3 24.1 %collective-permute-start = (f32[8,128,128]{2,1,0:T(8,128)}, f32[8,128,128]{2,1,0:T(8,128)S(1)}, u32[]{:S(2)}, u32[]{:S(2)}) collective-permute-start(f32[8,128,128]{2,1,0:T(8,128)} %get-tuple-element.10), channel_id=1, source_target_pairs={{0,1},{1,0},{2,3},{3,2},{4,5},{5,4},{6,7},{7,6},{8,9},{9,8},{10,11... | collective-permute-start | bytes 1572872 | tf_op jit(solution)/shard_map/ppermute | solution.py:370
  223.5 21.8 %all-to-all-start.1 = ((f32[8,128,128]{2,1,0:T(8,128)}), f32[8,128,128]{2,1,0:T(8,128)S(1)}, u32[]{:S(2)}, u32[]{:S(2)}) async-start(f32[8,128,128]{2,1,0:T(8,128)} %broadcast_in_dim.82), calls=%async_computation.1 | async-start | bytes 1048576 | tf_op jit(solution)/shard_map/all_to_all | solution.py:402
  228.1 19.9 %collective-permute-start.1 = (f32[8,128,128]{2,1,0:T(8,128)}, f32[8,128,128]{2,1,0:T(8,128)S(1)}, u32[]{:S(2)}, u32[]{:S(2)}) collective-permute-start(f32[8,128,128]{2,1,0:T(8,128)} %get-tuple-element.10), channel_id=1, source_target_pairs={{0,0},{1,8},{2,16},{3,24},{4,32},{5,40},{6,48},{7,56},{8,1},{9,9},... | collective-permute-start | bytes 1572872 | tf_op jit(solution)/shard_map/ppermute | solution.py:399
  247.9 13.1 %collective-permute-start.18 = (f32[4,128,128]{2,1,0:T(8,128)S(1)}, f32[4,128,128]{2,1,0:T(8,128)S(1)}, u32[]{:S(2)}, u32[]{:S(2)}) collective-permute-start(f32[4,128,128]{2,1,0:T(8,128)S(1)} %slice.24), channel_id=1, source_target_pairs={{32,80},{40,88},{48,64},{56,72},{33,81},{41,89},{49,65},{57,73},{3... | collective-permute-start | bytes 786440 | tf_op jit(solution)/shard_map/ppermute | solution.py:385
  249.2 16.2 %collective-permute-start.17 = (f32[4,128,128]{2,1,0:T(8,128)S(1)}, f32[4,128,128]{2,1,0:T(8,128)S(1)}, u32[]{:S(2)}, u32[]{:S(2)}) collective-permute-start(f32[4,128,128]{2,1,0:T(8,128)S(1)} %slice.24), channel_id=1, source_target_pairs={{32,16},{40,24},{48,0},{56,8},{33,17},{41,25},{49,1},{57,9},{34,18... | collective-permute-start | bytes 786440 | tf_op jit(solution)/shard_map/ppermute | solution.py:384
  250.5 14.9 %collective-permute-start.16 = (f32[4,128,128]{2,1,0:T(8,128)S(1)}, f32[4,128,128]{2,1,0:T(8,128)}, u32[]{:S(2)}, u32[]{:S(2)}) collective-permute-start(f32[4,128,128]{2,1,0:T(8,128)S(1)} %slice.24), channel_id=1, source_target_pairs={{0,64},{1,65},{2,66},{3,67},{4,68},{5,69},{6,70},{7,71},{8,72},{9,... | collective-permute-start | bytes 786440 | tf_op jit(solution)/shard_map/ppermute | solution.py:383
  251.8 20.0 %collective-permute-start.2 = (f32[8,128,128]{2,1,0:T(8,128)S(1)}, f32[8,128,128]{2,1,0:T(8,128)}, u32[]{:S(2)}, u32[]{:S(2)}) collective-permute-start(f32[8,128,128]{2,1,0:T(8,128)S(1)} %collective-permute-done.1), channel_id=1, source_target_pairs={{0,64},{64,0},{1,65},{65,1},{2,66},{66,2},{3,67},{67,3},{4,68},{68... | collective-permute-start | bytes 1572872 | tf_op jit(solution)/shard_map/ppermute | solution.py:370
  254.7 27.1 %collective-permute-start.13 = (f32[16,128,128]{2,1,0:T(8,128)S(1)}, f32[16,128,128]{2,1,0:T(8,128)S(1)}, u32[]{:S(2)}, u32[]{:S(2)}) collective-permute-start(f32[16,128,128]{2,1,0:T(8,128)S(1)} %pad_maximum_fusion.refs_10_), channel_id=1, source_target_pairs={{0,6},{1,7},{2,0},{3,1},{4,2},{5,3},{6,4},{7,5},{8,14},{9,15},{10,... | collective-permute-start | bytes 3145736 | tf_op jit(solution)/shard_map/ppermute | solution.py:370
  266.5 11.8 %collective-permute-start.19 = (f32[4,128,128]{2,1,0:T(8,128)S(1)}, f32[4,128,128]{2,1,0:T(8,128)S(1)}, u32[]{:S(2)}, u32[]{:S(2)}) collective-permute-start(f32[4,128,128]{2,1,0:T(8,128)S(1)} %select_select_fusion), channel_id=1, source_target_pairs={{0,16},{8,24},{16,0},{24,8},{32,48},{40,56},{48,32},{56,40},{1,17}... | collective-permute-start | bytes 786440 | tf_op jit(solution)/shard_map/ppermute | solution.py:370
  272.9 41.5 %copy-start.4 = (f32[16,128,128]{2,1,0:T(8,128)}, f32[16,128,128]{2,1,0:T(8,128)S(1)}, u32[]{:S(2)}) copy-start(f32[16,128,128]{2,1,0:T(8,128)S(1)} %constant_dynamic-update-slice_fusion) | copy-start | bytes 3145732
  273.0 26.4 %collective-permute-start.4 = (f32[16,128,128]{2,1,0:T(8,128)S(1)}, f32[16,128,128]{2,1,0:T(8,128)}, u32[]{:S(2)}, u32[]{:S(2)}) collective-permute-start(f32[16,128,128]{2,1,0:T(8,128)S(1)} %constant_dynamic-update-slice_fusion), channel_id=1, source_target_pairs={{0,48},{8,56},{16,0},{24,8},{32,16},{40,24},{48,32},{56,40},{1,49}... | collective-permute-start | bytes 3145736 | tf_op jit(solution)/shard_map/ppermute | solution.py:370
  278.3 26.6 %collective-permute-start.3 = (f32[16,128,128]{2,1,0:T(8,128)S(1)}, f32[16,128,128]{2,1,0:T(8,128)}, u32[]{:S(2)}, u32[]{:S(2)}) collective-permute-start(f32[16,128,128]{2,1,0:T(8,128)S(1)} %constant_dynamic-update-slice_fusion), channel_id=1, source_target_pairs={{0,16},{8,24},{16,32},{24,40},{32,48},{40,56},{48,0},{56,8},{1,17}... | collective-permute-start | bytes 3145736 | tf_op jit(solution)/shard_map/ppermute | solution.py:370
  278.3 31.4 %collective-permute-start.12 = (f32[16,128,128]{2,1,0:T(8,128)S(1)}, f32[16,128,128]{2,1,0:T(8,128)S(1)}, u32[]{:S(2)}, u32[]{:S(2)}) collective-permute-start(f32[16,128,128]{2,1,0:T(8,128)S(1)} %pad_maximum_fusion.refs_10_), channel_id=1, source_target_pairs={{0,2},{1,3},{2,4},{3,5},{4,6},{5,7},{6,0},{7,1},{8,10},{9,11},{10,... | collective-permute-start | bytes 3145736 | tf_op jit(solution)/shard_map/ppermute | solution.py:370
  278.3 35.0 %collective-permute-start.7 = (f32[16,128,128]{2,1,0:T(8,128)S(1)}, f32[16,128,128]{2,1,0:T(8,128)S(1)}, u32[]{:S(2)}, u32[]{:S(2)}) collective-permute-start(f32[16,128,128]{2,1,0:T(8,128)S(1)} %constant_dynamic-update-slice_fusion), channel_id=1, source_target_pairs={{0,8},{8,0},{16,24},{24,16},{32,40},{40,32},{48,56},{56,48},{1,9},... | collective-permute-start | bytes 3145736 | tf_op jit(solution)/shard_map/ppermute | solution.py:370
  281.8 27.8 %collective-permute-start.20 = (f32[8,128,128]{2,1,0:T(8,128)S(1)}, f32[8,128,128]{2,1,0:T(8,128)S(1)}, u32[]{:S(2)}, u32[]{:S(2)}) collective-permute-start(f32[8,128,128]{2,1,0:T(8,128)S(1)} %pad_maximum_fusion.1.refs_15_), channel_id=1, source_target_pairs={{0,8},{8,0},{16,24},{24,16},{32,40},{40,32},{48,56},{56,48},{1,9},... | collective-permute-start | bytes 1572872 | tf_op jit(solution)/shard_map/ppermute | solution.py:370
  299.4 16.1 %collective-permute-start.15 = (f32[8,128,128]{2,1,0:T(8,128)S(1)}, f32[8,128,128]{2,1,0:T(8,128)S(1)}, u32[]{:S(2)}, u32[]{:S(2)}) collective-permute-start(f32[8,128,128]{2,1,0:T(8,128)S(1)} %slice.28), channel_id=1, source_target_pairs={{0,6},{1,7},{2,0},{3,1},{4,2},{5,3},{6,4},{7,5},{8,14},{9,15},{10,... | collective-permute-start | bytes 1572872 | tf_op jit(solution)/shard_map/ppermute | solution.py:370
  305.0 11.6 %collective-permute-start.6 = (f32[8,128,128]{2,1,0:T(8,128)S(1)}, f32[8,128,128]{2,1,0:T(8,128)}, u32[]{:S(2)}, u32[]{:S(2)}) collective-permute-start(f32[8,128,128]{2,1,0:T(8,128)S(1)} %slice.26), channel_id=1, source_target_pairs={{0,48},{8,56},{16,0},{24,8},{32,16},{40,24},{48,32},{56,40},{1,49}... | collective-permute-start | bytes 1572872 | tf_op jit(solution)/shard_map/ppermute | solution.py:370
  309.6 11.3 %collective-permute-start.5 = (f32[8,128,128]{2,1,0:T(8,128)S(1)}, f32[8,128,128]{2,1,0:T(8,128)}, u32[]{:S(2)}, u32[]{:S(2)}) collective-permute-start(f32[8,128,128]{2,1,0:T(8,128)S(1)} %slice.25), channel_id=1, source_target_pairs={{0,16},{8,24},{16,32},{24,40},{32,48},{40,56},{48,0},{56,8},{1,17}... | collective-permute-start | bytes 1572872 | tf_op jit(solution)/shard_map/ppermute | solution.py:370
  309.7 26.5 %collective-permute-start.9 = (f32[16,128,128]{2,1,0:T(8,128)}, f32[16,128,128]{2,1,0:T(8,128)}, u32[]{:S(2)}, u32[]{:S(2)}) collective-permute-start(f32[16,128,128]{2,1,0:T(8,128)} %collective-permute-done.4), channel_id=1, source_target_pairs={{0,8},{8,0},{16,24},{24,16},{32,40},{40,32},{48,56},{56,48},{1,9},... | collective-permute-start | bytes 3145736 | tf_op jit(solution)/shard_map/ppermute | solution.py:370
  313.3 2.1 copy-start.7
  313.3 22.9 %collective-permute-start.8 = (f32[16,128,128]{2,1,0:T(8,128)}, f32[16,128,128]{2,1,0:T(8,128)}, u32[]{:S(2)}, u32[]{:S(2)}) collective-permute-start(f32[16,128,128]{2,1,0:T(8,128)} %collective-permute-done.3), channel_id=1, source_target_pairs={{0,8},{8,0},{16,24},{24,16},{32,40},{40,32},{48,56},{56,48},{1,9},... | collective-permute-start | bytes 3145736 | tf_op jit(solution)/shard_map/ppermute | solution.py:370
  314.5 1.0 copy-start.2
  315.5 0.8 copy-start.9
  316.3 19.9 %collective-permute-start.14 = (f32[8,128,128]{2,1,0:T(8,128)}, f32[8,128,128]{2,1,0:T(8,128)}, u32[]{:S(2)}, u32[]{:S(2)}) collective-permute-start(f32[8,128,128]{2,1,0:T(8,128)} %slice.27), channel_id=1, source_target_pairs={{0,2},{1,3},{2,4},{3,5},{4,6},{5,7},{6,0},{7,1},{8,10},{9,11},{10,... | collective-permute-start | bytes 1572872 | tf_op jit(solution)/shard_map/ppermute | solution.py:370
  316.5 19.7 %collective-permute-start.11 = (f32[8,128,128]{2,1,0:T(8,128)}, f32[8,128,128]{2,1,0:T(8,128)}, u32[]{:S(2)}, u32[]{:S(2)}) collective-permute-start(f32[8,128,128]{2,1,0:T(8,128)} %collective-permute-done.6), channel_id=1, source_target_pairs={{0,8},{8,0},{16,24},{24,16},{32,40},{40,32},{48,56},{56,48},{1,9},... | collective-permute-start | bytes 1572872 | tf_op jit(solution)/shard_map/ppermute | solution.py:370
  320.9 15.3 %collective-permute-start.10 = (f32[8,128,128]{2,1,0:T(8,128)}, f32[8,128,128]{2,1,0:T(8,128)}, u32[]{:S(2)}, u32[]{:S(2)}) collective-permute-start(f32[8,128,128]{2,1,0:T(8,128)} %collective-permute-done.5), channel_id=1, source_target_pairs={{0,8},{8,0},{16,24},{24,16},{32,40},{40,32},{48,56},{56,48},{1,9},... | collective-permute-start | bytes 1572872 | tf_op jit(solution)/shard_map/ppermute | solution.py:370
  325.4 10.8 %copy-start.3 = (f32[16,128,128]{2,1,0:T(8,128)S(1)}, f32[16,128,128]{2,1,0:T(8,128)}, u32[]{:S(2)}) copy-start(f32[16,128,128]{2,1,0:T(8,128)} %copy-done.2) | copy-start | bytes 3145732
  325.4 10.8 %copy-start.5 = (f32[16,128,128]{2,1,0:T(8,128)S(1)}, f32[16,128,128]{2,1,0:T(8,128)}, u32[]{:S(2)}) copy-start(f32[16,128,128]{2,1,0:T(8,128)} %copy-done.4) | copy-start | bytes 3145732
  325.4 10.8 %copy-start.8 = (f32[16,128,128]{2,1,0:T(8,128)S(1)}, f32[16,128,128]{2,1,0:T(8,128)}, u32[]{:S(2)}) copy-start(f32[16,128,128]{2,1,0:T(8,128)} %copy-done.7) | copy-start | bytes 3145732
  325.5 10.8 %copy-start.10 = (f32[8,128,128]{2,1,0:T(8,128)S(1)}, f32[8,128,128]{2,1,0:T(8,128)}, u32[]{:S(2)}) copy-start(f32[8,128,128]{2,1,0:T(8,128)} %copy-done.9) | copy-start | bytes 1572868
  332.9 3.3 copy-start.1

commit v6 on v5

--- a/solution.py
+++ b/solution.py
@@ -83,7 +83,7 @@
 
         return n + hit.astype(i32)
 
-    count = lax.fori_loop(0, slots, scan, 0)
+    count = lax.fori_loop(0, slots, scan, 0, unroll=8)
     if not panel:
         out[...] = jnp.zeros_like(out)
     lax.fori_loop(0, count, lambda n, c: (fetch(0, n).wait(), c)[1], 0)
@@ -284,7 +284,8 @@
 ):
     columns, pieces, corner = refs[:10], refs[10:15], refs[15:17]
     front, inverses, out = refs[17:20]
-    z, right, raw, own, f0, f1, left, r_rows, r_cols, low = refs[20:]
+    z, right, raw, own, f0, f1, r_rows, r_cols, low = refs[20:]
+    left = z.at[:, :KP]
     step = pl.program_id(0)
 
     @pl.when(step == 0)
@@ -309,7 +310,7 @@
             source = (at[1] + dy - at[3] + 8) % 4 * 2 + core
             rows = pl.ds(pl.multiple_of((at[0] ^ other) * TILE, TILE), TILE)
             lanes = pl.ds(pl.multiple_of(source * TILE, TILE), TILE)
-            raw[rows, lanes] = ref[n, 0]
+            raw[rows, lanes] = ref[n * LROWS + step]
     right_rows(right, raw[...])
     change = times_transposed(z[...], right[...])
     for t in range(LROWS):
@@ -337,11 +338,7 @@
         out_shape=jax.ShapeDtypeStruct((LROWS, LCOLS, TILE, TILE), f32),
         in_specs=[
             pl.BlockSpec(memory_space=pltpu.SMEM),
-            *(
-                pl.BlockSpec((x.shape[0], 1, TILE, TILE), lambda j: (0, j, 0, 0))
-                for x in columns
-            ),
-            *[vmem] * 7,
+            *[vmem] * 17,
             block,
             vmem,
         ],
@@ -353,12 +350,11 @@
             pltpu.VMEM((LROWS, TILE, TILE), f32),
             pltpu.VMEM((height, PANEL), f32),
             pltpu.VMEM((height, PANEL), f32),
-            pltpu.VMEM((height, KP), bf16),
             pltpu.VMEM((PANEL, KP), bf16),
             pltpu.VMEM((KP, PANEL), bf16),
             pltpu.VMEM((PANEL, PANEL), f32),
         ],
-        compiler_params=pltpu.CompilerParams(vmem_limit_bytes=40 * MIB),
+        compiler_params=pltpu.CompilerParams(vmem_limit_bytes=32 * MIB),
         cost_estimate=pl.CostEstimate(
             flops=24_000_000_000, bytes_accessed=30 * MIB, transcendentals=0
         ),
@@ -370,11 +366,15 @@
     return lax.ppermute(x, axis, [(i, to(i)) for i in range(size)])
 
 
-def ring_gather(own, axis):
-    half = own.shape[0] // 2
+def both_ways(own, axis):
     up, down = lambda i: (i + 2) % 8, lambda i: (i - 2) % 8
-    before, behind = move(own, axis, 8, up), move(own, axis, 8, down)
-    return [own, before, behind, move(before[:half], axis, 8, up), move(behind[half:], axis, 8, down)]
+    return [move(own, axis, 8, up), move(own, axis, 8, down)]
+
+
+def opposite(before, behind, axis):
+    half = before.shape[0] // 2
+    up, down = lambda i: (i + 2) % 8, lambda i: (i - 2) % 8
+    return [move(before[:half], axis, 8, up), move(behind[half:], axis, 8, down)]
 
 
 def gather_corner(top):
@@ -388,7 +388,7 @@
     return [both, move(both, "row", 8, lambda i: i ^ 1)]
 
 
-def gather(panel):
+def gather(panel, arrived, landing):
     there = []
     for y in range(4):
         for core in range(2):
@@ -401,13 +401,17 @@
     top = jnp.broadcast_to(panel[:1], (8, TILE, TILE))
     top = lax.all_to_all(top, "col", split_axis=0, concat_axis=0, tiled=True)[:PT]
     pair, top, across = lax.optimization_barrier((pair, top, across))
-    pieces = ring_gather(pair, "col")
+    other = move(across, "sib", 2, lambda i: 1 - i)
+    pieces = [pair, *both_ways(pair, "col")]
+    across, other, top = lax.optimization_barrier((across, other, top))
+    columns = [jnp.concatenate([across, other], axis=0)]
+    columns += both_ways(columns[0], "row")
     corner = gather_corner(top)
-    pair = jnp.concatenate([across, move(across, "sib", 2, lambda i: 1 - i)], axis=0)
-    columns = ring_gather(pair, "row")
-    columns = columns + [move(x, "row", 8, lambda i: i ^ 1) for x in columns]
-    columns = [x.reshape(-1, LROWS, TILE, TILE) for x in columns]
-    return columns, pieces, corner
+    *columns, front = lax.optimization_barrier((*columns, add_up(False, arrived, landing)))
+    columns += opposite(*columns[1:], "row")
+    pieces += opposite(*pieces[1:], "col")
+    columns += [move(x, "row", 8, lambda i: i ^ 1) for x in columns]
+    return columns, pieces, corner, front
 
 
 def local(child_tiles, child_rows, child_slots, tile_count, inverses):
@@ -445,12 +449,11 @@
         outgoing, ("sib", "row", "col"), split_axis=0, concat_axis=0, tiled=True
     )
     panel, landing = add_up(True, arrived)
-    columns, pieces, corner = gather(panel)
+    columns, pieces, corner, front = gather(panel, arrived, landing)
     row = lax.axis_index("row")
     col = lax.axis_index("col")
     at = jnp.stack([lax.axis_index("sib"), row // 2, row % 2, col // 2, col % 2])
     at = at.astype(i32)
-    front = add_up(False, arrived, landing)
     out = update(at, columns, front, pieces, corner, inverses)
     return out.reshape(LROWS, 1, LCOLS, 1, TILE, TILE)
 

time: 372 us -> 383 us (1.030)
  waiting for transfers between devices: 36.6 us -> 69.7 us
  starting transfers between devices: 57.3 us -> 34.1 us
  local copies, waits for them, and re-layouts: 14.8 us -> 19.9 us
    ppermute x17, waiting for transfers between devices: 18.9 us -> 46.6 us  [move(): return lax.ppermute(x, axis, [(i, to(i)) for i in range(size)])]
    ppermute x17, starting transfers between devices: 43.5 us -> 19.5 us  [move(): return lax.ppermute(x, axis, [(i, to(i)) for i in range(size)])]
    unnamed x23 -> x19, local copies, waits for them, and re-layouts: 8.49 us -> 12.7 us
  transfers between devices with their start and end apart: 22 -> 22, of which waited for: 8 -> 9; matrix products, arithmetic and copies ran while one was open for 2% -> 3% of each run, Pallas kernels for 2% -> 2%
where the time goes in v6:
time: 383 us; the launch traced here: 382 us
  blocking collectives  204 us (53%)
  waiting for transfers between devices  69.7 us (18%)
  Pallas kernels  49.5 us (13%)
  starting transfers between devices  34.1 us (9%)
  local copies, waits for them, and re-layouts  19.9 us (5%)
  other arithmetic  4.13 us (1%)
    all_to_all x1, blocking collectives, local(): lax.all_to_all(outgoing, ('sib', 'row', 'col'), split_axis=0, concat_axis...  204 us
    ppermute x17, waiting for transfers between devices, move(): return lax.ppermute(x, axis, [(i, to(i)) for i in range(size)])  46.6 us
    pallas_call x1, Pallas kernels, update(): pl.pallas_call(update_kernel, grid=(LCOLS // 2,), out_shape=jax.ShapeDtyp...  34.3 us
    ppermute x17, starting transfers between devices, move(): return lax.ppermute(x, axis, [(i, to(i)) for i in range(size)])  19.5 us
    unnamed x19, local copies, waits for them, and re-layouts  12.7 us
    all_to_all x1, waiting for transfers between devices, gather(): lax.all_to_all(top, 'col', split_axis=0, concat_axis=0, tiled=True)[:PT]  9.86 us
    ppermute x1, waiting for transfers between devices, gather_corner(): b = lax.ppermute(top, 'row', flip)  8.02 us
  transfers between devices with their start and end apart: 22, of which 9 were waited for; matrix products, arithmetic and copies ran while one was open for 3% of the time, Pallas kernels for 2%

profile of v6, /device:TPU:3, one launch (start us, length us, event | category | flops | bytes accessed | tf_op | source)
XLA Modules:
  0.0 382.1 jit_solution(11341451612090848412)
XLA Ops:
  0.7 0.7 and_select_fusion.5
  1.4 0.7 select_reduce_fusion.1
  2.8 3.4 copy-done
  6.2 2.6 pack.1
  8.8 203.8 %all_to_all.10.refs_0_.refs_1_ = f32[128,264,128]{2,1,0:T(8,128)} all-to-all(f32[128,264,128]{2,1,0:T(8,128)S(1)} %pack.1), channel_id=1, replica_groups=mesh['sib'=2,'row'=8,'col'=8] {'sib','row','col'}, dimensions={0} | all-to-all | bytes 34603008 | tf_op jit(solution)/shard_map/all_to_all | solution.py:448
  212.6 6.5 %add_panel.1 = (f32[8,128,128]{2,1,0:T(8,128)}, s32[8,128]{1,0:T(8,128)}) custom-call(f32[128,264,128]{2,1,0:T(8,128)} %all_to_all.10.refs_0_.refs_1_), custom_call_target="tpu_custom_call" | custom-call | tf_op jit(solution)/shard_map/add_panel/pallas_call | solution.py:115
  219.1 0.6 collective-permute-start
  219.7 0.9 slice_bitcast_fusion
  220.6 0.8 broadcast_in_dim.82
  221.5 5.3 %all-to-all-start.1 = ((f32[8,128,128]{2,1,0:T(8,128)}), f32[8,128,128]{2,1,0:T(8,128)S(1)}, u32[]{:S(2)}, u32[]{:S(2)}) async-start(f32[8,128,128]{2,1,0:T(8,128)} %broadcast_in_dim.82), calls=%async_computation.1 | async-start | bytes 1048576 | tf_op jit(solution)/shard_map/all_to_all | solution.py:402
  226.8 5.4 %collective-permute-start.1 = (f32[8,128,128]{2,1,0:T(8,128)}, f32[8,128,128]{2,1,0:T(8,128)S(1)}, u32[]{:S(2)}, u32[]{:S(2)}) collective-permute-start(f32[8,128,128]{2,1,0:T(8,128)} %get-tuple-element.17), channel_id=1, source_target_pairs={{0,0},{1,8},{2,16},{3,24},{4,32},{5,40},{6,48},{7,56},{8,1},{9,9},... | collective-permute-start | bytes 1572872 | tf_op jit(solution)/shard_map/ppermute | solution.py:399
  232.2 9.9 %all-to-all-done.1 = f32[8,128,128]{2,1,0:T(8,128)S(1)} async-done(((f32[8,128,128]{2,1,0:T(8,128)}), f32[8,128,128]{2,1,0:T(8,128)S(1)}, u32[]{:S(2)}, u32[]{:S(2)}) %all-to-all-start.1) | async-done | bytes 524320 | tf_op jit(solution)/shard_map/all_to_all | solution.py:402
  242.1 1.1 pad_maximum_fusion.refs_10_
  243.2 2.6 collective-permute-done.1
  245.8 4.9 %collective-permute-start.2 = (f32[8,128,128]{2,1,0:T(8,128)S(1)}, f32[8,128,128]{2,1,0:T(8,128)S(1)}, u32[]{:S(2)}, u32[]{:S(2)}) collective-permute-start(f32[8,128,128]{2,1,0:T(8,128)S(1)} %collective-permute-done.1), channel_id=1, source_target_pairs={{0,64},{64,0},{1,65},{65,1},{2,66},{66,2},{3,67},{67,3},{4,68},{68... | collective-permute-start | bytes 1572872 | tf_op jit(solution)/shard_map/ppermute | solution.py:366
  250.7 2.6 collective-permute-start.13
  253.3 7.0 %collective-permute-done.2 = f32[8,128,128]{2,1,0:T(8,128)S(1)} collective-permute-done((f32[8,128,128]{2,1,0:T(8,128)S(1)}, f32[8,128,128]{2,1,0:T(8,128)S(1)}, u32[]{:S(2)}, u32[]{:S(2)}) %collective-permute-start.2) | collective-permute-done | bytes 524320 | tf_op jit(solution)/shard_map/ppermute | solution.py:366
  260.3 1.3 collective-permute-start.18
  261.6 1.3 collective-permute-start.17
  262.9 1.3 collective-permute-start.16
  264.2 0.8 constant_dynamic-update-slice_fusion.1
  265.0 1.9 constant_dynamic-update-slice_fusion.refs_0_
  266.9 2.7 collective-permute-done.18
  269.6 0.6 collective-permute-start.4
  270.2 8.0 %collective-permute-done.17 = f32[4,128,128]{2,1,0:T(8,128)S(1)} collective-permute-done((f32[4,128,128]{2,1,0:T(8,128)S(1)}, f32[4,128,128]{2,1,0:T(8,128)S(1)}, u32[]{:S(2)}, u32[]{:S(2)}) %collective-permute-start.17) | collective-permute-done | bytes 262176 | tf_op jit(solution)/shard_map/ppermute | solution.py:384
  278.2 2.1 collective-permute-start.3
  280.3 1.0 select_select_fusion
  281.4 26.8 %collective-permute-done.19 = f32[4,128,128]{2,1,0:T(8,128)S(1)} collective-permute-done((f32[4,128,128]{2,1,0:T(8,128)S(1)}, f32[4,128,128]{2,1,0:T(8,128)S(1)}, u32[]{:S(2)}, u32[]{:S(2)}) %collective-permute-start.19) | collective-permute-done | bytes 262176 | tf_op jit(solution)/shard_map/ppermute | solution.py:366
  308.2 1.4 collective-permute-start.20
  309.7 1.9 collective-permute-start.15
  311.6 1.1 slice.25
  312.8 6.2 %add_all.1.refs_17_ = f32[8,16,128,128]{3,2,1,0:T(8,128)S(1)} custom-call(s32[8,128]{1,0:T(8,128)S(1)} %copy-done.2, f32[128,264,128]{2,1,0:T(8,128)} %all_to_all.10.refs_0_.refs_1_), custom_call_target="tpu_custom_call" | custom-call | flops 1000 | bytes 25165824 | tf_op jit(solution)/shard_map/add_all/pallas_call | solution.py:132
  319.0 3.2 copy-done.1
  322.2 1.1 slice.20
  323.9 1.1 slice.21
  324.9 1.7 collective-permute-start.6
  326.6 0.6 collective-permute-start.5
  327.3 0.8 copy-done.4
  328.6 0.8 copy-done.6
  329.4 10.0 %collective-permute-done.6.refs_4_ = f32[8,128,128]{2,1,0:T(8,128)} collective-permute-done((f32[8,128,128]{2,1,0:T(8,128)S(1)}, f32[8,128,128]{2,1,0:T(8,128)}, u32[]{:S(2)}, u32[]{:S(2)}) %collective-permute-start.6) | collective-permute-done | bytes 524320 | tf_op jit(solution)/shard_map/ppermute | solution.py:366
  339.4 0.7 collective-permute-start.11
  340.2 1.0 collective-permute-done.5.refs_3_
  341.2 1.1 collective-permute-start.10
  342.4 1.8 collective-permute-done.10.refs_8_
  344.2 1.6 copy-done.3
  345.8 1.0 copy-done.5
  346.8 1.0 copy-done.7
  347.8 34.3 %update.1 = f32[8,16,128,128]{3,2,1,0:T(8,128)} custom-call(s32[5]{0:T(128)S(1)} %stack.23.at, f32[16,128,128]{2,1,0:T(8,128)} %constant_dynamic-update-slice_fusion.refs_0_, f32[16,128,128]{2,1,0:T(8,128)} %collective-permute-done.3.refs_1_, f32[16,128,128]{2,1,0:T(8,128)} %collective-permute-done.4.refs_2_, f32[8,128,128]{2,1,0:T(8,128)} %collective-permute-done.5.refs_3_, ...), custom_call_target="tpu_custom_call" | custom-call | flops 24000000000 | bytes 31457280 | tf_op jit(solution)/shard_map/update/pallas_call | solution.py:335
  (43 shorter events, 2.2 us)
Async XLA Ops:
  2.8 3.4 copy-start
  219.1 93.6 %copy-start.2 = (s32[8,128]{1,0:T(8,128)S(1)}, s32[8,128]{1,0:T(8,128)}, u32[]{:S(2)}) copy-start(s32[8,128]{1,0:T(8,128)} %get-tuple-element.22.refs_0_) | copy-start | bytes 12292
  219.1 22.9 %collective-permute-start = (f32[8,128,128]{2,1,0:T(8,128)}, f32[8,128,128]{2,1,0:T(8,128)S(1)}, u32[]{:S(2)}, u32[]{:S(2)}) collective-permute-start(f32[8,128,128]{2,1,0:T(8,128)} %get-tuple-element.17), channel_id=1, source_target_pairs={{0,1},{1,0},{2,3},{3,2},{4,5},{5,4},{6,7},{7,6},{8,9},{9,8},{10,11... | collective-permute-start | bytes 1572872 | tf_op jit(solution)/shard_map/ppermute | solution.py:366
  221.5 20.6 %all-to-all-start.1 = ((f32[8,128,128]{2,1,0:T(8,128)}), f32[8,128,128]{2,1,0:T(8,128)S(1)}, u32[]{:S(2)}, u32[]{:S(2)}) async-start(f32[8,128,128]{2,1,0:T(8,128)} %broadcast_in_dim.82), calls=%async_computation.1 | async-start | bytes 1048576 | tf_op jit(solution)/shard_map/all_to_all | solution.py:402
  226.8 19.1 %collective-permute-start.1 = (f32[8,128,128]{2,1,0:T(8,128)}, f32[8,128,128]{2,1,0:T(8,128)S(1)}, u32[]{:S(2)}, u32[]{:S(2)}) collective-permute-start(f32[8,128,128]{2,1,0:T(8,128)} %get-tuple-element.17), channel_id=1, source_target_pairs={{0,0},{1,8},{2,16},{3,24},{4,32},{5,40},{6,48},{7,56},{8,1},{9,9},... | collective-permute-start | bytes 1572872 | tf_op jit(solution)/shard_map/ppermute | solution.py:399
  245.8 14.5 %collective-permute-start.2 = (f32[8,128,128]{2,1,0:T(8,128)S(1)}, f32[8,128,128]{2,1,0:T(8,128)S(1)}, u32[]{:S(2)}, u32[]{:S(2)}) collective-permute-start(f32[8,128,128]{2,1,0:T(8,128)S(1)} %collective-permute-done.1), channel_id=1, source_target_pairs={{0,64},{64,0},{1,65},{65,1},{2,66},{66,2},{3,67},{67,3},{4,68},{68... | collective-permute-start | bytes 1572872 | tf_op jit(solution)/shard_map/ppermute | solution.py:366
  250.7 58.9 %collective-permute-start.13 = (f32[16,128,128]{2,1,0:T(8,128)S(1)}, f32[16,128,128]{2,1,0:T(8,128)S(1)}, u32[]{:S(2)}, u32[]{:S(2)}) collective-permute-start(f32[16,128,128]{2,1,0:T(8,128)S(1)} %pad_maximum_fusion.refs_10_), channel_id=1, source_target_pairs={{0,6},{1,7},{2,0},{3,1},{4,2},{5,3},{6,4},{7,5},{8,14},{9,15},{10,... | collective-permute-start | bytes 3145736 | tf_op jit(solution)/shard_map/ppermute | solution.py:366
  253.3 58.3 %collective-permute-start.12 = (f32[16,128,128]{2,1,0:T(8,128)S(1)}, f32[16,128,128]{2,1,0:T(8,128)}, u32[]{:S(2)}, u32[]{:S(2)}) collective-permute-start(f32[16,128,128]{2,1,0:T(8,128)S(1)} %pad_maximum_fusion.refs_10_), channel_id=1, source_target_pairs={{0,2},{1,3},{2,4},{3,5},{4,6},{5,7},{6,0},{7,1},{8,10},{9,11},{10,... | collective-permute-start | bytes 3145736 | tf_op jit(solution)/shard_map/ppermute | solution.py:366
  260.3 1.3 copy-start.8
  260.3 9.3 %collective-permute-start.18 = (f32[4,128,128]{2,1,0:T(8,128)S(1)}, f32[4,128,128]{2,1,0:T(8,128)S(1)}, u32[]{:S(2)}, u32[]{:S(2)}) collective-permute-start(f32[4,128,128]{2,1,0:T(8,128)S(1)} %slice.24), channel_id=1, source_target_pairs={{32,80},{40,88},{48,64},{56,72},{33,81},{41,89},{49,65},{57,73},{3... | collective-permute-start | bytes 786440 | tf_op jit(solution)/shard_map/ppermute | solution.py:385
  261.6 16.6 %collective-permute-start.17 = (f32[4,128,128]{2,1,0:T(8,128)S(1)}, f32[4,128,128]{2,1,0:T(8,128)S(1)}, u32[]{:S(2)}, u32[]{:S(2)}) collective-permute-start(f32[4,128,128]{2,1,0:T(8,128)S(1)} %slice.24), channel_id=1, source_target_pairs={{32,16},{40,24},{48,0},{56,8},{33,17},{41,25},{49,1},{57,9},{34,18... | collective-permute-start | bytes 786440 | tf_op jit(solution)/shard_map/ppermute | solution.py:384
  262.9 17.4 %collective-permute-start.16 = (f32[4,128,128]{2,1,0:T(8,128)S(1)}, f32[4,128,128]{2,1,0:T(8,128)}, u32[]{:S(2)}, u32[]{:S(2)}) collective-permute-start(f32[4,128,128]{2,1,0:T(8,128)S(1)} %slice.24), channel_id=1, source_target_pairs={{0,64},{1,65},{2,66},{3,67},{4,68},{5,69},{6,70},{7,71},{8,72},{9,... | collective-permute-start | bytes 786440 | tf_op jit(solution)/shard_map/ppermute | solution.py:383
  269.6 52.6 %collective-permute-start.4 = (f32[16,128,128]{2,1,0:T(8,128)}, f32[16,128,128]{2,1,0:T(8,128)}, u32[]{:S(2)}, u32[]{:S(2)}) collective-permute-start(f32[16,128,128]{2,1,0:T(8,128)} %constant_dynamic-update-slice_fusion.refs_0_), channel_id=1, source_target_pairs={{0,48},{8,56},{16,0},{24,8},{32,16},{40,24},{48,32},{56,40},{1,49}... | collective-permute-start | bytes 3145736 | tf_op jit(solution)/shard_map/ppermute | solution.py:366
  278.2 44.0 %collective-permute-start.3 = (f32[16,128,128]{2,1,0:T(8,128)}, f32[16,128,128]{2,1,0:T(8,128)}, u32[]{:S(2)}, u32[]{:S(2)}) collective-permute-start(f32[16,128,128]{2,1,0:T(8,128)} %constant_dynamic-update-slice_fusion.refs_0_), channel_id=1, source_target_pairs={{0,16},{8,24},{16,32},{24,40},{32,48},{40,56},{48,0},{56,8},{1,17}... | collective-permute-start | bytes 3145736 | tf_op jit(solution)/shard_map/ppermute | solution.py:366
  281.3 26.9 %collective-permute-start.19 = (f32[4,128,128]{2,1,0:T(8,128)S(1)}, f32[4,128,128]{2,1,0:T(8,128)S(1)}, u32[]{:S(2)}, u32[]{:S(2)}) collective-permute-start(f32[4,128,128]{2,1,0:T(8,128)S(1)} %select_select_fusion), channel_id=1, source_target_pairs={{0,16},{8,24},{16,0},{24,8},{32,48},{40,56},{48,32},{56,40},{1,17}... | collective-permute-start | bytes 786440 | tf_op jit(solution)/shard_map/ppermute | solution.py:366
  308.2 18.4 %collective-permute-start.20 = (f32[8,128,128]{2,1,0:T(8,128)S(1)}, f32[8,128,128]{2,1,0:T(8,128)S(1)}, u32[]{:S(2)}, u32[]{:S(2)}) collective-permute-start(f32[8,128,128]{2,1,0:T(8,128)S(1)} %pad_maximum_fusion.1.refs_15_), channel_id=1, source_target_pairs={{0,8},{8,0},{16,24},{24,16},{32,40},{40,32},{48,56},{56,48},{1,9},... | collective-permute-start | bytes 1572872 | tf_op jit(solution)/shard_map/ppermute | solution.py:366
  309.7 17.6 %collective-permute-start.15 = (f32[8,128,128]{2,1,0:T(8,128)S(1)}, f32[8,128,128]{2,1,0:T(8,128)S(1)}, u32[]{:S(2)}, u32[]{:S(2)}) collective-permute-start(f32[8,128,128]{2,1,0:T(8,128)S(1)} %slice.26), channel_id=1, source_target_pairs={{0,6},{1,7},{2,0},{3,1},{4,2},{5,3},{6,4},{7,5},{8,14},{9,15},{10,... | collective-permute-start | bytes 1572872 | tf_op jit(solution)/shard_map/ppermute | solution.py:366
  312.7 15.9 %collective-permute-start.14 = (f32[8,128,128]{2,1,0:T(8,128)S(1)}, f32[8,128,128]{2,1,0:T(8,128)S(1)}, u32[]{:S(2)}, u32[]{:S(2)}) collective-permute-start(f32[8,128,128]{2,1,0:T(8,128)S(1)} %slice.25), channel_id=1, source_target_pairs={{0,2},{1,3},{2,4},{3,5},{4,6},{5,7},{6,0},{7,1},{8,10},{9,11},{10,... | collective-permute-start | bytes 1572872 | tf_op jit(solution)/shard_map/ppermute | solution.py:366
  319.0 3.2 copy-start.1
  323.3 20.9 %collective-permute-start.8 = (f32[16,128,128]{2,1,0:T(8,128)}, f32[16,128,128]{2,1,0:T(8,128)}, u32[]{:S(2)}, u32[]{:S(2)}) collective-permute-start(f32[16,128,128]{2,1,0:T(8,128)} %collective-permute-done.3.refs_1_), channel_id=1, source_target_pairs={{0,8},{8,0},{16,24},{24,16},{32,40},{40,32},{48,56},{56,48},{1,9},... | collective-permute-start | bytes 3145736 | tf_op jit(solution)/shard_map/ppermute | solution.py:366
  324.9 14.5 %collective-permute-start.6 = (f32[8,128,128]{2,1,0:T(8,128)S(1)}, f32[8,128,128]{2,1,0:T(8,128)}, u32[]{:S(2)}, u32[]{:S(2)}) collective-permute-start(f32[8,128,128]{2,1,0:T(8,128)S(1)} %slice.21), channel_id=1, source_target_pairs={{0,48},{8,56},{16,0},{24,8},{32,16},{40,24},{48,32},{56,40},{1,49}... | collective-permute-start | bytes 1572872 | tf_op jit(solution)/shard_map/ppermute | solution.py:366
  326.6 14.5 %collective-permute-start.5 = (f32[8,128,128]{2,1,0:T(8,128)S(1)}, f32[8,128,128]{2,1,0:T(8,128)}, u32[]{:S(2)}, u32[]{:S(2)}) collective-permute-start(f32[8,128,128]{2,1,0:T(8,128)S(1)} %slice.20), channel_id=1, source_target_pairs={{0,16},{8,24},{16,32},{24,40},{32,48},{40,56},{48,0},{56,8},{1,17}... | collective-permute-start | bytes 1572872 | tf_op jit(solution)/shard_map/ppermute | solution.py:366
  327.3 0.8 copy-start.4
  328.1 16.1 %collective-permute-start.7 = (f32[16,128,128]{2,1,0:T(8,128)}, f32[16,128,128]{2,1,0:T(8,128)}, u32[]{:S(2)}, u32[]{:S(2)}) collective-permute-start(f32[16,128,128]{2,1,0:T(8,128)} %constant_dynamic-update-slice_fusion.refs_0_), channel_id=1, source_target_pairs={{0,8},{8,0},{16,24},{24,16},{32,40},{40,32},{48,56},{56,48},{1,9},... | collective-permute-start | bytes 3145736 | tf_op jit(solution)/shard_map/ppermute | solution.py:366
  328.6 0.8 copy-start.6
  329.4 14.8 %collective-permute-start.9 = (f32[16,128,128]{2,1,0:T(8,128)}, f32[16,128,128]{2,1,0:T(8,128)}, u32[]{:S(2)}, u32[]{:S(2)}) collective-permute-start(f32[16,128,128]{2,1,0:T(8,128)} %collective-permute-done.4.refs_2_), channel_id=1, source_target_pairs={{0,8},{8,0},{16,24},{24,16},{32,40},{40,32},{48,56},{56,48},{1,9},... | collective-permute-start | bytes 3145736 | tf_op jit(solution)/shard_map/ppermute | solution.py:366
  339.4 3.0 collective-permute-start.11
  341.2 3.0 collective-permute-start.10
  344.2 1.6 copy-start.3
  345.8 1.0 copy-start.5
  346.8 1.0 copy-start.7

commit v7 on v6

--- a/solution.py
+++ b/solution.py
@@ -310,7 +310,7 @@
             source = (at[1] + dy - at[3] + 8) % 4 * 2 + core
             rows = pl.ds(pl.multiple_of((at[0] ^ other) * TILE, TILE), TILE)
             lanes = pl.ds(pl.multiple_of(source * TILE, TILE), TILE)
-            raw[rows, lanes] = ref[n * LROWS + step]
+            raw[rows, lanes] = ref[n, 0]
     right_rows(right, raw[...])
     change = times_transposed(z[...], right[...])
     for t in range(LROWS):
@@ -338,7 +338,11 @@
         out_shape=jax.ShapeDtypeStruct((LROWS, LCOLS, TILE, TILE), f32),
         in_specs=[
             pl.BlockSpec(memory_space=pltpu.SMEM),
-            *[vmem] * 17,
+            *(
+                pl.BlockSpec((x.shape[0], 1, TILE, TILE), lambda j: (0, j, 0, 0))
+                for x in columns
+            ),
+            *[vmem] * 7,
             block,
             vmem,
         ],
@@ -354,7 +358,7 @@
             pltpu.VMEM((KP, PANEL), bf16),
             pltpu.VMEM((PANEL, PANEL), f32),
         ],
-        compiler_params=pltpu.CompilerParams(vmem_limit_bytes=32 * MIB),
+        compiler_params=pltpu.CompilerParams(vmem_limit_bytes=36 * MIB),
         cost_estimate=pl.CostEstimate(
             flops=24_000_000_000, bytes_accessed=30 * MIB, transcendentals=0
         ),
@@ -384,8 +388,7 @@
     b = lax.ppermute(top, "row", flip)
     c = lax.ppermute(top, ("sib", "row"), [(i, 8 + j) for i, j in flip])
     mine = jnp.where(row >= 4, jnp.where(sib == 0, top, a), jnp.where(sib == 0, b, c))
-    both = jnp.concatenate([mine, move(mine, "row", 8, lambda i: i ^ 2)], axis=0)
-    return [both, move(both, "row", 8, lambda i: i ^ 1)]
+    return jnp.concatenate([mine, move(mine, "row", 8, lambda i: i ^ 2)], axis=0)
 
 
 def gather(panel, arrived, landing):
@@ -401,16 +404,18 @@
     top = jnp.broadcast_to(panel[:1], (8, TILE, TILE))
     top = lax.all_to_all(top, "col", split_axis=0, concat_axis=0, tiled=True)[:PT]
     pair, top, across = lax.optimization_barrier((pair, top, across))
-    other = move(across, "sib", 2, lambda i: 1 - i)
     pieces = [pair, *both_ways(pair, "col")]
-    across, other, top = lax.optimization_barrier((across, other, top))
-    columns = [jnp.concatenate([across, other], axis=0)]
-    columns += both_ways(columns[0], "row")
+    pieces += opposite(*pieces[1:], "col")
     corner = gather_corner(top)
-    *columns, front = lax.optimization_barrier((*columns, add_up(False, arrived, landing)))
+    pair = jnp.concatenate([across, move(across, "sib", 2, lambda i: 1 - i)], axis=0)
+    pair, corner = lax.optimization_barrier((pair, corner))
+    columns = [pair, *both_ways(pair, "row")]
+    corner = [corner, move(corner, "row", 8, lambda i: i ^ 1)]
+    front = add_up(False, arrived, landing)
+    *columns, front = lax.optimization_barrier((*columns, front))
     columns += opposite(*columns[1:], "row")
-    pieces += opposite(*pieces[1:], "col")
-    columns += [move(x, "row", 8, lambda i: i ^ 1) for x in columns]
+    columns = columns + [move(x, "row", 8, lambda i: i ^ 1) for x in columns]
+    columns = [x.reshape(-1, LROWS, TILE, TILE) for x in columns]
     return columns, pieces, corner, front
 
 

time: 383 us -> 367 us (0.958)
  waiting for transfers between devices: 69.7 us -> 48.3 us
  starting transfers between devices: 34.1 us -> 42 us
    ppermute x17, waiting for transfers between devices: 46.6 us -> 24.9 us  [move(): return lax.ppermute(x, axis, [(i, to(i)) for i in range(size)])]
    ppermute x17, starting transfers between devices: 19.5 us -> 27.7 us  [move(): return lax.ppermute(x, axis, [(i, to(i)) for i in range(size)])]
    ppermute x1, waiting for transfers between devices: 2.7 us -> 7.15 us  [gather_corner(): c = lax.ppermute(top, ('sib', 'row'), [(i, 8 + j) for i, j in flip])]
    unnamed x19 -> x24, local copies, waits for them, and re-layouts: 12.7 us -> 15.2 us
  transfers between devices with their start and end apart: 22 -> 22, of which waited for: 9 -> 9; matrix products, arithmetic and copies ran while one was open for 3% -> 1% of each run, Pallas kernels for 2% -> 2%
where the time goes in v7:
time: 367 us; the launch traced here: 365 us
  blocking collectives  205 us (56%)
  waiting for transfers between devices  48.3 us (13%)
  Pallas kernels  46.7 us (13%)
  starting transfers between devices  42 us (11%)
  local copies, waits for them, and re-layouts  19.4 us (5%)
    all_to_all x1, blocking collectives, local(): lax.all_to_all(outgoing, ('sib', 'row', 'col'), split_axis=0, concat_axis...  205 us
    pallas_call x1, Pallas kernels, update(): pl.pallas_call(update_kernel, grid=(LCOLS // 2,), out_shape=jax.ShapeDtyp...  32.5 us
    ppermute x17, starting transfers between devices, move(): return lax.ppermute(x, axis, [(i, to(i)) for i in range(size)])  27.7 us
    ppermute x17, waiting for transfers between devices, move(): return lax.ppermute(x, axis, [(i, to(i)) for i in range(size)])  24.9 us
    unnamed x24, local copies, waits for them, and re-layouts  15.2 us
    all_to_all x1, waiting for transfers between devices, gather(): lax.all_to_all(top, 'col', split_axis=0, concat_axis=0, tiled=True)[:PT]  7.83 us
  transfers between devices with their start and end apart: 22, of which 9 were waited for; matrix products, arithmetic and copies ran while one was open for 1% of the time, Pallas kernels for 2%

profile of v7, /device:TPU:3, one launch (start us, length us, event | category | flops | bytes accessed | tf_op | source)
XLA Modules:
  0.0 365.5 jit_solution(15207460689581361592)
XLA Ops:
  0.7 0.7 and_select_fusion.5
  1.4 0.7 select_reduce_fusion.1
  2.8 3.4 copy-done
  6.2 1.7 pack.1
  7.9 204.9 %all_to_all.10.refs_0_.refs_1_ = f32[128,264,128]{2,1,0:T(8,128)} all-to-all(f32[128,264,128]{2,1,0:T(8,128)S(1)} %pack.1), channel_id=1, replica_groups=mesh['sib'=2,'row'=8,'col'=8] {'sib','row','col'}, dimensions={0} | all-to-all | bytes 34603008 | tf_op jit(solution)/shard_map/all_to_all | solution.py:453
  212.8 6.4 %add_panel.1 = (f32[8,128,128]{2,1,0:T(8,128)}, s32[8,128]{1,0:T(8,128)}) custom-call(f32[128,264,128]{2,1,0:T(8,128)} %all_to_all.10.refs_0_.refs_1_), custom_call_target="tpu_custom_call" | custom-call | tf_op jit(solution)/shard_map/add_panel/pallas_call | solution.py:115
  219.2 1.6 collective-permute-start
  220.7 0.9 slice_bitcast_fusion
  221.6 0.8 broadcast_in_dim.82
  222.4 4.3 %all-to-all-start.1 = ((f32[8,128,128]{2,1,0:T(8,128)}), f32[8,128,128]{2,1,0:T(8,128)S(1)}, u32[]{:S(2)}, u32[]{:S(2)}) async-start(f32[8,128,128]{2,1,0:T(8,128)} %broadcast_in_dim.82), calls=%async_computation.1 | async-start | bytes 1048576 | tf_op jit(solution)/shard_map/all_to_all | solution.py:405
  226.7 6.1 %collective-permute-start.1 = (f32[8,128,128]{2,1,0:T(8,128)}, f32[8,128,128]{2,1,0:T(8,128)S(1)}, u32[]{:S(2)}, u32[]{:S(2)}) collective-permute-start(f32[8,128,128]{2,1,0:T(8,128)} %get-tuple-element.16), channel_id=1, source_target_pairs={{0,0},{1,8},{2,16},{3,24},{4,32},{5,40},{6,48},{7,56},{8,1},{9,9},... | collective-permute-start | bytes 1572872 | tf_op jit(solution)/shard_map/ppermute | solution.py:402
  232.8 7.8 %all-to-all-done.1 = f32[8,128,128]{2,1,0:T(8,128)S(1)} async-done(((f32[8,128,128]{2,1,0:T(8,128)}), f32[8,128,128]{2,1,0:T(8,128)S(1)}, u32[]{:S(2)}, u32[]{:S(2)}) %all-to-all-start.1) | async-done | bytes 524320 | tf_op jit(solution)/shard_map/all_to_all | solution.py:405
  240.7 1.1 pad_maximum_fusion.refs_10_
  241.9 4.0 %collective-permute-done.1 = f32[8,128,128]{2,1,0:T(8,128)S(1)} collective-permute-done((f32[8,128,128]{2,1,0:T(8,128)}, f32[8,128,128]{2,1,0:T(8,128)S(1)}, u32[]{:S(2)}, u32[]{:S(2)}) %collective-permute-start.1) | collective-permute-done | bytes 524320 | tf_op jit(solution)/shard_map/ppermute | solution.py:402
  245.9 1.3 collective-permute-start.5
  247.1 1.3 collective-permute-start.4
  248.4 1.3 collective-permute-start.3
  249.8 2.6 collective-permute-start.2
  252.3 7.1 %collective-permute-done.5 = f32[4,128,128]{2,1,0:T(8,128)S(1)} collective-permute-done((f32[4,128,128]{2,1,0:T(8,128)S(1)}, f32[4,128,128]{2,1,0:T(8,128)S(1)}, u32[]{:S(2)}, u32[]{:S(2)}) %collective-permute-start.5) | collective-permute-done | bytes 262176 | tf_op jit(solution)/shard_map/ppermute | solution.py:389
  259.5 4.5 %collective-permute-done.4 = f32[4,128,128]{2,1,0:T(8,128)S(1)} collective-permute-done((f32[4,128,128]{2,1,0:T(8,128)S(1)}, f32[4,128,128]{2,1,0:T(8,128)S(1)}, u32[]{:S(2)}, u32[]{:S(2)}) %collective-permute-start.4) | collective-permute-done | bytes 262176 | tf_op jit(solution)/shard_map/ppermute | solution.py:388
  264.0 1.1 collective-permute-start.6
  265.2 4.2 %collective-permute-start.17 = (f32[16,128,128]{2,1,0:T(8,128)S(1)}, f32[16,128,128]{2,1,0:T(8,128)S(1)}, u32[]{:S(2)}, u32[]{:S(2)}) collective-permute-start(f32[16,128,128]{2,1,0:T(8,128)S(1)} %pad_maximum_fusion.refs_10_), channel_id=1, source_target_pairs={{0,6},{1,7},{2,0},{3,1},{4,2},{5,3},{6,4},{7,5},{8,14},{9,15},{10,... | collective-permute-start | bytes 3145736 | tf_op jit(solution)/shard_map/ppermute | solution.py:370
  269.4 0.8 collective-permute-done.6
  270.3 6.5 %collective-permute-start.8 = (f32[16,128,128]{2,1,0:T(8,128)S(1)}, f32[16,128,128]{2,1,0:T(8,128)}, u32[]{:S(2)}, u32[]{:S(2)}) collective-permute-start(f32[16,128,128]{2,1,0:T(8,128)S(1)} %pad_maximum_fusion.1), channel_id=1, source_target_pairs={{0,48},{8,56},{16,0},{24,8},{32,16},{40,24},{48,32},{56,40},{1,49}... | collective-permute-start | bytes 3145736 | tf_op jit(solution)/shard_map/ppermute | solution.py:370
  276.8 2.5 collective-permute-start.20
  279.3 12.1 %collective-permute-done.17.refs_12_ = f32[16,128,128]{2,1,0:T(8,128)S(1)} collective-permute-done((f32[16,128,128]{2,1,0:T(8,128)S(1)}, f32[16,128,128]{2,1,0:T(8,128)S(1)}, u32[]{:S(2)}, u32[]{:S(2)}) %collective-permute-start.17) | collective-permute-done | bytes 1048608 | tf_op jit(solution)/shard_map/ppermute | solution.py:370
  291.5 3.6 collective-permute-start.19
  295.2 0.8 copy-done.4
  296.0 6.1 %add_all.1.refs_17_ = f32[8,16,128,128]{3,2,1,0:T(8,128)S(1)} custom-call(s32[8,128]{1,0:T(8,128)S(1)} %copy-done.6, f32[128,264,128]{2,1,0:T(8,128)} %all_to_all.10.refs_0_.refs_1_), custom_call_target="tpu_custom_call" | custom-call | flops 1000 | bytes 25165824 | tf_op jit(solution)/shard_map/add_all/pallas_call | solution.py:132
  302.2 3.3 copy-done.1
  305.4 1.1 slice.20
  306.5 1.5 collective-permute-start.12
  308.1 1.1 slice.21
  309.2 2.0 collective-permute-start.9
  311.3 0.8 copy-done.8
  312.1 0.3 collective-permute-start.11
  312.4 0.8 copy-done.10
  313.4 10.2 %collective-permute-done.10 = f32[8,128,128]{2,1,0:T(8,128)} collective-permute-done((f32[8,128,128]{2,1,0:T(8,128)S(1)}, f32[8,128,128]{2,1,0:T(8,128)}, u32[]{:S(2)}, u32[]{:S(2)}) %collective-permute-start.10) | collective-permute-done | bytes 524320 | tf_op jit(solution)/shard_map/ppermute | solution.py:370
  323.6 0.6 collective-permute-start.15
  324.2 0.8 collective-permute-start.14
  325.1 1.0 collective-permute-done.15
  326.0 0.8 collective-permute-done.14
  326.9 1.2 copy-done.3
  328.1 1.2 copy-done.5
  329.3 1.6 copy-done.7
  330.9 1.0 copy-done.9
  331.9 1.0 copy-done.11
  333.0 32.5 %update.1 = f32[8,16,128,128]{3,2,1,0:T(8,128)} custom-call(s32[5]{0:T(128)S(1)} %stack.23.at, f32[2,8,128,128]{3,2,1,0:T(8,128)S(1)} %bitcast.43, f32[2,8,128,128]{3,2,1,0:T(8,128)} %bitcast.12.refs_1_, f32[2,8,128,128]{3,2,1,0:T(8,128)} %bitcast.13.refs_2_, f32[1,8,128,128]{3,2,1,0:T(8,128)} %bitcast.14.refs_3_, f32[1,8,128,128]{3,2,1,0:T(8,128)} %bitcast.15.refs_4_, ...), custom_call_target="tpu_custom_call" | custom-call | flops 24000000000 | bytes 31457280 | tf_op jit(solution)/shard_map/update/pallas_call | solution.py:335
  (48 shorter events, 1.5 us)
Async XLA Ops:
  2.8 3.4 copy-start
  219.2 76.9 %copy-start.6 = (s32[8,128]{1,0:T(8,128)S(1)}, s32[8,128]{1,0:T(8,128)}, u32[]{:S(2)}) copy-start(s32[8,128]{1,0:T(8,128)} %get-tuple-element.20.refs_0_) | copy-start | bytes 12292
  219.2 21.5 %collective-permute-start = (f32[8,128,128]{2,1,0:T(8,128)}, f32[8,128,128]{2,1,0:T(8,128)S(1)}, u32[]{:S(2)}, u32[]{:S(2)}) collective-permute-start(f32[8,128,128]{2,1,0:T(8,128)} %get-tuple-element.16), channel_id=1, source_target_pairs={{0,1},{1,0},{2,3},{3,2},{4,5},{5,4},{6,7},{7,6},{8,9},{9,8},{10,11... | collective-permute-start | bytes 1572872 | tf_op jit(solution)/shard_map/ppermute | solution.py:370
  222.4 18.2 %all-to-all-start.1 = ((f32[8,128,128]{2,1,0:T(8,128)}), f32[8,128,128]{2,1,0:T(8,128)S(1)}, u32[]{:S(2)}, u32[]{:S(2)}) async-start(f32[8,128,128]{2,1,0:T(8,128)} %broadcast_in_dim.82), calls=%async_computation.1 | async-start | bytes 1048576 | tf_op jit(solution)/shard_map/all_to_all | solution.py:405
  226.7 19.1 %collective-permute-start.1 = (f32[8,128,128]{2,1,0:T(8,128)}, f32[8,128,128]{2,1,0:T(8,128)S(1)}, u32[]{:S(2)}, u32[]{:S(2)}) collective-permute-start(f32[8,128,128]{2,1,0:T(8,128)} %get-tuple-element.16), channel_id=1, source_target_pairs={{0,0},{1,8},{2,16},{3,24},{4,32},{5,40},{6,48},{7,56},{8,1},{9,9},... | collective-permute-start | bytes 1572872 | tf_op jit(solution)/shard_map/ppermute | solution.py:402
  245.9 13.6 %collective-permute-start.5 = (f32[4,128,128]{2,1,0:T(8,128)S(1)}, f32[4,128,128]{2,1,0:T(8,128)S(1)}, u32[]{:S(2)}, u32[]{:S(2)}) collective-permute-start(f32[4,128,128]{2,1,0:T(8,128)S(1)} %slice.24), channel_id=1, source_target_pairs={{32,80},{40,88},{48,64},{56,72},{33,81},{41,89},{49,65},{57,73},{3... | collective-permute-start | bytes 786440 | tf_op jit(solution)/shard_map/ppermute | solution.py:389
  247.1 16.8 %collective-permute-start.4 = (f32[4,128,128]{2,1,0:T(8,128)S(1)}, f32[4,128,128]{2,1,0:T(8,128)S(1)}, u32[]{:S(2)}, u32[]{:S(2)}) collective-permute-start(f32[4,128,128]{2,1,0:T(8,128)S(1)} %slice.24), channel_id=1, source_target_pairs={{32,16},{40,24},{48,0},{56,8},{33,17},{41,25},{49,1},{57,9},{34,18... | collective-permute-start | bytes 786440 | tf_op jit(solution)/shard_map/ppermute | solution.py:388
  248.4 15.5 %collective-permute-start.3 = (f32[4,128,128]{2,1,0:T(8,128)S(1)}, f32[4,128,128]{2,1,0:T(8,128)S(1)}, u32[]{:S(2)}, u32[]{:S(2)}) collective-permute-start(f32[4,128,128]{2,1,0:T(8,128)S(1)} %slice.24), channel_id=1, source_target_pairs={{0,64},{1,65},{2,66},{3,67},{4,68},{5,69},{6,70},{7,71},{8,72},{9,... | collective-permute-start | bytes 786440 | tf_op jit(solution)/shard_map/ppermute | solution.py:387
  249.8 20.5 %collective-permute-start.2 = (f32[8,128,128]{2,1,0:T(8,128)S(1)}, f32[8,128,128]{2,1,0:T(8,128)S(1)}, u32[]{:S(2)}, u32[]{:S(2)}) collective-permute-start(f32[8,128,128]{2,1,0:T(8,128)S(1)} %collective-permute-done.1), channel_id=1, source_target_pairs={{0,64},{64,0},{1,65},{65,1},{2,66},{66,2},{3,67},{67,3},{4,68},{68... | collective-permute-start | bytes 1572872 | tf_op jit(solution)/shard_map/ppermute | solution.py:370
  264.0 6.2 %collective-permute-start.6 = (f32[4,128,128]{2,1,0:T(8,128)S(1)}, f32[4,128,128]{2,1,0:T(8,128)S(1)}, u32[]{:S(2)}, u32[]{:S(2)}) collective-permute-start(f32[4,128,128]{2,1,0:T(8,128)S(1)} %select_select_fusion), channel_id=1, source_target_pairs={{0,16},{8,24},{16,0},{24,8},{32,48},{40,56},{48,32},{56,40},{1,17}... | collective-permute-start | bytes 786440 | tf_op jit(solution)/shard_map/ppermute | solution.py:370
  265.2 26.3 %collective-permute-start.17 = (f32[16,128,128]{2,1,0:T(8,128)S(1)}, f32[16,128,128]{2,1,0:T(8,128)S(1)}, u32[]{:S(2)}, u32[]{:S(2)}) collective-permute-start(f32[16,128,128]{2,1,0:T(8,128)S(1)} %pad_maximum_fusion.refs_10_), channel_id=1, source_target_pairs={{0,6},{1,7},{2,0},{3,1},{4,2},{5,3},{6,4},{7,5},{8,14},{9,15},{10,... | collective-permute-start | bytes 3145736 | tf_op jit(solution)/shard_map/ppermute | solution.py:370
  269.4 25.7 %collective-permute-start.16 = (f32[16,128,128]{2,1,0:T(8,128)S(1)}, f32[16,128,128]{2,1,0:T(8,128)S(1)}, u32[]{:S(2)}, u32[]{:S(2)}) collective-permute-start(f32[16,128,128]{2,1,0:T(8,128)S(1)} %pad_maximum_fusion.refs_10_), channel_id=1, source_target_pairs={{0,2},{1,3},{2,4},{3,5},{4,6},{5,7},{6,0},{7,1},{8,10},{9,11},{10,... | collective-permute-start | bytes 3145736 | tf_op jit(solution)/shard_map/ppermute | solution.py:370
  270.3 35.1 %collective-permute-start.8 = (f32[16,128,128]{2,1,0:T(8,128)S(1)}, f32[16,128,128]{2,1,0:T(8,128)}, u32[]{:S(2)}, u32[]{:S(2)}) collective-permute-start(f32[16,128,128]{2,1,0:T(8,128)S(1)} %pad_maximum_fusion.1), channel_id=1, source_target_pairs={{0,48},{8,56},{16,0},{24,8},{32,16},{40,24},{48,32},{56,40},{1,49}... | collective-permute-start | bytes 3145736 | tf_op jit(solution)/shard_map/ppermute | solution.py:370
  276.8 28.6 %collective-permute-start.7 = (f32[16,128,128]{2,1,0:T(8,128)S(1)}, f32[16,128,128]{2,1,0:T(8,128)}, u32[]{:S(2)}, u32[]{:S(2)}) collective-permute-start(f32[16,128,128]{2,1,0:T(8,128)S(1)} %pad_maximum_fusion.1), channel_id=1, source_target_pairs={{0,16},{8,24},{16,32},{24,40},{32,48},{40,56},{48,0},{56,8},{1,17}... | collective-permute-start | bytes 3145736 | tf_op jit(solution)/shard_map/ppermute | solution.py:370
  276.8 32.4 %collective-permute-start.20 = (f32[8,128,128]{2,1,0:T(8,128)S(1)}, f32[8,128,128]{2,1,0:T(8,128)S(1)}, u32[]{:S(2)}, u32[]{:S(2)}) collective-permute-start(f32[8,128,128]{2,1,0:T(8,128)S(1)} %pad_maximum_fusion.2.refs_15_), channel_id=1, source_target_pairs={{0,8},{8,0},{16,24},{24,16},{32,40},{40,32},{48,56},{56,48},{1,9},... | collective-permute-start | bytes 1572872 | tf_op jit(solution)/shard_map/ppermute | solution.py:370
  291.4 3.8 %copy-start.2 = (f32[16,128,128]{2,1,0:T(8,128)}, f32[16,128,128]{2,1,0:T(8,128)S(1)}, u32[]{:S(2)}) copy-start(f32[16,128,128]{2,1,0:T(8,128)S(1)} %collective-permute-done.17.refs_12_) | copy-start | bytes 3145732
  291.5 19.8 %collective-permute-start.19 = (f32[8,128,128]{2,1,0:T(8,128)S(1)}, f32[8,128,128]{2,1,0:T(8,128)S(1)}, u32[]{:S(2)}, u32[]{:S(2)}) collective-permute-start(f32[8,128,128]{2,1,0:T(8,128)S(1)} %slice.26), channel_id=1, source_target_pairs={{0,6},{1,7},{2,0},{3,1},{4,2},{5,3},{6,4},{7,5},{8,14},{9,15},{10,... | collective-permute-start | bytes 1572872 | tf_op jit(solution)/shard_map/ppermute | solution.py:370
  295.0 1.0 copy-start.4
  295.1 17.3 %collective-permute-start.18 = (f32[8,128,128]{2,1,0:T(8,128)S(1)}, f32[8,128,128]{2,1,0:T(8,128)S(1)}, u32[]{:S(2)}, u32[]{:S(2)}) collective-permute-start(f32[8,128,128]{2,1,0:T(8,128)S(1)} %slice.25), channel_id=1, source_target_pairs={{0,2},{1,3},{2,4},{3,5},{4,6},{5,7},{6,0},{7,1},{8,10},{9,11},{10,... | collective-permute-start | bytes 1572872 | tf_op jit(solution)/shard_map/ppermute | solution.py:370
  302.2 3.3 copy-start.1
  306.5 20.3 %collective-permute-start.12 = (f32[16,128,128]{2,1,0:T(8,128)}, f32[16,128,128]{2,1,0:T(8,128)}, u32[]{:S(2)}, u32[]{:S(2)}) collective-permute-start(f32[16,128,128]{2,1,0:T(8,128)} %collective-permute-done.7), channel_id=1, source_target_pairs={{0,8},{8,0},{16,24},{24,16},{32,40},{40,32},{48,56},{56,48},{1,9},... | collective-permute-start | bytes 3145736 | tf_op jit(solution)/shard_map/ppermute | solution.py:370
  309.2 14.4 %collective-permute-start.10 = (f32[8,128,128]{2,1,0:T(8,128)S(1)}, f32[8,128,128]{2,1,0:T(8,128)}, u32[]{:S(2)}, u32[]{:S(2)}) collective-permute-start(f32[8,128,128]{2,1,0:T(8,128)S(1)} %slice.21), channel_id=1, source_target_pairs={{0,48},{8,56},{16,0},{24,8},{32,16},{40,24},{48,32},{56,40},{1,49}... | collective-permute-start | bytes 1572872 | tf_op jit(solution)/shard_map/ppermute | solution.py:370
  309.2 14.9 %collective-permute-start.9 = (f32[8,128,128]{2,1,0:T(8,128)S(1)}, f32[8,128,128]{2,1,0:T(8,128)}, u32[]{:S(2)}, u32[]{:S(2)}) collective-permute-start(f32[8,128,128]{2,1,0:T(8,128)S(1)} %slice.20), channel_id=1, source_target_pairs={{0,16},{8,24},{16,32},{24,40},{32,48},{40,56},{48,0},{56,8},{1,17}... | collective-permute-start | bytes 1572872 | tf_op jit(solution)/shard_map/ppermute | solution.py:370
  311.3 0.8 copy-start.8
  312.1 14.8 %collective-permute-start.11 = (f32[16,128,128]{2,1,0:T(8,128)S(1)}, f32[16,128,128]{2,1,0:T(8,128)}, u32[]{:S(2)}, u32[]{:S(2)}) collective-permute-start(f32[16,128,128]{2,1,0:T(8,128)S(1)} %pad_maximum_fusion.1), channel_id=1, source_target_pairs={{0,8},{8,0},{16,24},{24,16},{32,40},{40,32},{48,56},{56,48},{1,9},... | collective-permute-start | bytes 3145736 | tf_op jit(solution)/shard_map/ppermute | solution.py:370
  312.4 0.8 copy-start.10
  313.2 13.7 %collective-permute-start.13 = (f32[16,128,128]{2,1,0:T(8,128)}, f32[16,128,128]{2,1,0:T(8,128)}, u32[]{:S(2)}, u32[]{:S(2)}) collective-permute-start(f32[16,128,128]{2,1,0:T(8,128)} %collective-permute-done.8), channel_id=1, source_target_pairs={{0,8},{8,0},{16,24},{24,16},{32,40},{40,32},{48,56},{56,48},{1,9},... | collective-permute-start | bytes 3145736 | tf_op jit(solution)/shard_map/ppermute | solution.py:370
  323.6 2.5 collective-permute-start.15
  324.2 2.7 collective-permute-start.14
  326.9 1.2 copy-start.3
  328.1 1.2 copy-start.5
  329.3 1.6 copy-start.7
  330.9 1.0 copy-start.9
  331.9 1.0 copy-start.11

commit v8 on v7

--- a/solution.py
+++ b/solution.py
@@ -358,7 +358,7 @@
             pltpu.VMEM((KP, PANEL), bf16),
             pltpu.VMEM((PANEL, PANEL), f32),
         ],
-        compiler_params=pltpu.CompilerParams(vmem_limit_bytes=36 * MIB),
+        compiler_params=pltpu.CompilerParams(vmem_limit_bytes=26 * MIB),
         cost_estimate=pl.CostEstimate(
             flops=24_000_000_000, bytes_accessed=30 * MIB, transcendentals=0
         ),

time: 367 us -> 370 us (level)
  starting transfers between devices: 42 us -> 33.1 us
  waiting for transfers between devices: 48.3 us -> 56.4 us
    ppermute x17, starting transfers between devices: 27.7 us -> 19.2 us  [move(): return lax.ppermute(x, axis, [(i, to(i)) for i in range(size)])]
    ppermute x17, waiting for transfers between devices: 24.9 us -> 29.3 us  [move(): return lax.ppermute(x, axis, [(i, to(i)) for i in range(size)])]
    unnamed x24 -> x26, local copies, waits for them, and re-layouts: 15.2 us -> 18.8 us
  transfers between devices with their start and end apart: 22 -> 22, of which waited for: 9 -> 10; matrix products, arithmetic and copies ran while one was open for 1% -> 1% of each run, Pallas kernels for 2% -> 2%
where the time goes in v8:
time: 370 us; the launch traced here: 369 us
  blocking collectives  205 us (55%)
  waiting for transfers between devices  56.4 us (15%)
  Pallas kernels  47.6 us (13%)
  starting transfers between devices  33.1 us (9%)
  local copies, waits for them, and re-layouts  23 us (6%)
    all_to_all x1, blocking collectives, local(): lax.all_to_all(outgoing, ('sib', 'row', 'col'), split_axis=0, concat_axis...  205 us
    pallas_call x1, Pallas kernels, update(): pl.pallas_call(update_kernel, grid=(LCOLS // 2,), out_shape=jax.ShapeDtyp...  32.2 us
    ppermute x17, waiting for transfers between devices, move(): return lax.ppermute(x, axis, [(i, to(i)) for i in range(size)])  29.3 us
    ppermute x17, starting transfers between devices, move(): return lax.ppermute(x, axis, [(i, to(i)) for i in range(size)])  19.2 us
    unnamed x26, local copies, waits for them, and re-layouts  18.8 us
    all_to_all x1, waiting for transfers between devices, gather(): lax.all_to_all(top, 'col', split_axis=0, concat_axis=0, tiled=True)[:PT]  10.2 us
  transfers between devices with their start and end apart: 22, of which 10 were waited for; matrix products, arithmetic and copies ran while one was open for 1% of the time, Pallas kernels for 2%

profile of v8, /device:TPU:3, one launch (start us, length us, event | category | flops | bytes accessed | tf_op | source)
XLA Modules:
  0.0 369.0 jit_solution(1931679985081068064)
XLA Ops:
  0.7 0.7 and_select_fusion.5
  1.4 0.7 select_reduce_fusion.1
  2.8 3.4 copy-done
  6.2 1.8 pack.1
  8.0 204.7 %all_to_all.10.refs_0_.refs_1_ = f32[128,264,128]{2,1,0:T(8,128)} all-to-all(f32[128,264,128]{2,1,0:T(8,128)S(1)} %pack.1), channel_id=1, replica_groups=mesh['sib'=2,'row'=8,'col'=8] {'sib','row','col'}, dimensions={0} | all-to-all | bytes 34603008 | tf_op jit(solution)/shard_map/all_to_all | solution.py:453
  212.7 7.3 %add_panel.1 = (f32[8,128,128]{2,1,0:T(8,128)}, s32[8,128]{1,0:T(8,128)}) custom-call(f32[128,264,128]{2,1,0:T(8,128)} %all_to_all.10.refs_0_.refs_1_), custom_call_target="tpu_custom_call" | custom-call | tf_op jit(solution)/shard_map/add_panel/pallas_call | solution.py:115
  220.0 0.9 slice_bitcast_fusion
  220.9 0.9 broadcast_in_dim.82
  221.8 4.2 %all-to-all-start.1 = ((f32[8,128,128]{2,1,0:T(8,128)}), f32[8,128,128]{2,1,0:T(8,128)S(1)}, u32[]{:S(2)}, u32[]{:S(2)}) async-start(f32[8,128,128]{2,1,0:T(8,128)} %broadcast_in_dim.82), calls=%async_computation.1 | async-start | bytes 1048576 | tf_op jit(solution)/shard_map/all_to_all | solution.py:405
  226.0 5.9 %collective-permute-start.1 = (f32[8,128,128]{2,1,0:T(8,128)}, f32[8,128,128]{2,1,0:T(8,128)S(1)}, u32[]{:S(2)}, u32[]{:S(2)}) collective-permute-start(f32[8,128,128]{2,1,0:T(8,128)} %get-tuple-element.16), channel_id=1, source_target_pairs={{0,0},{1,8},{2,16},{3,24},{4,32},{5,40},{6,48},{7,56},{8,1},{9,9},... | collective-permute-start | bytes 1572872 | tf_op jit(solution)/shard_map/ppermute | solution.py:402
  231.9 10.2 %all-to-all-done.1 = f32[8,128,128]{2,1,0:T(8,128)S(1)} async-done(((f32[8,128,128]{2,1,0:T(8,128)}), f32[8,128,128]{2,1,0:T(8,128)S(1)}, u32[]{:S(2)}, u32[]{:S(2)}) %all-to-all-start.1) | async-done | bytes 524320 | tf_op jit(solution)/shard_map/all_to_all | solution.py:405
  242.2 1.1 pad_maximum_fusion.refs_10_
  243.3 3.3 collective-permute-done.1
  246.6 1.3 collective-permute-start.5
  247.9 1.3 collective-permute-start.4
  249.2 1.3 collective-permute-start.3
  250.5 2.2 collective-permute-start.2
  252.7 6.2 %collective-permute-done.5 = f32[4,128,128]{2,1,0:T(8,128)S(1)} collective-permute-done((f32[4,128,128]{2,1,0:T(8,128)S(1)}, f32[4,128,128]{2,1,0:T(8,128)S(1)}, u32[]{:S(2)}, u32[]{:S(2)}) %collective-permute-start.5) | collective-permute-done | bytes 262176 | tf_op jit(solution)/shard_map/ppermute | solution.py:389
  258.9 7.4 %collective-permute-done.4 = f32[4,128,128]{2,1,0:T(8,128)S(1)} collective-permute-done((f32[4,128,128]{2,1,0:T(8,128)S(1)}, f32[4,128,128]{2,1,0:T(8,128)S(1)}, u32[]{:S(2)}, u32[]{:S(2)}) %collective-permute-start.4) | collective-permute-done | bytes 262176 | tf_op jit(solution)/shard_map/ppermute | solution.py:388
  266.4 2.9 collective-permute-start.17
  269.3 4.4 %collective-permute-done.6 = f32[4,128,128]{2,1,0:T(8,128)S(1)} collective-permute-done((f32[4,128,128]{2,1,0:T(8,128)S(1)}, f32[4,128,128]{2,1,0:T(8,128)S(1)}, u32[]{:S(2)}, u32[]{:S(2)}) %collective-permute-start.6) | collective-permute-done | bytes 262176 | tf_op jit(solution)/shard_map/ppermute | solution.py:370
  273.9 2.3 collective-permute-start.8
  276.2 2.6 collective-permute-start.20
  278.8 12.6 %collective-permute-done.17.refs_12_ = f32[16,128,128]{2,1,0:T(8,128)S(1)} collective-permute-done((f32[16,128,128]{2,1,0:T(8,128)S(1)}, f32[16,128,128]{2,1,0:T(8,128)S(1)}, u32[]{:S(2)}, u32[]{:S(2)}) %collective-permute-start.17) | collective-permute-done | bytes 1048608 | tf_op jit(solution)/shard_map/ppermute | solution.py:370
  291.4 3.6 collective-permute-start.19
  295.1 0.8 copy-done.5
  296.0 6.3 %add_all.1.refs_17_ = f32[8,16,128,128]{3,2,1,0:T(8,128)S(1)} custom-call(s32[8,128]{1,0:T(8,128)S(1)} %copy-done.7, f32[128,264,128]{2,1,0:T(8,128)} %all_to_all.10.refs_0_.refs_1_), custom_call_target="tpu_custom_call" | custom-call | flops 1000 | bytes 25165824 | tf_op jit(solution)/shard_map/add_all/pallas_call | solution.py:132
  302.3 3.4 copy-done.1
  305.7 1.1 slice.20
  306.7 1.7 collective-permute-start.12
  308.4 1.1 slice.21
  309.6 1.5 collective-permute-start.9
  311.1 0.8 copy-done.9
  311.9 0.6 collective-permute-start.11
  312.5 0.8 copy-done.11
  313.3 10.0 %collective-permute-done.10 = f32[8,128,128]{2,1,0:T(8,128)} collective-permute-done((f32[8,128,128]{2,1,0:T(8,128)S(1)}, f32[8,128,128]{2,1,0:T(8,128)}, u32[]{:S(2)}, u32[]{:S(2)}) %collective-permute-start.10) | collective-permute-done | bytes 524320 | tf_op jit(solution)/shard_map/ppermute | solution.py:370
  323.2 0.8 collective-permute-start.15
  324.0 0.5 collective-permute-done.9
  324.5 0.8 collective-permute-start.14
  325.4 0.5 collective-permute-done.15
  325.9 1.3 collective-permute-done.14
  327.2 3.4 copy-done.2
  330.6 1.2 copy-done.4
  331.8 1.2 copy-done.6
  333.1 1.6 copy-done.8
  334.7 1.0 copy-done.10
  335.7 1.0 copy-done.12
  336.7 32.2 %update.1 = f32[8,16,128,128]{3,2,1,0:T(8,128)} custom-call(s32[5]{0:T(128)S(1)} %stack.23.at, f32[2,8,128,128]{3,2,1,0:T(8,128)S(1)} %bitcast.43, f32[2,8,128,128]{3,2,1,0:T(8,128)} %bitcast.12.refs_1_, f32[2,8,128,128]{3,2,1,0:T(8,128)} %bitcast.13.refs_2_, f32[1,8,128,128]{3,2,1,0:T(8,128)} %bitcast.14.refs_3_, f32[1,8,128,128]{3,2,1,0:T(8,128)} %bitcast.15.refs_4_, ...), custom_call_target="tpu_custom_call" | custom-call | flops 24000000000 | bytes 31457280 | tf_op jit(solution)/shard_map/update/pallas_call | solution.py:335
  (50 shorter events, 1.4 us)
Async XLA Ops:
  2.8 3.4 copy-start
  219.9 76.0 %copy-start.7 = (s32[8,128]{1,0:T(8,128)S(1)}, s32[8,128]{1,0:T(8,128)}, u32[]{:S(2)}) copy-start(s32[8,128]{1,0:T(8,128)} %get-tuple-element.20.refs_0_) | copy-start | bytes 12292
  219.9 22.2 %collective-permute-start = (f32[8,128,128]{2,1,0:T(8,128)}, f32[8,128,128]{2,1,0:T(8,128)S(1)}, u32[]{:S(2)}, u32[]{:S(2)}) collective-permute-start(f32[8,128,128]{2,1,0:T(8,128)} %get-tuple-element.16), channel_id=1, source_target_pairs={{0,1},{1,0},{2,3},{3,2},{4,5},{5,4},{6,7},{7,6},{8,9},{9,8},{10,11... | collective-permute-start | bytes 1572872 | tf_op jit(solution)/shard_map/ppermute | solution.py:370
  221.8 20.4 %all-to-all-start.1 = ((f32[8,128,128]{2,1,0:T(8,128)}), f32[8,128,128]{2,1,0:T(8,128)S(1)}, u32[]{:S(2)}, u32[]{:S(2)}) async-start(f32[8,128,128]{2,1,0:T(8,128)} %broadcast_in_dim.82), calls=%async_computation.1 | async-start | bytes 1048576 | tf_op jit(solution)/shard_map/all_to_all | solution.py:405
  226.0 20.6 %collective-permute-start.1 = (f32[8,128,128]{2,1,0:T(8,128)}, f32[8,128,128]{2,1,0:T(8,128)S(1)}, u32[]{:S(2)}, u32[]{:S(2)}) collective-permute-start(f32[8,128,128]{2,1,0:T(8,128)} %get-tuple-element.16), channel_id=1, source_target_pairs={{0,0},{1,8},{2,16},{3,24},{4,32},{5,40},{6,48},{7,56},{8,1},{9,9},... | collective-permute-start | bytes 1572872 | tf_op jit(solution)/shard_map/ppermute | solution.py:402
  246.6 12.2 %collective-permute-start.5 = (f32[4,128,128]{2,1,0:T(8,128)S(1)}, f32[4,128,128]{2,1,0:T(8,128)S(1)}, u32[]{:S(2)}, u32[]{:S(2)}) collective-permute-start(f32[4,128,128]{2,1,0:T(8,128)S(1)} %slice.24), channel_id=1, source_target_pairs={{32,80},{40,88},{48,64},{56,72},{33,81},{41,89},{49,65},{57,73},{3... | collective-permute-start | bytes 786440 | tf_op jit(solution)/shard_map/ppermute | solution.py:389
  247.9 18.3 %collective-permute-start.4 = (f32[4,128,128]{2,1,0:T(8,128)S(1)}, f32[4,128,128]{2,1,0:T(8,128)S(1)}, u32[]{:S(2)}, u32[]{:S(2)}) collective-permute-start(f32[4,128,128]{2,1,0:T(8,128)S(1)} %slice.24), channel_id=1, source_target_pairs={{32,16},{40,24},{48,0},{56,8},{33,17},{41,25},{49,1},{57,9},{34,18... | collective-permute-start | bytes 786440 | tf_op jit(solution)/shard_map/ppermute | solution.py:388
  249.2 17.0 %collective-permute-start.3 = (f32[4,128,128]{2,1,0:T(8,128)S(1)}, f32[4,128,128]{2,1,0:T(8,128)S(1)}, u32[]{:S(2)}, u32[]{:S(2)}) collective-permute-start(f32[4,128,128]{2,1,0:T(8,128)S(1)} %slice.24), channel_id=1, source_target_pairs={{0,64},{1,65},{2,66},{3,67},{4,68},{5,69},{6,70},{7,71},{8,72},{9,... | collective-permute-start | bytes 786440 | tf_op jit(solution)/shard_map/ppermute | solution.py:387
  250.5 23.3 %collective-permute-start.2 = (f32[8,128,128]{2,1,0:T(8,128)S(1)}, f32[8,128,128]{2,1,0:T(8,128)S(1)}, u32[]{:S(2)}, u32[]{:S(2)}) collective-permute-start(f32[8,128,128]{2,1,0:T(8,128)S(1)} %collective-permute-done.1), channel_id=1, source_target_pairs={{0,64},{64,0},{1,65},{65,1},{2,66},{66,2},{3,67},{67,3},{4,68},{68... | collective-permute-start | bytes 1572872 | tf_op jit(solution)/shard_map/ppermute | solution.py:370
  266.3 7.5 %collective-permute-start.6 = (f32[4,128,128]{2,1,0:T(8,128)S(1)}, f32[4,128,128]{2,1,0:T(8,128)S(1)}, u32[]{:S(2)}, u32[]{:S(2)}) collective-permute-start(f32[4,128,128]{2,1,0:T(8,128)S(1)} %select_select_fusion), channel_id=1, source_target_pairs={{0,16},{8,24},{16,0},{24,8},{32,48},{40,56},{48,32},{56,40},{1,17}... | collective-permute-start | bytes 786440 | tf_op jit(solution)/shard_map/ppermute | solution.py:370
  266.4 25.0 %collective-permute-start.17 = (f32[16,128,128]{2,1,0:T(8,128)S(1)}, f32[16,128,128]{2,1,0:T(8,128)S(1)}, u32[]{:S(2)}, u32[]{:S(2)}) collective-permute-start(f32[16,128,128]{2,1,0:T(8,128)S(1)} %pad_maximum_fusion.refs_10_), channel_id=1, source_target_pairs={{0,6},{1,7},{2,0},{3,1},{4,2},{5,3},{6,4},{7,5},{8,14},{9,15},{10,... | collective-permute-start | bytes 3145736 | tf_op jit(solution)/shard_map/ppermute | solution.py:370
  269.3 25.7 %collective-permute-start.16 = (f32[16,128,128]{2,1,0:T(8,128)S(1)}, f32[16,128,128]{2,1,0:T(8,128)S(1)}, u32[]{:S(2)}, u32[]{:S(2)}) collective-permute-start(f32[16,128,128]{2,1,0:T(8,128)S(1)} %pad_maximum_fusion.refs_10_), channel_id=1, source_target_pairs={{0,2},{1,3},{2,4},{3,5},{4,6},{5,7},{6,0},{7,1},{8,10},{9,11},{10,... | collective-permute-start | bytes 3145736 | tf_op jit(solution)/shard_map/ppermute | solution.py:370
  273.9 31.8 %collective-permute-start.8 = (f32[16,128,128]{2,1,0:T(8,128)S(1)}, f32[16,128,128]{2,1,0:T(8,128)}, u32[]{:S(2)}, u32[]{:S(2)}) collective-permute-start(f32[16,128,128]{2,1,0:T(8,128)S(1)} %pad_maximum_fusion.1), channel_id=1, source_target_pairs={{0,48},{8,56},{16,0},{24,8},{32,16},{40,24},{48,32},{56,40},{1,49}... | collective-permute-start | bytes 3145736 | tf_op jit(solution)/shard_map/ppermute | solution.py:370
  276.2 29.5 %collective-permute-start.7 = (f32[16,128,128]{2,1,0:T(8,128)S(1)}, f32[16,128,128]{2,1,0:T(8,128)}, u32[]{:S(2)}, u32[]{:S(2)}) collective-permute-start(f32[16,128,128]{2,1,0:T(8,128)S(1)} %pad_maximum_fusion.1), channel_id=1, source_target_pairs={{0,16},{8,24},{16,32},{24,40},{32,48},{40,56},{48,0},{56,8},{1,17}... | collective-permute-start | bytes 3145736 | tf_op jit(solution)/shard_map/ppermute | solution.py:370
  276.2 33.4 %collective-permute-start.20 = (f32[8,128,128]{2,1,0:T(8,128)S(1)}, f32[8,128,128]{2,1,0:T(8,128)S(1)}, u32[]{:S(2)}, u32[]{:S(2)}) collective-permute-start(f32[8,128,128]{2,1,0:T(8,128)S(1)} %pad_maximum_fusion.2.refs_15_), channel_id=1, source_target_pairs={{0,8},{8,0},{16,24},{24,16},{32,40},{40,32},{48,56},{56,48},{1,9},... | collective-permute-start | bytes 1572872 | tf_op jit(solution)/shard_map/ppermute | solution.py:370
  291.3 3.8 %copy-start.3 = (f32[16,128,128]{2,1,0:T(8,128)}, f32[16,128,128]{2,1,0:T(8,128)S(1)}, u32[]{:S(2)}) copy-start(f32[16,128,128]{2,1,0:T(8,128)S(1)} %collective-permute-done.17.refs_12_) | copy-start | bytes 3145732
  291.4 19.7 %collective-permute-start.19 = (f32[8,128,128]{2,1,0:T(8,128)S(1)}, f32[8,128,128]{2,1,0:T(8,128)S(1)}, u32[]{:S(2)}, u32[]{:S(2)}) collective-permute-start(f32[8,128,128]{2,1,0:T(8,128)S(1)} %slice.26), channel_id=1, source_target_pairs={{0,6},{1,7},{2,0},{3,1},{4,2},{5,3},{6,4},{7,5},{8,14},{9,15},{10,... | collective-permute-start | bytes 1572872 | tf_op jit(solution)/shard_map/ppermute | solution.py:370
  295.0 1.0 copy-start.5
  295.0 17.4 %collective-permute-start.18 = (f32[8,128,128]{2,1,0:T(8,128)S(1)}, f32[8,128,128]{2,1,0:T(8,128)S(1)}, u32[]{:S(2)}, u32[]{:S(2)}) collective-permute-start(f32[8,128,128]{2,1,0:T(8,128)S(1)} %slice.25), channel_id=1, source_target_pairs={{0,2},{1,3},{2,4},{3,5},{4,6},{5,7},{6,0},{7,1},{8,10},{9,11},{10,... | collective-permute-start | bytes 1572872 | tf_op jit(solution)/shard_map/ppermute | solution.py:370
  302.3 3.4 copy-start.1
  306.7 20.5 %collective-permute-start.12 = (f32[16,128,128]{2,1,0:T(8,128)}, f32[16,128,128]{2,1,0:T(8,128)}, u32[]{:S(2)}, u32[]{:S(2)}) collective-permute-start(f32[16,128,128]{2,1,0:T(8,128)} %collective-permute-done.7), channel_id=1, source_target_pairs={{0,8},{8,0},{16,24},{24,16},{32,40},{40,32},{48,56},{56,48},{1,9},... | collective-permute-start | bytes 3145736 | tf_op jit(solution)/shard_map/ppermute | solution.py:370
  309.5 13.7 %collective-permute-start.10 = (f32[8,128,128]{2,1,0:T(8,128)S(1)}, f32[8,128,128]{2,1,0:T(8,128)}, u32[]{:S(2)}, u32[]{:S(2)}) collective-permute-start(f32[8,128,128]{2,1,0:T(8,128)S(1)} %slice.21), channel_id=1, source_target_pairs={{0,48},{8,56},{16,0},{24,8},{32,16},{40,24},{48,32},{56,40},{1,49}... | collective-permute-start | bytes 1572872 | tf_op jit(solution)/shard_map/ppermute | solution.py:370
  309.6 14.9 %collective-permute-start.9 = (f32[8,128,128]{2,1,0:T(8,128)S(1)}, f32[8,128,128]{2,1,0:T(8,128)}, u32[]{:S(2)}, u32[]{:S(2)}) collective-permute-start(f32[8,128,128]{2,1,0:T(8,128)S(1)} %slice.20), channel_id=1, source_target_pairs={{0,16},{8,24},{16,32},{24,40},{32,48},{40,56},{48,0},{56,8},{1,17}... | collective-permute-start | bytes 1572872 | tf_op jit(solution)/shard_map/ppermute | solution.py:370
  311.1 0.8 copy-start.9
  311.9 15.3 %collective-permute-start.11 = (f32[16,128,128]{2,1,0:T(8,128)S(1)}, f32[16,128,128]{2,1,0:T(8,128)}, u32[]{:S(2)}, u32[]{:S(2)}) collective-permute-start(f32[16,128,128]{2,1,0:T(8,128)S(1)} %pad_maximum_fusion.1), channel_id=1, source_target_pairs={{0,8},{8,0},{16,24},{24,16},{32,40},{40,32},{48,56},{56,48},{1,9},... | collective-permute-start | bytes 3145736 | tf_op jit(solution)/shard_map/ppermute | solution.py:370
  312.5 0.8 copy-start.11
  313.3 13.9 %collective-permute-start.13 = (f32[16,128,128]{2,1,0:T(8,128)}, f32[16,128,128]{2,1,0:T(8,128)}, u32[]{:S(2)}, u32[]{:S(2)}) collective-permute-start(f32[16,128,128]{2,1,0:T(8,128)} %collective-permute-done.8), channel_id=1, source_target_pairs={{0,8},{8,0},{16,24},{24,16},{32,40},{40,32},{48,56},{56,48},{1,9},... | collective-permute-start | bytes 3145736 | tf_op jit(solution)/shard_map/ppermute | solution.py:370
  323.2 2.7 collective-permute-start.15
  324.5 2.7 collective-permute-start.14
  327.2 3.4 copy-start.2
  330.6 1.2 copy-start.4
  331.8 1.2 copy-start.6
  333.1 1.6 copy-start.8
  334.7 1.0 copy-start.10
  335.7 1.0 copy-start.12

commit v9 on v8

--- a/solution.py
+++ b/solution.py
@@ -188,12 +188,14 @@
     return times(x[...], w[:, :BLOCK]), times(x[:, KB:], w[KB:, BLOCK:])
 
 
-def row_factors(at, pieces, corner, inverses, z, own, f0, f1, left, r_rows, r_cols, low):
+def row_factors(at, pieces, corner, inv_hbm, inverses, z, own, f0, f1, left, r_rows, r_cols, low, sems):
     dz, xh = at[3], at[4]
     row = (at[0] * 4 + at[1]) * 2 + at[2]
     col = dz * 2 + xh
     around = lambda d, other: (dz + d + 4) % 4 * 2 + (1 - xh if other else xh)
     here, up, down, far, far2 = pieces
+    fetch = pltpu.make_async_copy(inv_hbm, inverses, sems.at[0])
+    fetch.start()
     for piece, first, source in (
         (here, 0, around(0, False)),
         (here, 8, around(0, True)),
@@ -205,12 +207,12 @@
         (far2, 0, around(2, True)),
     ):
         lanes = pl.ds(pl.multiple_of(source % PT * TILE, TILE), TILE)
+        rows = pl.ds(first * TILE, LROWS * TILE)
         for panel, ref in enumerate((f0, f1)):
 
             @pl.when(source // PT == panel)
             def _():
-                for a in range(LROWS):
-                    ref[a * TILE : (a + 1) * TILE, lanes] = piece[first + a]
+                pltpu.make_async_copy(piece.at[rows, :], ref.at[:, lanes], sems.at[1]).start()
 
     tile = jnp.where(lax.broadcasted_iota(i32, (LROWS * TILE, 1), 0) < TILE, row, NF)
     my_lanes = pl.ds(pl.multiple_of(col % PT * TILE, TILE), TILE)
@@ -219,18 +221,22 @@
         for a in range(tiles):
             own[a] = ref[a * TILE : (a + 1) * TILE, my_lanes]
 
+    fetch.wait()
     right_rows(r_rows, inverses[0])
     y_bit = jnp.where(at[1] >= 2, at[1], 3 - at[1]) - 2
     for k in range(PT):
         i = (y_bit ^ (k & 1)) * 2 + (at[2] ^ (k >> 1))
         rows = pl.ds(pl.multiple_of(i * TILE, TILE), TILE)
         for j in range(PT):
-            here = corner[k >> 1][(k & 1) * PT + j]
-            low[rows, j * TILE : (j + 1) * TILE] = here
+            low[rows, j * TILE : (j + 1) * TILE] = corner[k >> 1][(k & 1) * PT + j]
     left_form(left.at[:PANEL], 0, low[...])
     one, two = inverse_transposed(left.at[:PANEL], r_rows)
     low[:, :BLOCK] = one
     low[:, BLOCK:] = two
+    for _ in range(8):
+        lanes = pl.ds(0, TILE)
+        rows = pl.ds(0, LROWS * TILE)
+        pltpu.make_async_copy(here.at[rows, :], f0.at[:, lanes], sems.at[1]).wait()
     left_form(left, 0, f0[...])
     one, two = inverse_transposed(left, r_rows)
     f0[:, :BLOCK] = jnp.where(tile >= PT, one, 0.0)
@@ -283,15 +289,15 @@
     at, *refs
 ):
     columns, pieces, corner = refs[:10], refs[10:15], refs[15:17]
-    front, inverses, out = refs[17:20]
-    z, right, raw, own, f0, f1, r_rows, r_cols, low = refs[20:]
+    front, inv_hbm, out = refs[17:20]
+    z, right, raw, own, f0, f1, r_rows, r_cols, low, inverses, sems = refs[20:]
     left = z.at[:, :KP]
     step = pl.program_id(0)
 
     @pl.when(step == 0)
     def _():
         row_factors(
-            at, pieces, corner, inverses, z, own, f0, f1, left, r_rows, r_cols, low
+            at, pieces, corner, inv_hbm, inverses, z, own, f0, f1, left, r_rows, r_cols, low, sems
         )
 
     for k in range(2):
@@ -342,9 +348,10 @@
                 pl.BlockSpec((x.shape[0], 1, TILE, TILE), lambda j: (0, j, 0, 0))
                 for x in columns
             ),
-            *[vmem] * 7,
+            *[pl.BlockSpec(memory_space=pl.ANY)] * 5,
+            *[vmem] * 2,
             block,
-            vmem,
+            pl.BlockSpec(memory_space=pl.ANY),
         ],
         out_specs=block,
         scratch_shapes=[
@@ -357,8 +364,10 @@
             pltpu.VMEM((PANEL, KP), bf16),
             pltpu.VMEM((KP, PANEL), bf16),
             pltpu.VMEM((PANEL, PANEL), f32),
+            pltpu.VMEM((NPANEL, PANEL, PANEL), f32),
+            pltpu.SemaphoreType.DMA((2,)),
         ],
-        compiler_params=pltpu.CompilerParams(vmem_limit_bytes=26 * MIB),
+        compiler_params=pltpu.CompilerParams(vmem_limit_bytes=40 * MIB),
         cost_estimate=pl.CostEstimate(
             flops=24_000_000_000, bytes_accessed=30 * MIB, transcendentals=0
         ),
@@ -416,6 +425,7 @@
     columns += opposite(*columns[1:], "row")
     columns = columns + [move(x, "row", 8, lambda i: i ^ 1) for x in columns]
     columns = [x.reshape(-1, LROWS, TILE, TILE) for x in columns]
+    pieces = [x.reshape(-1, TILE) for x in pieces]
     return columns, pieces, corner, front
 
 

time: 370 us -> 367 us (level)
  starting transfers between devices: 33.1 us -> 40.3 us
  waiting for transfers between devices: 56.4 us -> 50.5 us
  local copies, waits for them, and re-layouts: 23 us -> 17.8 us
    ppermute x17, starting transfers between devices: 19.2 us -> 26.2 us  [move(): return lax.ppermute(x, axis, [(i, to(i)) for i in range(size)])]
    unnamed x26 -> x22, local copies, waits for them, and re-layouts: 18.8 us -> 13.6 us
where the time goes in v9:
time: 367 us; the launch traced here: 366 us
  blocking collectives  204 us (56%)
  waiting for transfers between devices  50.5 us (14%)
  Pallas kernels  48.8 us (13%)
  starting transfers between devices  40.3 us (11%)
  local copies, waits for them, and re-layouts  17.8 us (5%)
    all_to_all x1, blocking collectives, local(): lax.all_to_all(outgoing, ('sib', 'row', 'col'), split_axis=0, concat_axis...  204 us
    pallas_call x1, Pallas kernels, update(): pl.pallas_call(update_kernel, grid=(LCOLS // 2,), out_shape=jax.ShapeDtyp...  33.7 us
    ppermute x17, waiting for transfers between devices, move(): return lax.ppermute(x, axis, [(i, to(i)) for i in range(size)])  26.9 us
    ppermute x17, starting transfers between devices, move(): return lax.ppermute(x, axis, [(i, to(i)) for i in range(size)])  26.2 us
    unnamed x22, local copies, waits for them, and re-layouts  13.6 us
    all_to_all x1, waiting for transfers between devices, gather(): lax.all_to_all(top, 'col', split_axis=0, concat_axis=0, tiled=True)[:PT]  8.62 us
    ppermute x1, waiting for transfers between devices, gather_corner(): c = lax.ppermute(top, ('sib', 'row'), [(i, 8 + j) for i, j in flip])  7.37 us
  transfers between devices with their start and end apart: 22, of which 10 were waited for; matrix products, arithmetic and copies ran while one was open for 1% of the time, Pallas kernels for 2%

profile of v9, /device:TPU:3, one launch (start us, length us, event | category | flops | bytes accessed | tf_op | source)
XLA Modules:
  0.0 365.9 jit_solution(4948207974474269469)
XLA Ops:
  0.7 0.7 and_select_fusion.5
  1.4 0.7 select_reduce_fusion.1
  2.8 3.4 copy-done
  6.2 2.2 pack.1
  8.4 204.1 %all_to_all.10.refs_0_.refs_1_ = f32[128,264,128]{2,1,0:T(8,128)} all-to-all(f32[128,264,128]{2,1,0:T(8,128)S(1)} %pack.1), channel_id=1, replica_groups=mesh['sib'=2,'row'=8,'col'=8] {'sib','row','col'}, dimensions={0} | all-to-all | bytes 34603008 | tf_op jit(solution)/shard_map/all_to_all | solution.py:463
  212.5 6.5 %add_panel.1 = (f32[8,128,128]{2,1,0:T(8,128)}, s32[8,128]{1,0:T(8,128)}) custom-call(f32[128,264,128]{2,1,0:T(8,128)} %all_to_all.10.refs_0_.refs_1_), custom_call_target="tpu_custom_call" | custom-call | tf_op jit(solution)/shard_map/add_panel/pallas_call | solution.py:115
  219.0 1.4 collective-permute-start
  220.4 0.9 slice_bitcast_fusion
  221.3 0.8 broadcast_in_dim.82
  222.1 4.5 %all-to-all-start.1 = ((f32[8,128,128]{2,1,0:T(8,128)}), f32[8,128,128]{2,1,0:T(8,128)S(1)}, u32[]{:S(2)}, u32[]{:S(2)}) async-start(f32[8,128,128]{2,1,0:T(8,128)} %broadcast_in_dim.82), calls=%async_computation.1 | async-start | bytes 1048576 | tf_op jit(solution)/shard_map/all_to_all | solution.py:414
  226.6 5.7 %collective-permute-start.1 = (f32[8,128,128]{2,1,0:T(8,128)}, f32[8,128,128]{2,1,0:T(8,128)S(1)}, u32[]{:S(2)}, u32[]{:S(2)}) collective-permute-start(f32[8,128,128]{2,1,0:T(8,128)} %get-tuple-element.16), channel_id=1, source_target_pairs={{0,0},{1,8},{2,16},{3,24},{4,32},{5,40},{6,48},{7,56},{8,1},{9,9},... | collective-permute-start | bytes 1572872 | tf_op jit(solution)/shard_map/ppermute | solution.py:411
  232.3 8.6 %all-to-all-done.1 = f32[8,128,128]{2,1,0:T(8,128)S(1)} async-done(((f32[8,128,128]{2,1,0:T(8,128)}), f32[8,128,128]{2,1,0:T(8,128)S(1)}, u32[]{:S(2)}, u32[]{:S(2)}) %all-to-all-start.1) | async-done | bytes 524320 | tf_op jit(solution)/shard_map/all_to_all | solution.py:414
  241.0 1.1 pad_maximum_fusion
  242.1 3.6 collective-permute-done.1
  245.7 1.3 collective-permute-start.5
  247.0 1.3 collective-permute-start.4
  248.3 1.3 collective-permute-start.3
  249.6 2.4 collective-permute-start.2
  252.0 7.4 %collective-permute-done.5 = f32[4,128,128]{2,1,0:T(8,128)S(1)} collective-permute-done((f32[4,128,128]{2,1,0:T(8,128)S(1)}, f32[4,128,128]{2,1,0:T(8,128)S(1)}, u32[]{:S(2)}, u32[]{:S(2)}) %collective-permute-start.5) | collective-permute-done | bytes 262176 | tf_op jit(solution)/shard_map/ppermute | solution.py:398
  259.3 4.1 %collective-permute-done.4 = f32[4,128,128]{2,1,0:T(8,128)S(1)} collective-permute-done((f32[4,128,128]{2,1,0:T(8,128)S(1)}, f32[4,128,128]{2,1,0:T(8,128)S(1)}, u32[]{:S(2)}, u32[]{:S(2)}) %collective-permute-start.4) | collective-permute-done | bytes 262176 | tf_op jit(solution)/shard_map/ppermute | solution.py:397
  263.5 2.6 collective-permute-start.6
  266.0 4.0 %collective-permute-start.17 = (f32[16,128,128]{2,1,0:T(8,128)S(1)}, f32[16,128,128]{2,1,0:T(8,128)S(1)}, u32[]{:S(2)}, u32[]{:S(2)}) collective-permute-start(f32[16,128,128]{2,1,0:T(8,128)S(1)} %pad_maximum_fusion), channel_id=1, source_target_pairs={{0,6},{1,7},{2,0},{3,1},{4,2},{5,3},{6,4},{7,5},{8,14},{9,15},{10,... | collective-permute-start | bytes 3145736 | tf_op jit(solution)/shard_map/ppermute | solution.py:379
  270.0 1.5 collective-permute-done.6
  271.6 5.0 %collective-permute-start.8 = (f32[16,128,128]{2,1,0:T(8,128)S(1)}, f32[16,128,128]{2,1,0:T(8,128)}, u32[]{:S(2)}, u32[]{:S(2)}) collective-permute-start(f32[16,128,128]{2,1,0:T(8,128)S(1)} %pad_maximum_fusion.1), channel_id=1, source_target_pairs={{0,48},{8,56},{16,0},{24,8},{32,16},{40,24},{48,32},{56,40},{1,49}... | collective-permute-start | bytes 3145736 | tf_op jit(solution)/shard_map/ppermute | solution.py:379
  276.6 2.1 collective-permute-start.20
  278.7 13.3 %collective-permute-done.17 = f32[16,128,128]{2,1,0:T(8,128)S(1)} collective-permute-done((f32[16,128,128]{2,1,0:T(8,128)S(1)}, f32[16,128,128]{2,1,0:T(8,128)S(1)}, u32[]{:S(2)}, u32[]{:S(2)}) %collective-permute-start.17) | collective-permute-done | bytes 1048608 | tf_op jit(solution)/shard_map/ppermute | solution.py:379
  292.1 3.6 collective-permute-start.19
  295.8 0.8 copy-done.4
  296.6 6.4 %add_all.1.refs_17_ = f32[8,16,128,128]{3,2,1,0:T(8,128)S(1)} custom-call(s32[8,128]{1,0:T(8,128)S(1)} %copy-done.6, f32[128,264,128]{2,1,0:T(8,128)} %all_to_all.10.refs_0_.refs_1_), custom_call_target="tpu_custom_call" | custom-call | flops 1000 | bytes 25165824 | tf_op jit(solution)/shard_map/add_all/pallas_call | solution.py:132
  303.1 3.3 copy-done.1
  306.4 1.1 slice.20
  307.4 1.2 collective-permute-start.12
  308.6 1.1 slice.21
  309.9 1.3 collective-permute-start.9
  311.3 0.8 copy-done.7
  312.0 0.6 collective-permute-start.11
  312.6 0.8 copy-done.9
  313.4 10.0 %collective-permute-done.10 = f32[8,128,128]{2,1,0:T(8,128)} collective-permute-done((f32[8,128,128]{2,1,0:T(8,128)S(1)}, f32[8,128,128]{2,1,0:T(8,128)}, u32[]{:S(2)}, u32[]{:S(2)}) %collective-permute-start.10) | collective-permute-done | bytes 524320 | tf_op jit(solution)/shard_map/ppermute | solution.py:379
  323.4 0.8 collective-permute-start.15
  324.2 0.3 collective-permute-done.9
  324.5 1.1 collective-permute-start.14
  325.7 0.4 collective-permute-done.15
  326.1 1.4 collective-permute-done.14
  327.5 1.2 copy-done.3
  328.7 1.2 copy-done.5
  330.0 1.0 copy-done.8
  331.0 1.0 copy-done.10
  332.0 33.7 %update.1 = f32[8,16,128,128]{3,2,1,0:T(8,128)} custom-call(s32[5]{0:T(128)S(1)} %stack.23.at, f32[2,8,128,128]{3,2,1,0:T(8,128)S(1)} %bitcast.49, f32[2,8,128,128]{3,2,1,0:T(8,128)} %bitcast.12.refs_1_, f32[2,8,128,128]{3,2,1,0:T(8,128)} %bitcast.13.refs_2_, f32[1,8,128,128]{3,2,1,0:T(8,128)} %bitcast.14.refs_3_, f32[1,8,128,128]{3,2,1,0:T(8,128)} %bitcast.15.refs_4_, ...), custom_call_target="tpu_custom_call" | custom-call | flops 24000000000 | bytes 31457280 | tf_op jit(solution)/shard_map/update/pallas_call | solution.py:341
  (46 shorter events, 1.4 us)
Async XLA Ops:
  2.8 3.4 copy-start
  219.0 77.6 %copy-start.6 = (s32[8,128]{1,0:T(8,128)S(1)}, s32[8,128]{1,0:T(8,128)}, u32[]{:S(2)}) copy-start(s32[8,128]{1,0:T(8,128)} %get-tuple-element.20.refs_0_) | copy-start | bytes 12292
  219.0 21.9 %collective-permute-start = (f32[8,128,128]{2,1,0:T(8,128)}, f32[8,128,128]{2,1,0:T(8,128)S(1)}, u32[]{:S(2)}, u32[]{:S(2)}) collective-permute-start(f32[8,128,128]{2,1,0:T(8,128)} %get-tuple-element.16), channel_id=1, source_target_pairs={{0,1},{1,0},{2,3},{3,2},{4,5},{5,4},{6,7},{7,6},{8,9},{9,8},{10,11... | collective-permute-start | bytes 1572872 | tf_op jit(solution)/shard_map/ppermute | solution.py:379
  222.1 18.8 %all-to-all-start.1 = ((f32[8,128,128]{2,1,0:T(8,128)}), f32[8,128,128]{2,1,0:T(8,128)S(1)}, u32[]{:S(2)}, u32[]{:S(2)}) async-start(f32[8,128,128]{2,1,0:T(8,128)} %broadcast_in_dim.82), calls=%async_computation.1 | async-start | bytes 1048576 | tf_op jit(solution)/shard_map/all_to_all | solution.py:414
  226.6 19.1 %collective-permute-start.1 = (f32[8,128,128]{2,1,0:T(8,128)}, f32[8,128,128]{2,1,0:T(8,128)S(1)}, u32[]{:S(2)}, u32[]{:S(2)}) collective-permute-start(f32[8,128,128]{2,1,0:T(8,128)} %get-tuple-element.16), channel_id=1, source_target_pairs={{0,0},{1,8},{2,16},{3,24},{4,32},{5,40},{6,48},{7,56},{8,1},{9,9},... | collective-permute-start | bytes 1572872 | tf_op jit(solution)/shard_map/ppermute | solution.py:411
  245.7 13.6 %collective-permute-start.5 = (f32[4,128,128]{2,1,0:T(8,128)S(1)}, f32[4,128,128]{2,1,0:T(8,128)S(1)}, u32[]{:S(2)}, u32[]{:S(2)}) collective-permute-start(f32[4,128,128]{2,1,0:T(8,128)S(1)} %slice.24), channel_id=1, source_target_pairs={{32,80},{40,88},{48,64},{56,72},{33,81},{41,89},{49,65},{57,73},{3... | collective-permute-start | bytes 786440 | tf_op jit(solution)/shard_map/ppermute | solution.py:398
  247.0 16.4 %collective-permute-start.4 = (f32[4,128,128]{2,1,0:T(8,128)S(1)}, f32[4,128,128]{2,1,0:T(8,128)S(1)}, u32[]{:S(2)}, u32[]{:S(2)}) collective-permute-start(f32[4,128,128]{2,1,0:T(8,128)S(1)} %slice.24), channel_id=1, source_target_pairs={{32,16},{40,24},{48,0},{56,8},{33,17},{41,25},{49,1},{57,9},{34,18... | collective-permute-start | bytes 786440 | tf_op jit(solution)/shard_map/ppermute | solution.py:397
  248.3 15.1 %collective-permute-start.3 = (f32[4,128,128]{2,1,0:T(8,128)S(1)}, f32[4,128,128]{2,1,0:T(8,128)S(1)}, u32[]{:S(2)}, u32[]{:S(2)}) collective-permute-start(f32[4,128,128]{2,1,0:T(8,128)S(1)} %slice.24), channel_id=1, source_target_pairs={{0,64},{1,65},{2,66},{3,67},{4,68},{5,69},{6,70},{7,71},{8,72},{9,... | collective-permute-start | bytes 786440 | tf_op jit(solution)/shard_map/ppermute | solution.py:396
  249.6 21.9 %collective-permute-start.2 = (f32[8,128,128]{2,1,0:T(8,128)S(1)}, f32[8,128,128]{2,1,0:T(8,128)S(1)}, u32[]{:S(2)}, u32[]{:S(2)}) collective-permute-start(f32[8,128,128]{2,1,0:T(8,128)S(1)} %collective-permute-done.1), channel_id=1, source_target_pairs={{0,64},{64,0},{1,65},{65,1},{2,66},{66,2},{3,67},{67,3},{4,68},{68... | collective-permute-start | bytes 1572872 | tf_op jit(solution)/shard_map/ppermute | solution.py:379
  263.5 8.0 %collective-permute-start.6 = (f32[4,128,128]{2,1,0:T(8,128)S(1)}, f32[4,128,128]{2,1,0:T(8,128)S(1)}, u32[]{:S(2)}, u32[]{:S(2)}) collective-permute-start(f32[4,128,128]{2,1,0:T(8,128)S(1)} %select_select_fusion), channel_id=1, source_target_pairs={{0,16},{8,24},{16,0},{24,8},{32,48},{40,56},{48,32},{56,40},{1,17}... | collective-permute-start | bytes 786440 | tf_op jit(solution)/shard_map/ppermute | solution.py:379
  266.0 26.0 %collective-permute-start.17 = (f32[16,128,128]{2,1,0:T(8,128)S(1)}, f32[16,128,128]{2,1,0:T(8,128)S(1)}, u32[]{:S(2)}, u32[]{:S(2)}) collective-permute-start(f32[16,128,128]{2,1,0:T(8,128)S(1)} %pad_maximum_fusion), channel_id=1, source_target_pairs={{0,6},{1,7},{2,0},{3,1},{4,2},{5,3},{6,4},{7,5},{8,14},{9,15},{10,... | collective-permute-start | bytes 3145736 | tf_op jit(solution)/shard_map/ppermute | solution.py:379
  270.0 25.7 %collective-permute-start.16 = (f32[16,128,128]{2,1,0:T(8,128)S(1)}, f32[16,128,128]{2,1,0:T(8,128)S(1)}, u32[]{:S(2)}, u32[]{:S(2)}) collective-permute-start(f32[16,128,128]{2,1,0:T(8,128)S(1)} %pad_maximum_fusion), channel_id=1, source_target_pairs={{0,2},{1,3},{2,4},{3,5},{4,6},{5,7},{6,0},{7,1},{8,10},{9,11},{10,... | collective-permute-start | bytes 3145736 | tf_op jit(solution)/shard_map/ppermute | solution.py:379
  271.6 34.7 %collective-permute-start.8 = (f32[16,128,128]{2,1,0:T(8,128)S(1)}, f32[16,128,128]{2,1,0:T(8,128)}, u32[]{:S(2)}, u32[]{:S(2)}) collective-permute-start(f32[16,128,128]{2,1,0:T(8,128)S(1)} %pad_maximum_fusion.1), channel_id=1, source_target_pairs={{0,48},{8,56},{16,0},{24,8},{32,16},{40,24},{48,32},{56,40},{1,49}... | collective-permute-start | bytes 3145736 | tf_op jit(solution)/shard_map/ppermute | solution.py:379
  276.6 29.7 %collective-permute-start.7 = (f32[16,128,128]{2,1,0:T(8,128)S(1)}, f32[16,128,128]{2,1,0:T(8,128)}, u32[]{:S(2)}, u32[]{:S(2)}) collective-permute-start(f32[16,128,128]{2,1,0:T(8,128)S(1)} %pad_maximum_fusion.1), channel_id=1, source_target_pairs={{0,16},{8,24},{16,32},{24,40},{32,48},{40,56},{48,0},{56,8},{1,17}... | collective-permute-start | bytes 3145736 | tf_op jit(solution)/shard_map/ppermute | solution.py:379
  276.6 33.3 %collective-permute-start.20 = (f32[8,128,128]{2,1,0:T(8,128)S(1)}, f32[8,128,128]{2,1,0:T(8,128)S(1)}, u32[]{:S(2)}, u32[]{:S(2)}) collective-permute-start(f32[8,128,128]{2,1,0:T(8,128)S(1)} %pad_maximum_fusion.2.refs_15_), channel_id=1, source_target_pairs={{0,8},{8,0},{16,24},{24,16},{32,40},{40,32},{48,56},{56,48},{1,9},... | collective-permute-start | bytes 1572872 | tf_op jit(solution)/shard_map/ppermute | solution.py:379
  292.0 3.8 %copy-start.2 = (f32[16,128,128]{2,1,0:T(8,128)}, f32[16,128,128]{2,1,0:T(8,128)S(1)}, u32[]{:S(2)}) copy-start(f32[16,128,128]{2,1,0:T(8,128)S(1)} %collective-permute-done.17) | copy-start | bytes 3145732
  292.1 19.2 %collective-permute-start.19 = (f32[8,128,128]{2,1,0:T(8,128)S(1)}, f32[8,128,128]{2,1,0:T(8,128)S(1)}, u32[]{:S(2)}, u32[]{:S(2)}) collective-permute-start(f32[8,128,128]{2,1,0:T(8,128)S(1)} %slice.26), channel_id=1, source_target_pairs={{0,6},{1,7},{2,0},{3,1},{4,2},{5,3},{6,4},{7,5},{8,14},{9,15},{10,... | collective-permute-start | bytes 1572872 | tf_op jit(solution)/shard_map/ppermute | solution.py:379
  295.7 1.0 copy-start.4
  295.7 16.9 %collective-permute-start.18 = (f32[8,128,128]{2,1,0:T(8,128)S(1)}, f32[8,128,128]{2,1,0:T(8,128)S(1)}, u32[]{:S(2)}, u32[]{:S(2)}) collective-permute-start(f32[8,128,128]{2,1,0:T(8,128)S(1)} %slice.25), channel_id=1, source_target_pairs={{0,2},{1,3},{2,4},{3,5},{4,6},{5,7},{6,0},{7,1},{8,10},{9,11},{10,... | collective-permute-start | bytes 1572872 | tf_op jit(solution)/shard_map/ppermute | solution.py:379
  303.1 3.3 copy-start.1
  307.4 20.1 %collective-permute-start.12 = (f32[16,128,128]{2,1,0:T(8,128)}, f32[16,128,128]{2,1,0:T(8,128)}, u32[]{:S(2)}, u32[]{:S(2)}) collective-permute-start(f32[16,128,128]{2,1,0:T(8,128)} %collective-permute-done.7), channel_id=1, source_target_pairs={{0,8},{8,0},{16,24},{24,16},{32,40},{40,32},{48,56},{56,48},{1,9},... | collective-permute-start | bytes 3145736 | tf_op jit(solution)/shard_map/ppermute | solution.py:379
  309.7 13.7 %collective-permute-start.10 = (f32[8,128,128]{2,1,0:T(8,128)S(1)}, f32[8,128,128]{2,1,0:T(8,128)}, u32[]{:S(2)}, u32[]{:S(2)}) collective-permute-start(f32[8,128,128]{2,1,0:T(8,128)S(1)} %slice.21), channel_id=1, source_target_pairs={{0,48},{8,56},{16,0},{24,8},{32,16},{40,24},{48,32},{56,40},{1,49}... | collective-permute-start | bytes 1572872 | tf_op jit(solution)/shard_map/ppermute | solution.py:379
  309.9 14.5 %collective-permute-start.9 = (f32[8,128,128]{2,1,0:T(8,128)S(1)}, f32[8,128,128]{2,1,0:T(8,128)}, u32[]{:S(2)}, u32[]{:S(2)}) collective-permute-start(f32[8,128,128]{2,1,0:T(8,128)S(1)} %slice.20), channel_id=1, source_target_pairs={{0,16},{8,24},{16,32},{24,40},{32,48},{40,56},{48,0},{56,8},{1,17}... | collective-permute-start | bytes 1572872 | tf_op jit(solution)/shard_map/ppermute | solution.py:379
  311.2 0.8 copy-start.7
  312.0 15.4 %collective-permute-start.11 = (f32[16,128,128]{2,1,0:T(8,128)S(1)}, f32[16,128,128]{2,1,0:T(8,128)}, u32[]{:S(2)}, u32[]{:S(2)}) collective-permute-start(f32[16,128,128]{2,1,0:T(8,128)S(1)} %pad_maximum_fusion.1), channel_id=1, source_target_pairs={{0,8},{8,0},{16,24},{24,16},{32,40},{40,32},{48,56},{56,48},{1,9},... | collective-permute-start | bytes 3145736 | tf_op jit(solution)/shard_map/ppermute | solution.py:379
  312.6 0.8 copy-start.9
  313.4 14.1 %collective-permute-start.13 = (f32[16,128,128]{2,1,0:T(8,128)}, f32[16,128,128]{2,1,0:T(8,128)}, u32[]{:S(2)}, u32[]{:S(2)}) collective-permute-start(f32[16,128,128]{2,1,0:T(8,128)} %collective-permute-done.8), channel_id=1, source_target_pairs={{0,8},{8,0},{16,24},{24,16},{32,40},{40,32},{48,56},{56,48},{1,9},... | collective-permute-start | bytes 3145736 | tf_op jit(solution)/shard_map/ppermute | solution.py:379
  323.4 2.7 collective-permute-start.15
  324.5 3.0 collective-permute-start.14
  327.5 1.2 copy-start.3
  328.7 1.2 copy-start.5
  329.9 1.0 copy-start.8
  331.0 1.0 copy-start.10
